TPU v7x, 32 devices: a whole 2x2x4 slice. The times are simulated.
32 devices in a mesh: tok: 8 (over z, y), head: 4 (over x, core).
Axes of the slice: x: 2, y: 2, z: 4, core: 2. Of those that a mesh axis runs over, the one named last changes fastest.
Arguments:
- hidden_in: bfloat16 [16384, 768], P('tok'), may hold values from -6 to 6
- norm_gain: float32 [768], replicated, may hold values from 0.1 to 1.9
- w_zx: bfloat16 [768, 2, 1536], P(None, None, 'head'), may hold values from -0.21875 to 0.21875
- w_bc: bfloat16 [768, 256], replicated, may hold values from -0.21875 to 0.21875
- w_dt: bfloat16 [768, 24], replicated, may hold values from -0.21875 to 0.21875
- dt_bias: float32 [24], replicated, may hold values from -6 to -4
- a_log: float32 [24], replicated, may hold values from -5.5 to 1.6
- conv_x: float32 [5, 1536], P(None, 'head'), may hold values from -3 to 3
- conv_bc: float32 [5, 256], replicated, may hold values from -3 to 3
- d_skip: float32 [24], replicated, may hold values from 0.5 to 1.5
- gate_gain: float32 [1536], P('head'), may hold values from 0.1 to 1.9
- w_out: bfloat16 [1536, 768], P('head'), may hold values from -0.15625 to 0.15625
- out_grad: bfloat16 [16384, 768], P('tok'), may hold values from -6 to 6
- group_first: int32 [64], P('tok'), may hold values from 0 to 1, as said below
- group_valid: int32 [64], P('tok'), may hold values from 128 to 256, as said below
Outputs:
- block_out: bfloat16 [16384, 768], P('tok')
- grad_in: float32 [16384, 768], P('tok')
- grad_norm_gain: float32 [768], replicated
- grad_w_zx: float32 [768, 2, 1536], P(None, None, 'head')
- grad_w_bc: float32 [768, 256], replicated
- grad_w_dt: float32 [768, 24], replicated
- grad_dt_bias: float32 [24], replicated
- grad_a_log: float32 [24], replicated
- grad_conv_x: float32 [5, 1536], P(None, 'head')
- grad_conv_bc: float32 [5, 256], replicated
- grad_d_skip: float32 [24], replicated
- grad_gate_gain: float32 [1536], P('head')
- grad_w_out: float32 [1536, 768], P('head')
Inputs may be any that keep to these rules, and one draw needn't show every extreme that they name: `group_first`: the first group begins a sequence; sequences occupy whole groups. `group_valid`: below 256 only in the last group of a sequence.
All inputs are finite; a program needn't handle non-finite values.
Results may differ from a plain program's by a relative error of at most 0.0029.
The roundings to bfloat16 on the way count: a program that leaves them out, or rounds other values in their place, can miss the bound.
Values may be sent and summed in bfloat16 or wider, within the bound.
No kernel may reach another device: no remote copies, remote signals or barrier semaphores. Data moves between devices by JAX's collectives and lax.ppermute only.
A program may use at most 192 MiB of HBM per device.

v0:
```python
import jax
import jax.numpy as jnp
from jax import lax
from jax.sharding import PartitionSpec as P

D = 768
H = 24
P_SIZE = 64
N = 128
KCONV = 4
GROUP = 256


NORM_EPS = 1e-05
PRECISE = lax.Precision.HIGHEST


def from_behind(block, axis, distance):
    devices = range(lax.axis_size(axis))
    route = [(i - distance, i) for i in devices if i - distance in devices]
    return lax.ppermute(block, axis, route)


def entering(shard, axis, combine, identity, reverse):
    count, mine = (lax.axis_size(axis), lax.axis_index(axis))
    everything = jax.tree.map(lambda part: lax.all_gather(part, axis), shard)
    start = jax.tree.map(
        lambda part, zero: jnp.broadcast_to(jnp.asarray(zero, part.dtype), part.shape),
        shard,
        identity,
    )

    def step(k, before):
        at = count - 1 - k if reverse else k
        reached = at > mine if reverse else at < mine
        new = combine(before, jax.tree.map(lambda part: part[at], everything))
        return jax.tree.map(lambda a, b: jnp.where(reached, a, b), new, before)

    return lax.fori_loop(0, count, step, start)


def rounded(value):
    return lax.optimization_barrier(value.astype(jnp.bfloat16)).astype(jnp.float32)


def contract(left, right, left_dim, right_dim):
    return lax.dot_general(
        left, right, (((left_dim,), (right_dim,)), ((), ())), preferred_element_type=jnp.float32
    )


def contract_exact(left, right, left_dim, right_dim):
    return lax.dot_general(
        left,
        right,
        (((left_dim,), (right_dim,)), ((), ())),
        precision=PRECISE,
        preferred_element_type=jnp.float32,
    )


def lag_keep(group_first, length):
    position = jnp.arange(length) % GROUP
    start_rows = jnp.repeat(group_first.astype(jnp.float32), GROUP, total_repeat_length=length)
    return [
        1.0 - (position < KCONV - 1 - tap_index).astype(jnp.float32) * start_rows
        for tap_index in range(KCONV)
    ]


def conv_silu(extended, conv_taps, keep_list):
    row_count = extended.shape[0] - (KCONV - 1)
    running = conv_taps[KCONV] + jnp.zeros((row_count, conv_taps.shape[1]), jnp.float32)
    for tap_index in range(KCONV):
        running = (
            running
            + conv_taps[tap_index]
            * extended[tap_index : tap_index + row_count]
            * keep_list[tap_index][:, None]
        )
    return jax.nn.silu(running)


def group_inner(x_blocks, write_blocks, step_blocks, decay_blocks, scores):
    length = decay_blocks.shape[1]
    cum_decay = jnp.cumsum(decay_blocks, axis=1)
    cum_heads = jnp.swapaxes(cum_decay, 1, 2)
    causal = jnp.tril(jnp.ones((length, length), bool))
    decay_gap = cum_heads[:, :, :, None] - cum_heads[:, :, None, :]
    weights = jnp.where(causal, jnp.exp(jnp.where(causal, decay_gap, 0.0)), 0.0) * scores[:, None]
    x_scaled = x_blocks * step_blocks[..., None]
    within = jnp.einsum("khls,kshp->klhp", weights, x_scaled, precision=PRECISE)
    to_end = jnp.exp(cum_decay[:, -1:, :] - cum_decay)
    group_states = jnp.einsum(
        "kshp,ksn->khpn", x_scaled * to_end[..., None], write_blocks, precision=PRECISE
    )
    return (within, group_states, cum_decay)


def group_outer(read_blocks, cum_decay, entry_states):
    return (
        jnp.einsum("kln,khpn->klhp", read_blocks, entry_states, precision=PRECISE)
        * jnp.exp(cum_decay)[..., None]
    )


def chain_merge(earlier, later):
    return (earlier[0] * later[0], later[0][:, None, None] * earlier[1] + later[1])


def on_device(
    hidden_in,
    norm_gain,
    w_zx,
    w_bc,
    w_dt,
    dt_bias,
    a_log,
    conv_x,
    conv_bc,
    d_skip,
    gate_gain,
    w_out,
    out_grad,
    group_first,
    group_valid,
):
    row_count = hidden_in.shape[0]
    local_width = w_zx.shape[2]
    heads_here = local_width // P_SIZE
    group_count = row_count // GROUP
    inner_width = H * P_SIZE
    head_count = lax.axis_size("head")
    head_index = lax.axis_index("head")
    head_start = head_index * heads_here
    zero_index = jnp.zeros((), jnp.int32)
    w_dt_here = lax.dynamic_slice_in_dim(w_dt, head_start, heads_here, 1)
    bias_here = lax.dynamic_slice_in_dim(dt_bias, head_start, heads_here, 0)
    alog_here = lax.dynamic_slice_in_dim(a_log, head_start, heads_here, 0)
    skip_here = lax.dynamic_slice_in_dim(d_skip, head_start, heads_here, 0)
    start_float = group_first.astype(jnp.float32)
    live_mask = (
        (jnp.arange(GROUP)[None, :] < group_valid[:, None]).astype(jnp.float32).reshape(row_count)
    )
    keep_list = lag_keep(group_first, row_count)
    upcast = hidden_in.astype(jnp.float32)
    inv_rms = lax.rsqrt(jnp.mean(upcast * upcast, axis=1, keepdims=True) + NORM_EPS)
    normed = upcast * inv_rms
    normed_low = (normed * norm_gain).astype(jnp.bfloat16)
    zx_flat = w_zx.reshape(D, 2 * local_width)
    proj_zx = jnp.dot(normed_low, zx_flat, preferred_element_type=jnp.float32).reshape(
        row_count, 2, local_width
    )
    gate_raw = proj_zx[:, 0]
    inner_raw = proj_zx[:, 1]
    state_raw = jnp.dot(normed_low, w_bc, preferred_element_type=jnp.float32)
    step_raw = jnp.dot(normed_low, w_dt_here, preferred_element_type=jnp.float32)
    mixed = jnp.concatenate([inner_raw, state_raw], axis=1)
    rim_prev = from_behind(mixed[row_count - (KCONV - 1) :], "tok", 1)
    extended = jnp.concatenate([rim_prev, mixed], axis=0)
    conv_taps = jnp.concatenate([conv_x, conv_bc], axis=1)

    def conv_here(ext_rows, tap_rows):
        return conv_silu(ext_rows, tap_rows, keep_list)

    activated, conv_pull = jax.vjp(conv_here, extended, conv_taps)
    x_low = rounded(activated[:, :local_width])
    write_bf = activated[:, local_width : local_width + N].astype(jnp.bfloat16)
    read_bf = activated[:, local_width + N :].astype(jnp.bfloat16)
    write_map = write_bf.astype(jnp.float32)
    read_map = read_bf.astype(jnp.float32)
    step_pre = step_raw + bias_here
    step_size = jax.nn.softplus(step_pre) * live_mask[:, None]
    decay_rate = -jnp.exp(alog_here)
    log_decay = step_size * decay_rate
    x_blocks = x_low.reshape(group_count, GROUP, heads_here, P_SIZE)
    write_blocks = write_map.reshape(group_count, GROUP, N)
    read_blocks = read_map.reshape(group_count, GROUP, N)
    step_blocks = step_size.reshape(group_count, GROUP, heads_here)
    decay_blocks = log_decay.reshape(group_count, GROUP, heads_here)
    scores = jnp.einsum(
        "kln,ksn->kls",
        read_bf.reshape(group_count, GROUP, N),
        write_bf.reshape(group_count, GROUP, N),
        preferred_element_type=jnp.float32,
    )
    (within, group_states, cum_decay), inner_pull = jax.vjp(
        group_inner, x_blocks, write_blocks, step_blocks, decay_blocks, scores
    )
    end_decay = cum_decay[:, -1, :]
    carry_scale = (1.0 - start_float)[:, None] * jnp.exp(end_decay)
    unit_scale = jnp.ones((heads_here,), jnp.float32)
    empty_state = jnp.zeros((heads_here, P_SIZE, N), jnp.float32)

    def fold_ahead(carry, item):
        scale_acc, state_acc = carry
        scale_now, state_now = item
        return ((scale_acc * scale_now, scale_now[:, None, None] * state_acc + state_now), None)

    (device_scale, device_state), _ = lax.scan(
        fold_ahead, (unit_scale, empty_state), (carry_scale, group_states)
    )
    _, prev_state = entering(
        (device_scale, device_state), "tok", chain_merge, (unit_scale, empty_state), False
    )

    def walk_ahead(state, item):
        is_start, end_now, state_now = item
        entry = (1.0 - is_start) * state
        return (jnp.exp(end_now)[:, None, None] * entry + state_now, entry)

    _, entry_states = lax.scan(walk_ahead, prev_state, (start_float, end_decay, group_states))
    across, outer_pull = jax.vjp(group_outer, read_blocks, cum_decay, entry_states)
    skip_cols = jnp.repeat(skip_here, P_SIZE)
    mixer_total = (within + across).reshape(row_count, local_width) + x_low * skip_cols
    gate_sig = jax.nn.sigmoid(gate_raw)
    gate_silu = gate_raw * gate_sig
    gated_out = mixer_total * gate_silu
    square_sum = lax.psum(jnp.sum(gated_out * gated_out, axis=1), "head")
    gate_inv = lax.rsqrt(square_sum / inner_width + NORM_EPS)[:, None]
    scaled = gated_out * gate_inv
    normed_out = (scaled * gate_gain).astype(jnp.bfloat16)
    partial_value = jnp.dot(normed_out, w_out, preferred_element_type=jnp.float32)
    share_cols = D // head_count
    block_out = (upcast + lax.psum(partial_value, "head")).astype(jnp.bfloat16)
    grad_resid = out_grad.astype(jnp.float32)
    grad_normed = contract(out_grad, w_out, 1, 1)
    grad_w_out = contract(normed_out, out_grad, 0, 0)
    grad_gate_gain = jnp.sum(grad_normed * scaled, axis=0)
    inner_sum = lax.psum(jnp.sum(grad_normed * gate_gain * gated_out, axis=1), "head")
    grad_gated = (
        gate_inv * gate_gain * grad_normed
        - gated_out * gate_inv**3 * (inner_sum / inner_width)[:, None]
    )
    grad_mixer = rounded(grad_gated * gate_silu)
    grad_gate = grad_gated * mixer_total * gate_sig * (1.0 + gate_raw * (1.0 - gate_sig))
    grad_skip_here = jnp.sum(
        (grad_mixer * x_low).reshape(row_count, heads_here, P_SIZE), axis=(0, 2)
    )
    grad_blocks = grad_mixer.reshape(group_count, GROUP, heads_here, P_SIZE)
    grad_read_out, grad_cum_out, entry_grad = outer_pull(grad_blocks)

    def fold_back(carry, item):
        scale_acc, grad_acc = carry
        scale_now, grad_now = item
        return ((scale_acc * scale_now, grad_now + scale_now[:, None, None] * grad_acc), None)

    back_items = (carry_scale, (1.0 - start_float)[:, None, None, None] * entry_grad)
    (back_scale, back_grad), _ = lax.scan(
        fold_back, (unit_scale, empty_state), back_items, reverse=True
    )
    _, end_grad = entering(
        (back_scale, back_grad), "tok", chain_merge, (unit_scale, empty_state), True
    )

    def walk_back(grad_state, item):
        is_start, end_now, entry_now, state_in = item
        grad_entry = entry_now + jnp.exp(end_now)[:, None, None] * grad_state
        grad_end = jnp.sum(grad_state * state_in, axis=(1, 2)) * jnp.exp(end_now)
        return ((1.0 - is_start) * grad_entry, (grad_state, grad_end))

    _, (grad_states, grad_end) = lax.scan(
        walk_back, end_grad, (start_float, end_decay, entry_grad, entry_states), reverse=True
    )
    grad_cum = grad_cum_out.at[:, -1, :].add(grad_end)
    grad_x, grad_write, grad_step, grad_decay, grad_scores = inner_pull(
        (grad_blocks, grad_states, grad_cum)
    )
    grad_write = grad_write + jnp.einsum(
        "kls,kln->ksn", grad_scores, read_blocks, precision=PRECISE
    )
    grad_read = jnp.einsum("kls,ksn->kln", grad_scores, write_blocks, precision=PRECISE)
    grad_x_low = grad_x.reshape(row_count, local_width) + grad_mixer * skip_cols
    grad_write_map = grad_write.reshape(row_count, N)
    grad_read_map = (grad_read + grad_read_out).reshape(row_count, N)
    grad_log = grad_decay.reshape(row_count, heads_here)
    grad_step_all = grad_step.reshape(row_count, heads_here) + grad_log * decay_rate
    grad_alog_here = jnp.sum(grad_log * log_decay, axis=0)
    grad_pre = grad_step_all * live_mask[:, None] * jax.nn.sigmoid(step_pre)
    grad_bias_here = jnp.sum(grad_pre, axis=0)
    grad_ext, grad_taps = conv_pull(
        jnp.concatenate([grad_x_low, grad_write_map, grad_read_map], axis=1)
    )
    rim_back = from_behind(grad_ext[: KCONV - 1], "tok", -1)
    grad_mixed = grad_ext[KCONV - 1 :].at[row_count - (KCONV - 1) :].add(rim_back)
    grad_zx_low = (
        jnp.stack([grad_gate, grad_mixed[:, :local_width]], axis=1)
        .astype(jnp.bfloat16)
        .reshape(row_count, 2 * local_width)
    )
    grad_pre_low = grad_pre.astype(jnp.bfloat16)
    normed_exact = normed_low.astype(jnp.float32)
    w_bc_exact = w_bc.astype(jnp.float32)
    grad_w_zx = contract(normed_low, grad_zx_low, 0, 0).reshape(D, 2, local_width)
    grad_w_dt = lax.dynamic_update_slice(
        jnp.zeros((D, H), jnp.float32),
        contract(normed_low, grad_pre_low, 0, 0),
        (zero_index, head_start),
    )
    grad_h_part = contract(grad_zx_low, zx_flat, 1, 1) + contract(grad_pre_low, w_dt_here, 1, 1)
    bc_partial = grad_mixed[:, local_width:]
    grad_bc_sum = lax.psum(bc_partial, "head")
    bc_cols = 2 * N // head_count
    bc_start = head_index * bc_cols
    bc_part = contract_exact(
        normed_exact, lax.dynamic_slice_in_dim(grad_bc_sum, bc_start, bc_cols, 1), 0, 0
    )
    grad_w_bc = lax.dynamic_update_slice(
        jnp.zeros((D, 2 * N), jnp.float32), bc_part, (zero_index, bc_start)
    )
    grad_h_bc = contract_exact(grad_bc_sum, w_bc_exact, 1, 1)
    grad_hidden = lax.psum(grad_h_part, "head")
    grad_hidden = grad_hidden + grad_h_bc
    own_cols = jnp.arange(D) // share_cols == head_index
    grad_norm_gain = jnp.where(own_cols, jnp.sum(grad_hidden * normed, axis=0), 0.0)
    row_dot = jnp.sum(grad_hidden * norm_gain * upcast, axis=1, keepdims=True)
    grad_in = inv_rms * norm_gain * grad_hidden - upcast * inv_rms**3 * row_dot / D + grad_resid

    def place_heads(values):
        return lax.dynamic_update_slice(jnp.zeros((H,), jnp.float32), values, (head_start,))

    sharded = lax.psum((grad_w_zx, grad_taps[:, :local_width], grad_gate_gain, grad_w_out), "tok")
    shared = lax.psum(
        (
            grad_norm_gain,
            grad_w_bc,
            grad_w_dt,
            place_heads(grad_bias_here),
            place_heads(grad_alog_here),
            grad_taps[:, local_width:],
            place_heads(grad_skip_here),
        ),
        ("tok", "head"),
    )
    return (
        block_out,
        grad_in,
        shared[0],
        sharded[0],
        shared[1],
        shared[2],
        shared[3],
        shared[4],
        sharded[1],
        shared[5],
        shared[6],
        sharded[2],
        sharded[3],
    )


def solution(mesh):
    return jax.shard_map(
        on_device,
        mesh=mesh,
        in_specs=(
            P("tok", None),
            P(),
            P(None, None, "head"),
            P(),
            P(),
            P(),
            P(),
            P(None, "head"),
            P(),
            P(),
            P("head"),
            P("head", None),
            P("tok", None),
            P("tok"),
            P("tok"),
        ),
        out_specs=(
            P("tok", None),
            P("tok", None),
            P(),
            P(None, None, "head"),
            P(),
            P(),
            P(),
            P(),
            P(None, "head"),
            P(),
            P(),
            P("head"),
            P("head", None),
        ),
        check_vma=False,
    )
```

profile of v0, /device:TPU:0, one launch (start us, length us, event | category | flops | bytes accessed | tf_op | source)
XLA Modules:
  0.0 964.6 jit_solution(6057639411973513614)
XLA Ops:
  40.5 5.1 fusion.92
  49.4 7.0 multiply_convert_fusion
  66.0 13.9 %while.95 = (s32[]{:T(128)}, f32[6]{0:T(128)S(1)}, f32[6,64,128]{2,1,0:T(8,128)S(1)}, f32[8,6]{1,0:T(8,128)}, f32[8,6,64,128]{3,2,1,0:T(8,128)}, /*index=5*/s32[]{:T(128)}, s32[]{:T(128)}) while((s32[]{:T(128)}, f32[6]{0:T(128)S(1)}, f32[6,64,128]{2,1,0:T(8,128)S(1)}, f32[8,6]{1,0:T(8,128)}, f32[8,6,64,128]{3,2,1,0:T(8,128)}, ...), condition=%wide.region_4.5_spmd.clone, body=%wide.region_3.4_spmd.clone.sunk | while | flops 147471 | bytes 590048 | solution.py:200
  91.7 19.7 %all-reduce.10 = f32[48]{0:T(128)S(1)} all-reduce(f32[48]{0:T(128)S(1)} %dynamic-update-slice.9), channel_id=2, replica_groups=mesh['tok'=8,'head'=4] {'tok'}, use_global_device_ids=true, to_apply=%add.10 | all-reduce | flops 48 | bytes 384
  114.4 10.9 %all-gather.7.cloned.1.call-done = f32[48,64,128]{2,1,0:T(8,128)} async-done(((f32[6,64,128]{2,1,0:T(8,128)}), f32[48,64,128]{2,1,0:T(8,128)}) %all-gather.7.cloned.1.call-update) | async-done | bytes 1572880 | tf_op jit(solution)/shard_map/all_gather | solution.py:26
  125.3 8.5 while.96
  135.2 29.6 %while.93 = (s32[]{:T(128)}, f32[6,64,128]{2,1,0:T(8,128)S(1)}, f32[8,6,64,128]{3,2,1,0:T(8,128)}, f32[8,6]{1,0:T(8,128)}, f32[8]{0:T(128)S(1)}, /*index=5*/f32[8,6,64,128]{3,2,1,0:T(8,128)}, s32[]{:T(128)}, f32[1]{0:T(128)}) while((s32[]{:T(128)}, f32[6,64,128]{2,1,0:T(8,128)S(1)}, f32[8,6,64,128]{3,2,1,0:T(8,128)}, f32[8,6]{1,0:T(8,128)}, ...), condition=%wide.region_8.9_spmd, body=%wide.region_7.8_spmd.sunk | while | flops 196611 | bytes 983757 | solution.py:212
  168.1 16.9 %bitcast_add_fusion.8 = f32[8,256,6,64]{1,3,2,0:T(8,128)S(1)} fusion(f32[8,256,6,64]{1,3,2,0:T(8,128)S(1)} %fusion.126, f32[8,256,256]{2,1,0:T(8,128)S(1)} %copy-done.34, f32[8,6,256]{2,1,0:T(8,128)S(1)} %copy-done.57, pred[256,256]{1,0:T(8,128)(4,1)} %iota_compare_fusion, f32[8,256,6,64]{1,0,3,2:T(8,128)S(1)} %bitcast.271, ...), kind=kOutput, calls=%fused_computation.94 | convolution fusion | flops 2430861312 | bytes 11747328 | tf_op jit(solution)/shard_map/jvp(khls,kshp->klhp)/dot_general | solution.py:92
  191.3 6.0 psum.112
  197.4 6.6 multiply_reduce_fusion.5
  204.0 6.3 psum.114
  223.1 13.9 %while.97 = (s32[]{:T(128)}, f32[6]{0:T(128)S(1)}, f32[6,64,128]{2,1,0:T(8,128)S(1)}, f32[8,6]{1,0:T(8,128)}, f32[8,6,64,128]{3,2,1,0:T(8,128)}, /*index=5*/s32[]{:T(128)}, s32[]{:T(128)}, s32[]{:T(128)}) while((s32[]{:T(128)}, f32[6]{0:T(128)S(1)}, f32[6,64,128]{2,1,0:T(8,128)S(1)}, f32[8,6]{1,0:T(8,128)}, ...), condition=%wide.region_15.16_spmd.clone, body=%wide.region_14.15_spmd.clone.sunk | while | flops 147472 | bytes 590068 | solution.py:249
  238.2 16.0 %fusion.19 = (f32[8,6,256]{2,1,0:T(8,128)}, f32[8,6,256]{2,1,0:T(8,128)}, f32[8,256,256]{2,1,0:T(8,128)S(1)}) fusion(f32[8,256,256]{2,1,0:T(8,128)} %fusion.125, f32[8,6,256]{2,1,0:T(8,128)S(1)} %copy-done.57, pred[256,256]{1,0:T(8,128)(4,1)S(1)} %copy-done.66, f32[8,256,6,64]{1,0,3,2:T(8,128)} %bitcast.268, f32[8,256,6]{1,2,0:T(8,128)S(1)} %bitcast.295, ...), kind=kOutput, calls=%fused_computation.46 | convolution fusion | flops 2450759680 | bytes 9175040 | tf_op jit(solution)/shard_map/transpose(jvp(khls,kshp->klhp))/dot_general | solution.py:92
  254.2 5.9 fusion.70
  265.0 20.3 %all-reduce.11 = f32[48]{0:T(128)S(1)} all-reduce(f32[48]{0:T(128)S(1)} %dynamic-update-slice.10), channel_id=4, replica_groups=mesh['tok'=8,'head'=4] {'tok'}, use_global_device_ids=true, to_apply=%add.11 | all-reduce | flops 48 | bytes 384
  285.4 5.4 fusion.115
  290.8 5.1 multiply_bitcast_fusion
  295.9 8.5 while.98
  304.7 30.8 %while.94 = (s32[]{:T(128)}, f32[6,64,128]{2,1,0:T(8,128)S(1)}, f32[8,6,64,128]{3,2,1,0:T(8,128)S(1)}, f32[8,6]{1,0:T(8,128)S(1)}, f32[8]{0:T(128)S(1)}, /*index...) while((s32[]{:T(128)}, f32[6,64,128]{2,1,0:T(8,128)S(1)}, ...), condition=%wide.region_20.21_spmd, body=%wide.region_18.20_spmd.sunk | while | flops 245764 | bytes 1180041 | solution.py:262
  335.5 7.9 fusion.71
  349.8 12.8 %multiply_reduce_fusion.7 = (f32[8,256,6]{1,2,0:T(8,128)}, f32[8,256,6]{1,2,0:T(8,128)}, f32[8,256,6,64]{1,3,2,0:T(8,128)S(1)}) fusion(f32[8,256,6,64]{1,3,2,0:T(8,128)} %fusion.127, f32[8,256,6,64]{1,0,3,2:T(8,128)} %bitcast.270, f32[8,256,6]{1,2,0:T(8,128)S(1)} %bitcast.297, f32[8,256,256]{2,1,0:T(8,128)} %fusion.125, f32[8,6,256]{2,1,0:T(8,128)S(1)} %copy-done.57, ...), kind=kOutput, calls=%fused_computation.100 | convolution fusion | flops 2434768896 | bytes 13418496 | tf_op jit(solution)/shard_map/transpose(jvp(khls,kshp->klhp))/dot_general | solution.py:92
  369.0 10.8 %multiply_reduce_fusion.3 = (f32[640]{0:T(1024)}, f32[640]{0:T(1024)}, f32[640]{0:T(1024)}, f32[640]{0:T(1024)}, f32[640]{0:T(1024)}, /*index=5*/f32[2048,640]{0,1:T(8,128)}) fusion(f32[2051,640]{0,1:T(8,128)S(1)} %bitcast.263, f32[2048]{0:T(1024)S(1)} %copy-done.61, f32[2048]{0:T(1024)S(1)} %get-tuple-element.881, f32[2048]{0:T(1024)S(1)} %get-tuple-element.880, ...), kind=kLoop, calls=%fused_computation.78 | loop fusion | flops 32764800 | bytes 36745728 | tf_op jit(solution)/shard_map/transpose(jvp())/reduce_sum | solution.py:77
  385.3 5.5 pad_add_fusion
  423.6 15.7 %reduce-window.26 = f32[8,6,2,128]{3,0,1,2:T(8,128)S(1)} reduce-window(f32[8,6,2,128]{3,0,1,2:T(8,128)} %copy.218, f32[]{:T(128)} %constant.408.clone.1), window={size=1x1x1x128 pad=0_0x0_0x0_0x0_127}, to_apply=%region_28.29 | reduce-window | flops 1560576 | bytes 98308 | tf_op jit(solution)/shard_map/reduce-window.5
  455.5 36.8 %all-reduce.14 = (f32[5,384]{1,0:T(8,128)}, f32[384]{0:T(512)}) all-reduce(f32[5,384]{1,0:T(8,128)S(1)} %slice.197, f32[384]{0:T(512)S(1)} %copy-done.102), channel_id=1, replica_groups=mesh['tok'=8,'head'=4] {'tok'}, use_global_device_ids=true, to_apply=%region_47.48 | all-reduce | flops 2304 | bytes 18432 | tf_op jit(solution)/shard_map/psum | solution.py:322
  492.2 52.3 %all-reduce.23.cloned.1.call-done = (f32[768,2,384]{2,0,1:T(8,128)}, f32[384,768]{1,0:T(8,128)}) async-done(((f32[768,2,384]{2,0,1:T(8,128)}, f32[384,768]{1,0:T(8,128)}), (f32[768,2,384]{2,0,1:T(8,128)}, f32[384,768]{1,0:T(8,128)})) %all-reduce.23.cloned.1.call-update) | async-done | bytes 3538960 | tf_op jit(solution)/shard_map/psum | solution.py:322
  549.5 252.9 %all-reduce.25.cloned.1.call-done = (f32[2048,768]{1,0:T(8,128)}, f32[2048,768]{1,0:T(8,128)}, f32[2048,256]{0,1:T(8,128)}) async-done(((f32[2048,768]{1,0:T(8,128)}, f32[2048,768]{1,0:T(8,128)}, f32[2048,256]{0,1:T(8,128)}), (f32[2048,768]{1,0:T(8,128)}, f32[2048,768]{1,0:T(8,128)}, f32[2048,256]{0,1:T(8,128)})) %all-reduce.25.cloned.1.call-update) | async-done | bytes 14680080 | tf_op jit(solution)/shard_map/psum | solution.py:225
  802.4 5.5 fusion.77
  808.0 10.8 %fusion.21 = (f32[768]{0:T(1024)S(1)}, f32[2048]{0:T(1024)S(1)}, f32[2048,768]{1,0:T(8,128)}) fusion(bf16[2048,768]{1,0:T(8,128)(2,1)S(1)} %copy-done.11, f32[2048]{0:T(1024)S(1)} %copy-done.59, f32[768]{0:T(1024)S(1)} %copy-done.77, f32[2048,768]{1,0:T(8,128)} %get-tuple-element.845, f32[2048,256]{0,1:T(8,128)S(1)} %copy-done.32, ...), kind=kOutput, calls=%fused_computation.50 | convolution fusion | flops 4844418048 | bytes 18241536 | tf_op jit(solution)/shard_map/dot_general | solution.py:53
  824.3 11.4 %fusion.27 = (f32[2048,768]{1,0:T(8,128)}, bf16[2048,768]{1,0:T(8,128)(2,1)}) fusion(bf16[2048,768]{1,0:T(8,128)(2,1)} %param.33, bf16[2048,768]{1,0:T(8,128)(2,1)} %param.45, f32[2048,768]{1,0:T(8,128)} %get-tuple-element.900, f32[2048]{0:T(1024)S(1)} %get-tuple-element.753, f32[2048]{0:T(1024)S(1)} %copy-done.83, f32[768]{0:T(1024)S(1)} %copy-done.77, ...), kind=kLoop, calls=%fused_computation.56 | loop fusion | flops 17301504 | bytes 28339200 | tf_op jit(solution)/shard_map/add | solution.py:317
  835.7 39.5 %all-reduce.12 = (f32[768]{0:T(1024)}, f32[24]{0:T(128)}, f32[24]{0:T(128)}, f32[5,256]{1,0:T(8,128)}, f32[24]{0:T(128)}) all-reduce(f32[768]{0:T(1024)S(1)} %fusion.106, f32[24]{0:T(128)S(1)} %dynamic_update_slice.40, f32[24]{0:T(128)S(1)} %dynamic_update_slice.41, ...), channel_id=1, replica_groups=mesh['tok'=8,'head'=4] {'tok','head'}, use_global_device_ids=true, to_apply=%region_34.35 | all-reduce | flops 2120 | bytes 16960 | tf_op jit(solution)/shard_map/psum | solution.py:323
  875.2 78.1 %all-reduce.21.cloned.1.call-done = (f32[768,256]{1,0:T(8,128)}, f32[768,24]{0,1:T(8,128)}) async-done(((f32[768,256]{1,0:T(8,128)}, f32[768,24]{0,1:T(8,128)}), (f32[768,256]{1,0:T(8,128)}, f32[768,24]{0,1:T(8,128)})) %all-reduce.21.cloned.1.call-update) | async-done | bytes 860176 | tf_op jit(solution)/shard_map/psum | solution.py:323
  (536 shorter events, 264.8 us)
Async XLA Ops:
  7.2 190.2 %copy-start = (bf16[384,768]{1,0:T(8,128)(2,1)S(1)}, bf16[384,768]{1,0:T(8,128)(2,1)}, u32[]{:S(2)}) copy-start(bf16[384,768]{1,0:T(8,128)(2,1)} %param.44) | copy-start | bytes 1769476
  7.2 118.1 %all-gather.7.cloned.1.call-start = ((), (), s32[]{:S(2)}) async-start(), calls=%async_computation | async-start | bytes 1769472 | tf_op jit(solution)/shard_map/all_gather | solution.py:26
  16.1 33.3 %copy-start.10 = (f32[2048,256]{0,1:T(8,128)}, f32[2048,256]{0,1:T(8,128)S(1)}, u32[]{:S(2)}) copy-start(f32[2048,256]{0,1:T(8,128)S(1)} %fusion.124) | copy-start | bytes 6291460
  25.1 20.7 %collective-permute-start = (f32[3,640]{0,1:T(8,128)}, f32[3,640]{0,1:T(8,128)S(1)}, u32[]{:S(2)}, u32[]{:S(2)}) collective-permute-start(f32[3,640]{0,1:T(8,128)} %fusion.79), channel_id=1, source_target_pairs={{0,4},{4,8},{8,12},{12,16},{16,20},{20,24},{24,28},{1,5},{5,9},{9,... | collective-permute-start | bytes 23048 | tf_op jit(solution)/shard_map/ppermute | solution.py:21
  57.4 233.4 %copy-start.14 = (bf16[2048,384]{0,1:T(8,128)(2,1)}, bf16[2048,384]{0,1:T(8,128)(2,1)S(1)}, u32[]{:S(2)}) copy-start(bf16[2048,384]{0,1:T(8,128)(2,1)S(1)} %slice.184) | copy-start | bytes 4718596
  62.4 22.2 %copy-start.35 = (bf16[2048,128]{0,1:T(8,128)(2,1)S(1)}, bf16[2048,128]{0,1:T(8,128)(2,1)}, u32[]{:S(2)}) copy-start(bf16[2048,128]{0,1:T(8,128)(2,1)} %get-tuple-element.870) | copy-start | bytes 1572868
  80.6 215.3 %all-gather.9.cloned.1.call-start = ((), (), s32[]{:S(2)}) async-start(), calls=%async_computation.1 | async-start | bytes 1769472 | tf_op jit(solution)/shard_map/all_gather | solution.py:26
  111.5 23.6 %copy-start.79 = (f32[8]{0:T(128)S(1)}, f32[8]{0:T(128)}, u32[]{:S(2)}) copy-start(f32[8]{0:T(128)} %copy-done.78) | copy-start | bytes 100
  135.2 32.9 %copy-start.51 = (f32[8,256,6]{1,2,0:T(8,128)S(1)}, f32[8,256,6]{1,2,0:T(8,128)}, u32[]{:S(2)}) copy-start(f32[8,256,6]{1,2,0:T(8,128)} %get-tuple-element.876) | copy-start | bytes 147460
  135.2 32.9 %copy-start.57 = (f32[8,6,256]{2,1,0:T(8,128)S(1)}, f32[8,6,256]{2,1,0:T(8,128)}, u32[]{:S(2)}) copy-start(f32[8,6,256]{2,1,0:T(8,128)} %copy-done.56) | copy-start | bytes 147460
  164.8 23.4 %slice-start.2 = ((s8[6291456]{0:T(1024)(128)(4,1)}), s8[4194304]{0:T(1024)(128)(4,1)S(1)}, s32[]{:S(2)}) async-start(s8[6291456]{0:T(1024)(128)(4,1)} %bitcast.274), calls=%async_computation.7 | async-start | bytes 8388608
  168.0 17.0 %copy-start.22 = (f32[8,256,6,64]{1,3,2,0:T(8,128)}, f32[8,256,6,64]{1,3,2,0:T(8,128)S(1)}, u32[]{:S(2)}) copy-start(f32[8,256,6,64]{1,3,2,0:T(8,128)S(1)} %fusion.126) | copy-start | bytes 9437188
  168.1 20.2 %slice-start.3 = ((s8[6291456]{0:T(1024)(128)(4,1)}), s8[2097152]{0:T(1024)(128)(4,1)S(1)}, s32[]{:S(2)}) async-start(s8[6291456]{0:T(1024)(128)(4,1)} %bitcast.274), calls=%async_computation.8 | async-start | bytes 4194304
  223.1 15.1 %copy-start.66 = (pred[256,256]{1,0:T(8,128)(4,1)S(1)}, pred[256,256]{1,0:T(8,128)(4,1)}, u32[]{:S(2)}) copy-start(pred[256,256]{1,0:T(8,128)(4,1)} %iota_compare_fusion) | copy-start | bytes 196612
  237.7 306.9 %all-reduce.23.cloned.1.call-start = ((), (), s32[]{:S(2)}) async-start(), calls=%async_computation.3 | async-start | bytes 7077888 | tf_op jit(solution)/shard_map/psum | solution.py:322
  238.1 16.0 %copy-start.7 = (f32[48,8,8,256]{3,2,1,0:T(8,128)S(1)}, f32[48,8,8,256]{3,2,1,0:T(8,128)}, u32[]{:S(2)}) copy-start(f32[48,8,8,256]{3,2,1,0:T(8,128)} %copy-done.6) | copy-start | bytes 9437188
  238.1 16.0 %copy-start.18 = (f32[8,6,64,128]{3,2,1,0:T(8,128)S(1)}, f32[8,6,64,128]{3,2,1,0:T(8,128)}, u32[]{:S(2)}) copy-start(f32[8,6,64,128]{3,2,1,0:T(8,128)} %get-tuple-element.1250) | copy-start | bytes 4718596
  304.7 30.9 %copy-start.48 = (f32[8,256,6]{1,2,0:T(8,128)S(1)}, f32[8,256,6]{1,2,0:T(8,128)}, u32[]{:S(2)}) copy-start(f32[8,256,6]{1,2,0:T(8,128)} %get-tuple-element.877) | copy-start | bytes 147460
  369.0 10.9 %copy-start.69 = (f32[640]{0:T(1024)S(1)}, f32[640]{0:T(1024)}, u32[]{:S(2)}) copy-start(f32[640]{0:T(1024)} %copy-done.68) | copy-start | bytes 7684
  369.0 10.9 %copy-start.71 = (f32[640]{0:T(1024)S(1)}, f32[640]{0:T(1024)}, u32[]{:S(2)}) copy-start(f32[640]{0:T(1024)} %copy-done.70) | copy-start | bytes 7684
  369.0 10.9 %copy-start.73 = (f32[640]{0:T(1024)S(1)}, f32[640]{0:T(1024)}, u32[]{:S(2)}) copy-start(f32[640]{0:T(1024)} %copy-done.72) | copy-start | bytes 7684
  384.0 10.6 %collective-permute-start.1 = (f32[3,640]{0,1:T(8,128)S(1)}, f32[3,640]{0,1:T(8,128)S(1)}, u32[]{:S(2)}, u32[]{:S(2)}) collective-permute-start(f32[3,640]{0,1:T(8,128)S(1)} %pad_add_fusion.1), channel_id=1, source_target_pairs={{4,0},{8,4},{12,8},{16,12},{20,16},{24,20},{28,24},{5,1},{9,5},{13... | collective-permute-start | bytes 23048 | tf_op jit(solution)/shard_map/ppermute | solution.py:21
  405.7 396.7 %all-reduce.25.cloned.1.call-start = ((), (), s32[]{:S(2)}) async-start(), calls=%async_computation.4 | async-start | bytes 29360128 | tf_op jit(solution)/shard_map/psum | solution.py:225
  410.7 28.9 %copy-start.50 = (f32[2048,6]{0,1:T(8,128)S(1)}, f32[2048,6]{0,1:T(8,128)}, u32[]{:S(2)}) copy-start(f32[2048,6]{0,1:T(8,128)} %copy-done.49) | copy-start | bytes 147460
  410.7 28.9 %copy-start.52 = (f32[2048,6]{0,1:T(8,128)S(1)}, f32[2048,6]{0,1:T(8,128)}, u32[]{:S(2)}) copy-start(f32[2048,6]{0,1:T(8,128)} %get-tuple-element.896) | copy-start | bytes 147460
  410.8 28.9 %copy-start.55 = (f32[1,2,8,128]{3,1,2,0:T(2,128)S(1)}, f32[1,2,8,128]{3,1,2,0:T(2,128)}, u32[]{:S(2)}) copy-start(f32[1,2,8,128]{3,1,2,0:T(2,128)} %copy-done.54) | copy-start | bytes 24580
  410.8 28.9 %copy-start.99 = (f32[6]{0:T(128)S(1)}, f32[6]{0:T(128)}, u32[]{:S(2)}) copy-start(f32[6]{0:T(128)} %copy-done.98) | copy-start | bytes 76
  415.4 28.6 %copy-start.44 = (bf16[768,2,384]{2,1,0:T(2,128)(2,1)S(1)}, bf16[768,2,384]{2,1,0:T(2,128)(2,1)}, u32[]{:S(2)}) copy-start(bf16[768,2,384]{2,1,0:T(2,128)(2,1)} %param.35) | copy-start | bytes 3538948
  451.2 502.1 %all-reduce.21.cloned.1.call-start = ((), (), s32[]{:S(2)}) async-start(), calls=%async_computation.2 | async-start | bytes 1720320 | tf_op jit(solution)/shard_map/psum | solution.py:323
  455.1 352.9 %copy-start.53 = (f32[768,24]{0,1:T(8,128)}, f32[768,24]{0,1:T(8,128)S(1)}, u32[]{:S(2)}) copy-start(f32[768,24]{0,1:T(8,128)S(1)} %dynamic_update_slice.39) | copy-start | bytes 221188
  808.0 16.2 %copy-start.83 = (f32[2048]{0:T(1024)S(1)}, f32[2048]{0:T(1024)}, u32[]{:S(2)}) copy-start(f32[2048]{0:T(1024)} %get-tuple-element.884) | copy-start | bytes 24580
  824.3 132.6 %copy-start.45 = (f32[384,768]{1,0:T(8,128)S(1)}, f32[384,768]{1,0:T(8,128)}, u32[]{:S(2)}) copy-start(f32[384,768]{1,0:T(8,128)} %get-tuple-element.1291) | copy-start | bytes 3538948
  (93 other events, 429.9 us)
Sparse Core Ops, SparseCore 0:
  80.7 44.5 all-gather.6
  237.8 43.0 all-gather.8
  405.8 138.7 all-reduce.22
  548.1 254.2 all-reduce.24
  824.4 128.8 all-reduce.20
where the time goes:
time: 973 us; the launch traced here: 965 us
  waiting for transfers between devices  394 us (40%)
  other arithmetic  176 us (18%)
  matrix products  134 us (14%)
  blocking collectives  129 us (13%)
  local copies, waits for them, and re-layouts  96.4 us (10%)
  between operations  16.4 us (2%)
  loops' own time  12 us (1%)
    psum x1, waiting for transfers between devices, on_device(): block_out = (upcast + lax.psum(partial_value, 'head')).astype(jnp.bfloat16)  253 us
    psum x1, waiting for transfers between devices, on_device(): lax.psum((grad_norm_gain, grad_w_bc, grad_w_dt, place_heads(grad_bias_her...  78.1 us
    psum x1, waiting for transfers between devices, on_device(): lax.psum((grad_w_zx, grad_taps[:, :local_width], grad_gate_gain, grad_w_o...  52.3 us
    dot_general x3, matrix products, group_inner(): within = jnp.einsum('khls,kshp->klhp', weights, x_scaled, precision=PRECISE)  45.7 us
    unnamed x2, blocking collectives  40 us
    psum x1, blocking collectives, on_device(): lax.psum((grad_norm_gain, grad_w_bc, grad_w_dt, place_heads(grad_bias_her...  39.5 us
    psum x1, blocking collectives, on_device(): lax.psum((grad_w_zx, grad_taps[:, :local_width], grad_gate_gain, grad_w_o...  36.8 us
    unnamed x258, local copies, waits for them, and re-layouts  31.5 us
  transfers between devices with their start and end apart: 7, of which 4 were waited for; matrix products, arithmetic and copies ran while one was open for 14% of the time, Pallas kernels for 0%

commit v1 on v0

v1 whole, which is shorter than its diff:
```python
import functools

import jax
import jax.numpy as jnp
from jax import lax
from jax.experimental import pallas as pl
from jax.experimental.pallas import tpu as pltpu
from jax.sharding import PartitionSpec as P

P_SIZE = 64
N = 128
KCONV = 4
GROUP = 256
CHUNK = 128
LANES = 128
PARTS = GROUP // CHUNK
EPS = 1e-05
VMEM_LIMIT = 16 * 1024 * 1024
F32 = jnp.float32
BF16 = jnp.bfloat16


def mm(a, b, ca=1, cb=0):
    return lax.dot_general(a, b, (((ca,), (cb,)), ((), ())), preferred_element_type=F32)


def iota(shape, dim):
    return lax.broadcasted_iota(jnp.int32, shape, dim)


def spread(cols, width):
    rows = cols.shape[0]
    low = iota((rows, LANES), 1) < P_SIZE
    tiles = [
        jnp.where(low, cols[:, 2 * p : 2 * p + 1], cols[:, 2 * p + 1 : 2 * p + 2])
        for p in range(width // LANES)
    ]
    return jnp.concatenate(tiles, axis=1)


def gather_heads(width):
    return (iota((width, LANES), 0) // P_SIZE == iota((width, LANES), 1)).astype(BF16)


def fold_rows(value):
    rows, width = value.shape
    return value.reshape(rows // 8, 8, width).sum(axis=0)


def tri(kind):
    row, col = iota((CHUNK, CHUNK), 0), iota((CHUNK, CHUNK), 1)
    return {"le": col <= row, "ge": col >= row, "lt": col < row}[kind]


def pair_rows(tile):
    low = iota(tile.shape, 1) < P_SIZE
    zero = jnp.zeros_like(tile)
    return jnp.concatenate([jnp.where(low, tile, zero), jnp.where(low, zero, tile)], axis=0)


def split2(value):
    high = value.astype(BF16)
    return high, (value - high.astype(F32)).astype(BF16)


def split3(value):
    high, rest = split2(value)
    return high, rest, (value - high.astype(F32) - rest.astype(F32)).astype(BF16)


def mm_left(a, b, ca=1, cb=0):
    high, low = split2(a)
    return mm(high, b, ca, cb) + mm(low, b, ca, cb)


def mm_right(a, b, ca=1, cb=0):
    high, low = split2(b)
    return mm(a, high, ca, cb) + mm(a, low, ca, cb)


def mm_both(a, b, ca=1, cb=0):
    ah, al = split2(a)
    bh, bl = split2(b)
    return mm(ah, bh, ca, cb) + mm(al, bh, ca, cb) + mm(ah, bl, ca, cb)


def stacked(value):
    return jnp.concatenate(
        [value[:, c : c + LANES] for c in range(0, value.shape[1], LANES)], axis=0
    )


def tree(terms):
    while len(terms) > 1:
        terms = [terms[k] + terms[k + 1] for k in range(0, len(terms), 2)]
    return terms[0]


def rms_inv(u):
    return lax.rsqrt(jnp.mean(u * u, axis=1, keepdims=True) + EPS)


def k_project(hid, gain, w_x, w_bc, w_dt, hp, h_o, v_o, pre_o):
    width = w_x.shape[1]
    u = hid[...].astype(F32)
    h = (u * rms_inv(u) * gain[...]).astype(BF16)
    h_o[...] = h
    v_o[:, :width] = mm(h, w_x[...])
    v_o[:, width:] = mm(h, w_bc[...])
    pre_o[...] = mm(h, w_dt[...]) + hp[0:1, :]


def k_conv(
    first, valid, v, pre, rim, gain, w_x, w_bc, hp, cx, cb,
    cv_o, xs_o, bc_o, dt_o, cum_o, ent_o, pd_o, fin_o,
    vbuf, state, decay,
):
    g = pl.program_id(0)
    width = w_x.shape[1]

    @pl.when(g == 0)
    def _():
        u = rim[...].astype(F32)
        hr = (u * rms_inv(u) * gain[...]).astype(BF16)
        vbuf[0:8, :width] = mm(hr, w_x[...])[8:16]
        vbuf[0:8, width:] = mm(hr, w_bc[...])[8:16]
        state[...] = jnp.zeros_like(state)
        decay[...] = jnp.ones_like(decay)

    keep = 1.0 - first[g].astype(F32)
    vbuf[0:8, :] = vbuf[0:8, :] * keep
    state[...] = state[...] * keep
    decay[...] = decay[...] * keep
    vbuf[8:, :] = v[...]
    taps = jnp.concatenate([cx[...], cb[...]], axis=1)
    conv = taps[KCONV : KCONV + 1, :] + taps[0:1, :] * vbuf[5 : 5 + GROUP, :]
    for k in range(1, KCONV):
        conv = conv + taps[k : k + 1, :] * vbuf[5 + k : 5 + k + GROUP, :]
    cv_o[...] = conv
    act = (conv * jax.nn.sigmoid(conv)).astype(BF16)
    xs_o[...] = act[:, :width]
    bc_o[...] = act[:, width:]
    vbuf[0:8, :] = vbuf[GROUP : GROUP + 8, :]
    raw = pre[...]
    live = iota((GROUP, LANES), 0) < valid[g]
    soft = jnp.maximum(raw, 0.0) + jnp.log1p(jnp.exp(-jnp.abs(raw)))
    dt = jnp.where(live, soft, 0.0)
    dt_o[...] = dt
    ld = dt * -jnp.exp(hp[1:2, :])
    lower = tri("le").astype(BF16)
    lower = jnp.concatenate([lower] * 3, axis=1)
    for c in range(PARTS):
        rows = slice(c * CHUNK, (c + 1) * CHUNK)
        cum = mm(lower, jnp.concatenate(split3(ld[rows]), axis=0))
        cum_o[rows, :] = cum
        end = cum[CHUNK - 1 : CHUNK, :]
        factor = dt[rows] * jnp.exp(end - cum)
        ent_o[c] = state[...]
        pd_o[c] = decay[0:1]
        xd = act[rows, :width].astype(F32) * spread(factor, width)
        new = mm_right(act[rows, width : width + N], xd, 0, 0)
        ec = spread(jnp.exp(end), width)
        state[...] = state[...] * ec + new
        decay[...] = decay[...] * ec

    @pl.when(g == pl.num_programs(0) - 1)
    def _():
        fin_o[0:N, :] = state[...]
        fin_o[N:, :] = decay[...]


def k_proj(h, og, w_z, w_out, z_o, gyn_o):
    z_o[...] = mm(h[...], w_z[...])
    gyn_o[...] = mm(og[...], w_out[...], 1, 1)


def k_within(xs, bc, dt, cum, y_o):
    width = xs.shape[1]
    mask = tri("le")
    for c in range(PARTS):
        rows = slice(c * CHUNK, (c + 1) * CHUNK)
        scores = mm(bc[rows, N:], bc[rows, :N], 1, 1)
        a = cum[rows, :]
        b = jnp.transpose(a - jnp.log(dt[rows, :]))
        for p in range(width // LANES):
            lanes = slice(p * LANES, (p + 1) * LANES)
            weights = []
            for h in (2 * p, 2 * p + 1):
                gap = a[:, h : h + 1] - b[h : h + 1, :]
                weights.append(jnp.where(mask, jnp.exp(gap), 0.0) * scores)
            y_o[rows, lanes] = mm_left(jnp.concatenate(weights, axis=1), pair_rows(xs[rows, lanes]))


def k_gate(ent, pd, prev, bc, cum, yw, xs, z, gyn, gain, hp, mix_o, ent_o, sums_o):
    width = xs.shape[1]
    skip = spread(hp[2:3, :], width)
    for c in range(PARTS):
        rows = slice(c * CHUNK, (c + 1) * CHUNK)
        entry = ent[c] + pd[c] * prev[0:N, :]
        ent_o[c] = entry
        across = mm_right(bc[rows, N:], entry) * spread(jnp.exp(cum[rows, :]), width)
        mix_o[rows, :] = yw[rows, :] + across + skip * xs[rows, :].astype(F32)
    zz = z[...]
    gated = mix_o[...] * (zz * jax.nn.sigmoid(zz))
    square = jnp.sum(gated * gated, axis=1, keepdims=True)
    inner = jnp.sum(gyn[...] * gain[...] * gated, axis=1, keepdims=True)
    lane = iota((GROUP, LANES), 1)
    both = jnp.where(lane == 0, square, inner)
    sums_o[...] = jnp.transpose(both)[0:2, :]


def k_gate_back(
    total, count, first, mix, z, gyn, gain, xs, bc, cum, *rest,
):
    sums = rest[:count]
    yn_o, g_o, gz_o, ds_o, qd_o, again_o, askip_o, fin_o, state, decay = rest[count:]
    i = pl.program_id(0)
    g = pl.num_programs(0) - 1 - i
    width = xs.shape[1]

    @pl.when(i == 0)
    def _():
        state[...] = jnp.zeros_like(state)
        decay[...] = jnp.ones_like(decay)
        again_o[...] = jnp.zeros_like(again_o)
        askip_o[...] = jnp.zeros_like(askip_o)

    rows2 = tree([part[...] for part in sums])
    both = jnp.transpose(jnp.concatenate([rows2, jnp.zeros((LANES - 2, GROUP), F32)], axis=0))
    inv = lax.rsqrt(both[:, 0:1] / total + EPS)
    inner = both[:, 1:2] / total
    zz = z[...]
    sig = jax.nn.sigmoid(zz)
    silu = zz * sig
    mixer = mix[...]
    gated = mixer * silu
    scaled = gated * inv
    gy = gyn[...]
    gn = gain[...]
    yn_o[...] = (scaled * gn).astype(BF16)
    again_o[...] += fold_rows(gy * scaled)
    gg = inv * gn * gy - gated * (inv * inv * inv * inner)
    gm = (gg * silu).astype(BF16)
    g_o[...] = gm
    gz_o[...] = (gg * mixer * sig * (1.0 + zz * (1.0 - sig))).astype(BF16)
    gmf = gm.astype(F32)
    askip_o[...] += fold_rows(gmf * xs[...].astype(F32))
    for c in reversed(range(PARTS)):
        rows = slice(c * CHUNK, (c + 1) * CHUNK)
        ecum = spread(jnp.exp(cum[rows, :]), width)
        ds_o[c] = state[...]
        qd_o[c] = decay[0:1]
        new = mm_right(bc[rows, N:], gmf[rows] * ecum, 0, 0)
        ec = ecum[CHUNK - 1 : CHUNK, :]
        state[...] = state[...] * ec + new
        decay[...] = decay[...] * ec
    keep = 1.0 - first[g].astype(F32)
    state[...] = state[...] * keep
    decay[...] = decay[...] * keep

    @pl.when(i == pl.num_programs(0) - 1)
    def _():
        fin_o[0:N, :] = state[...]
        fin_o[N:, :] = decay[...]


def k_weights(place, yn, og, h, gz, keep_o, send_o, acc_z, acc_out):
    i = pl.program_id(0)

    @pl.when(i == 0)
    def _():
        acc_z[...] = jnp.zeros_like(acc_z)
        acc_out[...] = jnp.zeros_like(acc_out)

    acc_z[...] += mm(h[...], gz[...], 0, 0)
    acc_out[...] += mm(yn[...], og[...], 0, 0)

    @pl.when(i == pl.num_programs(0) - 1)
    def _():
        count = keep_o.shape[0]
        rz, ro = acc_z.shape[0] // (2 * count), acc_out.shape[0] // (2 * count)
        side = place[3] % 2
        for k in range(count):
            for out, at in ((keep_o, 2 * k + side), (send_o, 2 * k + 1 - side)):
                out[k] = jnp.concatenate(
                    [
                        stacked(acc_z[pl.ds(pl.multiple_of(at * rz, 8), rz), :]),
                        stacked(acc_out[pl.ds(pl.multiple_of(at * ro, 8), ro), :]),
                    ],
                    axis=0,
                )


def k_pair(place, keep, arrived, *outs):
    for k, out in enumerate(outs):
        at = (place[3] // 2) ^ k
        out[...] = (keep[at] + arrived[at]).astype(BF16)


def k_join(mask, place, mine, other, out):
    count = mine.shape[0]
    upper = (place[3] // mask) % 2
    out[pl.ds(upper * count, count)] = mine[...]
    out[pl.ds((1 - upper) * count, count)] = other[...]


def k_within_back(
    xs, bc, g, dt, cum, mix, ent, hp,
    dxw_o, dbc_o, rq_o, qw_o,
):
    width = xs.shape[1]
    mask = tri("ge")
    heads = gather_heads(width)
    skip = spread(hp[2:3, :], width)
    for c in range(PARTS):
        rows = slice(c * CHUNK, (c + 1) * CHUNK)
        bw, cr = bc[rows, :N], bc[rows, N:]
        scores = mm(bw, cr, 1, 1)
        a = cum[rows, :]
        b = a - jnp.log(dt[rows, :])
        at = jnp.transpose(a)
        dscore = jnp.zeros((CHUNK, CHUNK), F32)
        for p in range(width // LANES):
            lanes = slice(p * LANES, (p + 1) * LANES)
            decays = [
                jnp.where(mask, jnp.exp(at[h : h + 1, :] - b[:, h : h + 1]), 0.0)
                for h in (2 * p, 2 * p + 1)
            ]
            gt = g[rows, lanes]
            pairs = mm(pair_rows(xs[rows, lanes]), gt, 1, 1)
            dscore = dscore + pairs[:CHUNK] * decays[0] + pairs[CHUNK:] * decays[1]
            weights = jnp.concatenate([d * scores for d in decays], axis=1)
            dxw_o[rows, lanes] = mm_left(weights, pair_rows(gt))
        high, low = split2(dscore)
        gf = g[rows, :].astype(F32)
        xf = xs[rows, :].astype(F32)
        ge = gf * spread(jnp.exp(a), width)
        dbc_o[rows, :N] = mm(high, cr) + mm(low, cr)
        dbc_o[rows, N:] = mm(high, bw, 0, 0) + mm(low, bw, 0, 0) + mm_both(ge, ent[c], 1, 1)
        row_part = mm_left(gf * (mix[rows, :] - skip * xf), heads)
        col_part = mm_left(xf * dxw_o[rows, :], heads)
        rq_o[rows, :] = row_part - col_part
        qw_o[rows, :] = col_part


def silu_slope(value):
    sig = jax.nn.sigmoid(value)
    return sig * (1.0 + value * (1.0 - sig))


def k_rim(first, xs, bc, g, dt, cum, cend, dxw, dbc, cv, ds, qd, endg, hp, out, lead_o):
    i = pl.program_id(0)
    width = xs.shape[1]
    d_state = ds[0] + qd[0] * endg[0:N, :]
    factor = spread(dt[...] * jnp.exp(cend[7:8, :] - cum[...]), width)
    skip = spread(hp[2:3, :], width)
    xd = xs[...].astype(F32) * factor
    gx = dxw[...] + factor * mm_right(bc[:, :N], d_state) + g[...].astype(F32) * skip
    gb = dbc[:, :N] + mm_both(xd, d_state, 1, 1)
    slope = silu_slope(cv[...]) * (1.0 - first[i].astype(F32))
    out[0, :, :width] = gx * slope[:, :width]
    out[0, :, width : width + N] = gb * slope[:, width : width + N]
    out[0, :, width + N :] = dbc[:, N:] * slope[:, width + N :]

    @pl.when(i == 0)
    def _():
        lead_o[...] = out[0, 0:8, :]


def k_back(
    place, valid, h, xs, bc, g, pre, dt, cum, v, cv, dxw, dbc, rq, qw, ent, ds, qd, endg,
    rims, rim_in, cx, cb, hp, acc_gain, acc_skip,
    gx_o, gbc_o, gpre_o, grads_o, keep_o, send_o,
    gbuf, small_o, acc_x, acc_bc, acc_dt, acc_taps, acc_heads,
):
    i = pl.program_id(0)
    last = pl.num_programs(0) - 1
    width = xs.shape[1]
    heads = gather_heads(width)
    skip = spread(hp[2:3, :], width)
    rate = -jnp.exp(hp[1:2, :])

    @pl.when(i == 0)
    def _():
        for ref in (acc_x, acc_bc, acc_dt, acc_taps, acc_heads):
            ref[...] = jnp.zeros_like(ref)

    upper, below = tri("ge").astype(BF16), tri("lt").astype(BF16)
    both = jnp.concatenate([upper, upper, below, below], axis=1)
    for c in range(PARTS):
        rows = slice(c * CHUNK, (c + 1) * CHUNK)
        d_state = ds[c] + qd[c] * endg[0:N, :]
        d_high, d_low = split2(d_state)
        a = cum[rows, :]
        end = a[CHUNK - 1 : CHUNK, :]
        factor = spread(dt[rows, :] * jnp.exp(end - a), width)
        xf = xs[rows, :].astype(F32)
        bw = bc[rows, :N]
        dxs = factor * (mm(bw, d_high) + mm(bw, d_low))
        x_high, x_low = split2(xf * factor)
        gb = dbc[rows, :N] + (mm(x_high, d_high, 1, 1) + mm(x_low, d_high, 1, 1) + mm(x_high, d_low, 1, 1))
        gx = dxw[rows, :] + dxs + g[rows, :].astype(F32) * skip
        slope = silu_slope(cv[rows, :])
        gbuf[rows, :width] = gx * slope[:, :width]
        gbuf[rows, width : width + N] = gb * slope[:, width : width + N]
        gbuf[rows, width + N :] = dbc[rows, N:] * slope[:, width + N :]
        qs = mm_left(xf * dxs, heads)
        carried = mm_left(fold_rows(d_state * ent[c]), heads)
        ends = jnp.sum(carried, axis=0, keepdims=True) * jnp.exp(end)
        g_ld = mm(both, jnp.concatenate(split2(rq[rows, :]) + split2(qs), axis=0)) + ends
        step = dt[rows, :]
        direct = jnp.where(step > 0.0, (qw[rows, :] + qs) / jnp.where(step > 0.0, step, 1.0), 0.0)
        live = iota((CHUNK, LANES), 0) + c * CHUNK < valid[i]
        own = iota((CHUNK, LANES), 1) < width // P_SIZE
        g_pre = jnp.where(
            live & own, (direct + g_ld * rate) * jax.nn.sigmoid(pre[rows, :]), 0.0
        )
        acc_heads[0:8, :] += fold_rows(g_pre)
        acc_heads[8:16, :] += fold_rows(g_ld * step * rate)
        low = g_pre.astype(BF16)
        gpre_o[rows, :] = low
        acc_dt[...] += mm(pltpu.roll(low.astype(F32), place[1], 1).astype(BF16), h[rows, :], 0, 0)[0 : acc_dt.shape[0]]

    @pl.when(i < last)
    def _():
        gbuf[GROUP:, :] = rims[0, 0:8, :]

    @pl.when(i == last)
    def _():
        gbuf[GROUP:, :] = rim_in[0:8, :]

    taps = jnp.concatenate([cx[...], cb[...]], axis=1)
    vv = v[...]
    gv = jnp.zeros_like(vv)
    for k in range(KCONV):
        shifted = gbuf[KCONV - 1 - k : KCONV - 1 - k + GROUP, :]
        gv = gv + taps[k : k + 1, :] * shifted
        acc_taps[8 * k : 8 * k + 8, :] += fold_rows(vv * shifted)
    acc_taps[8 * KCONV :, :] += fold_rows(gbuf[0:GROUP, :])
    gx_low = gv[:, :width].astype(BF16)
    bc_high, bc_low = split2(gv[:, width:])
    gx_o[...] = gx_low
    gbc_o[:, : 2 * N] = bc_high
    gbc_o[:, 2 * N :] = bc_low
    hh = h[...]
    acc_x[...] += mm(hh, gx_low, 0, 0)
    acc_bc[...] += mm(hh, bc_high, 0, 0) + mm(hh, bc_low, 0, 0)

    @pl.when(i == last)
    def _():
        count = grads_o.shape[0]
        rx = acc_x.shape[0] // count
        for k in range(count):
            grads_o[k] = stacked(acc_x[k * rx : (k + 1) * rx, :]).astype(BF16)
        dim = acc_bc.shape[0]
        at = 0

        def put(value):
            nonlocal at
            small_o[at : at + value.shape[0], :] = value
            at += value.shape[0]

        put(acc_bc[:, :LANES])
        put(acc_bc[:, LANES:])
        put(stacked(acc_dt[...]))

        def line(value):
            return jnp.sum(value, axis=0, keepdims=True)

        def lane_home(value):
            return pltpu.roll(jnp.broadcast_to(value, (8, LANES)), place[1], 1)[0:1]

        own = iota((1, LANES), 1) < width // P_SIZE
        taps_sum = [line(acc_taps[8 * k : 8 * k + 8, :]) for k in range(KCONV + 1)]
        skips = mm_left(acc_skip[...], heads)
        head_rows = [
            lane_home(jnp.where(own, line(x), 0.0))
            for x in (acc_heads[0:8, :], acc_heads[8:16, :], skips)
        ]
        put(jnp.concatenate([t[:, width : width + N] for t in taps_sum] + head_rows, axis=0))
        spare = jnp.zeros((8 - KCONV - 1, LANES), F32)
        put(jnp.concatenate([t[:, width + N :] for t in taps_sum] + [spare], axis=0))
        small_o[at:, :] = jnp.zeros_like(small_o[at:, :])
        gains = line(acc_gain[...])
        tiles = width // LANES
        own_rows = jnp.concatenate(
            [
                jnp.concatenate(
                    [t[:, k * LANES : (k + 1) * LANES] for t in taps_sum]
                    + [gains[:, k * LANES : (k + 1) * LANES], spare[0:2]],
                    axis=0,
                )
                for k in range(tiles)
            ],
            axis=0,
        )
        small_o[pl.ds(pl.multiple_of(at + place[2] * (8 * tiles), 8), 8 * tiles), :] = own_rows
        rows = keep_o.shape[0]
        keep_o[...] = small_o[pl.ds(pl.multiple_of(place[0] * rows, 8), rows), :]
        send_o[...] = small_o[pl.ds(pl.multiple_of((1 - place[0]) * rows, 8), rows), :]


def input_grad(hid, gz, gx, gbc, gpre, w_z, w_x, w_bc, w_dt):
    gh = (
        mm(gpre[...], w_dt[...], 1, 1)
        + mm(gz[...], w_z[...], 1, 1)
        + mm(gx[...], w_x[...], 1, 1)
        + mm(gbc[:, : 2 * N], w_bc[...], 1, 1)
        + mm(gbc[:, 2 * N :], w_bc[...], 1, 1)
    )
    u = hid[...].astype(F32)
    return gh, fold_rows(gh * (u * rms_inv(u)))


def k_input_sent(place, *refs):
    out, norm_o = refs[9:]

    @pl.when(pl.program_id(0) == 0)
    def _():
        norm_o[...] = jnp.zeros_like(norm_o)

    gh, norm = input_grad(*refs[:9])
    out[...] = gh
    norm_o[...] += norm


def k_input_own(place, *refs):
    arrived, before, out, norm_o, acc = refs[9:]
    i = pl.program_id(0)

    @pl.when(i == 0)
    def _():
        acc[...] = before[...]

    gh, norm = input_grad(*refs[:9])
    out[...] = (gh + arrived[...]).astype(BF16)
    acc[...] += norm

    @pl.when(i == pl.num_programs(0) - 1)
    def _():
        rows = acc.shape[1] // LANES
        norm_o[0:rows, :] = stacked(jnp.sum(acc[...], axis=0, keepdims=True))
        norm_o[rows:, :] = jnp.zeros((8 - rows, LANES), F32)


def k_reduce(*refs):
    out = refs[-1]
    out[...] = tree([part[...].astype(F32) for part in refs[:-1]]).astype(BF16)


def k_halve(mask, place, kept, arrived, keep_o, send_o):
    rows = keep_o.shape[0]
    upper = (place[2] // mask) % 2
    for out, at in ((keep_o, upper * rows), (send_o, (1 - upper) * rows)):
        at = pl.multiple_of(at, 8)
        out[...] = kept[pl.ds(at, rows), :] + arrived[pl.ds(at, rows), :]


def k_pieces(kept, arrived, norm, out):
    count = out.shape[0]
    rows = kept.shape[0] // count
    spare = jnp.zeros((7, LANES), F32)
    for k in range(count):
        own = slice(k * rows, (k + 1) * rows)
        out[k, 0:rows, :] = kept[own, :] + arrived[own, :]
        line = norm[k : k + 1, :] if k < 8 else spare[0:1]
        out[k, rows:, :] = jnp.concatenate([line, spare], axis=0)


def k_reduce_both(large, small, out):
    count = out.shape[0]
    total = tree([large[k].astype(F32) for k in range(count)]).astype(BF16)
    rest = tree([small[k] for k in range(count)])
    joined = jnp.concatenate([total, *split2(rest)], axis=0)
    for k in range(count):
        out[k] = joined


def k_quarter(cut, parts, out):
    count = parts.shape[0]
    rows = out.shape[0] // count - 1
    for k in range(count):
        value = parts[k, cut:, :].astype(F32)
        value = value[: rows + 8] + value[rows + 8 :]
        out[k * rows : (k + 1) * rows, :] = value[:rows]
        out[count * rows + k : count * rows + k + 1, :] = value[rows : rows + 1]


def unstack(value, rows):
    return jnp.concatenate(
        [value[k : k + rows, :] for k in range(0, value.shape[0], rows)], axis=1
    )


def k_unpack(place, mine, other, b, w_zx_o, w_out_o):
    count = b.shape[0]
    dim, _, real = w_zx_o.shape
    rz = dim // count
    width = -(-real // LANES) * LANES
    cut = rz * width // LANES
    ro = width // count
    side = place[3] % 2
    for k in range(count // 2):
        for part, at in ((mine, 2 * k + side), (other, 2 * k + 1 - side)):
            piece = part[k].astype(F32)
            w_zx_o[pl.ds(at * rz, rz), 0, :] = unstack(piece[0:cut], rz)[:, :real]
            w_out_o[pl.ds(pl.multiple_of(at * ro, 8), ro), :] = unstack(piece[cut:], ro)
    for k in range(count):
        own = unstack(b[k, 0:cut, :].astype(F32), rz)[:, :real]
        w_zx_o[k * rz : (k + 1) * rz, 1, :] = own


def k_small(place, *refs):
    count = len(refs) - 9
    w_bc_o, w_dt_o, bc_taps_o, bias_o, alog_o, skip_o, norm_o, own_o, buf = refs[count:]
    quarter = buf.shape[0] // count
    norms = []
    for k in range(count):
        from_head, at = place[2] ^ k, 0
        for mask in powers(count):
            at = 2 * at + (from_head // mask) % 2
        buf[pl.ds(pl.multiple_of(at * quarter, 8), quarter), :] = refs[k][0:quarter, :]
        norms.append(refs[k][quarter : quarter + 8, :])
    norm = tree(norms)
    dim = w_bc_o.shape[0]
    for k in range(dim // LANES):
        norm_o[:, k * LANES : (k + 1) * LANES] = norm[k : k + 1, :]
    w_bc_o[:, :LANES] = buf[0:dim, :]
    w_bc_o[:, LANES:] = buf[dim : 2 * dim, :]
    at = 2 * dim
    heads = w_dt_o.shape[0]
    w_dt_o[...] = unstack(buf[at : at + heads * dim // LANES, :], heads)
    at += heads * dim // LANES
    bc_taps_o[...] = unstack(buf[at : at + 16, :], 8)[0 : KCONV + 1]
    for k, out in enumerate((bias_o, alog_o, skip_o)):
        out[...] = buf[at + KCONV + 1 + k : at + KCONV + 2 + k, 0 : out.shape[1]]
    tiles = -(-own_o.shape[1] // LANES)
    own = buf[pl.ds(pl.multiple_of(at + 16 + place[2] * (8 * tiles), 8), 8 * tiles), :]
    own_o[...] = unstack(own, 8)[:, 0 : own_o.shape[1]]


def k_out(hid, *refs):
    count = (len(refs) - 1) // 2
    out = refs[-1]
    total = tree([mm(refs[k][...], refs[count + k][...]) for k in range(count)])
    out[...] = (hid[...].astype(F32) + total).astype(BF16)


def k_in_back(place, hid, og, gain, *refs):
    i = pl.program_id(0)
    half = pl.num_programs(0) // 2
    count = (len(refs) - 1) // 2
    out = refs[-1]

    def finish(parts):
        gh = tree([part[...].astype(F32) for part in parts])
        u = hid[...].astype(F32)
        inv = rms_inv(u)
        scaled = gh * gain[...]
        dot = jnp.sum(scaled * u, axis=1, keepdims=True) / u.shape[1]
        out[...] = inv * scaled - u * (inv * inv * inv * dot) + og[...].astype(F32)

    @pl.when(i < half)
    def _():
        finish(refs[:count])

    @pl.when(i >= half)
    def _():
        finish(refs[count : 2 * count])


def row_block(shape, rows, at=None):
    at = at or (lambda i, *s: i)
    rest = tuple(shape[1:])
    return pl.BlockSpec((rows,) + rest, lambda i, *s: (at(i, *s),) + (0,) * len(rest))


def whole(shape):
    return pl.BlockSpec(tuple(shape), lambda i, *s: (0,) * len(shape))


SMEM = pl.BlockSpec(memory_space=pltpu.SMEM)


class Kept:
    def __init__(self, rows, at=None):
        self.rows = rows
        self.at = at or (lambda i, *s: i)

    def view(self, ref, i, scalars):
        start = pl.multiple_of(self.at(i, *scalars) * self.rows, self.rows)
        return ref.at[pl.ds(start, self.rows)]


def call(kernel, steps, ins, outs, scratch, flops, name, place=None):
    moved = sum(a.size * a.dtype.itemsize for a, _ in ins)
    for shape, dtype, _ in outs:
        moved += functools.reduce(lambda x, y: x * y, shape) * jnp.dtype(dtype).itemsize
    scalars = [] if place is None else [place]
    specs = [spec for _, spec in ins] + [spec for _, _, spec in outs]
    first = len(scalars)

    def body(*refs):
        i = pl.program_id(0)
        seen = list(refs)
        for k, spec in enumerate(specs):
            if isinstance(spec, Kept):
                seen[first + k] = spec.view(refs[first + k], i, refs[:first])
        kernel(*seen)

    places = [
        pl.BlockSpec(memory_space=pltpu.VMEM) if isinstance(spec, Kept) else spec for spec in specs
    ]
    return pl.pallas_call(
        body,
        grid_spec=pltpu.PrefetchScalarGridSpec(
            num_scalar_prefetch=len(scalars),
            grid=(steps,),
            in_specs=places[: len(ins)],
            out_specs=places[len(ins) :],
            scratch_shapes=scratch,
        ),
        out_shape=[jax.ShapeDtypeStruct(s, d) for s, d, _ in outs],
        compiler_params=pltpu.CompilerParams(
            dimension_semantics=("arbitrary",), vmem_limit_bytes=VMEM_LIMIT
        ),
        cost_estimate=pl.CostEstimate(flops=flops, bytes_accessed=moved, transcendentals=0),
        name=name,
    )(*scalars, *[a for a, _ in ins])


def swap(value, axis, mask):
    return lax.ppermute(value, axis, [(i, i ^ mask) for i in range(lax.axis_size(axis))])


def after(value, *others):
    return lax.optimization_barrier((value,) + others)[0]


def powers(count):
    return [1 << k for k in range(count.bit_length() - 1)]


def k_merge(mask, backward, first, place, *refs):
    total, other = refs[:2]
    before = None if first else refs[2]
    outs = refs[2 if first else 3 :]
    upper = (place[3] // mask) % 2 == 1
    later = jnp.logical_not(upper) if backward else upper

    def merge(early, late, out):
        scale = late[N : N + 1, :]
        out[0:N, :] = scale * early[0:N, :] + late[0:N, :]
        out[N:, :] = scale * early[N:, :]

    @pl.when(later)
    def _():
        if first:
            outs[0][...] = other[...]
        else:
            merge(other, before, outs[0])
        if len(outs) > 1:
            merge(other, total, outs[1])

    @pl.when(jnp.logical_not(later))
    def _():
        if first:
            outs[0][0:N, :] = jnp.zeros((N, total.shape[1]), F32)
            outs[0][N:, :] = jnp.ones((8, total.shape[1]), F32)
        else:
            outs[0][...] = before[...]
        if len(outs) > 1:
            merge(total, other, outs[1])


def carried_in(total, backward, place):
    before, firsts = [], []
    shape = total.shape
    masks = powers(lax.axis_size("tok"))
    for mask in masks:
        ins = [total, swap(total, "tok", mask)] + before
        last = mask == masks[-1]
        found = call(
            functools.partial(k_merge, mask, backward, not before),
            1,
            [(a, whole(shape)) for a in ins],
            [(shape, F32, whole(shape))] * (1 if last else 2),
            [],
            10**6,
            "merge",
            place,
        )
        before, total = [found[0]], found[-1]
        firsts.append(found[0])
    return before[0], firsts[0]


def exchange(pieces, axis):
    return lax.all_to_all(pieces, axis, 0, 0, tiled=True)


def distances(value, axis, step):
    return [value] + [swap(value, axis, step * k) for k in range(1, lax.axis_size(axis) // step)]


def head_gathered(value):
    found = [value]
    masks = powers(lax.axis_size("head"))
    for mask in masks[1:] + masks[:1]:
        found = found + [swap(a, "head", mask) for a in found]
    return found


def on_device(
    hidden_in, norm_gain, w_zx, w_bc, w_dt, dt_bias, a_log, conv_x, conv_bc, d_skip, gate_gain,
    w_out, out_grad, group_first, group_valid,
):
    tokens, dim = hidden_in.shape
    real = w_zx.shape[2]
    own_heads = real // P_SIZE
    heads = w_dt.shape[1]
    groups = tokens // GROUP
    chunks = groups * PARTS
    width = -(-real // LANES) * LANES
    extra = width - real
    conv_width = width + 2 * N
    tok_count = lax.axis_size("tok")
    head_count = lax.axis_size("head")
    head_start = lax.axis_index("head") * own_heads

    def wide(a, dim_at, by=extra):
        return jnp.pad(a, [(0, by if k == dim_at else 0) for k in range(a.ndim)]) if by else a

    route = [(i - 1, i) for i in range(1, tok_count)]
    rim = lax.ppermute(hidden_in[tokens - 16 :], "tok", route)
    w_z = wide(w_zx[:, 0], 1)
    w_x = wide(w_zx[:, 1], 1)
    w_o = wide(w_out, 0)
    w_dt_here = wide(lax.dynamic_slice_in_dim(w_dt, head_start, own_heads, 1), 1, LANES - own_heads)
    per_head = jnp.stack([dt_bias, a_log, d_skip])
    per_head = lax.dynamic_slice_in_dim(per_head, head_start, own_heads, 1)
    per_head = jnp.pad(per_head, ((0, 5), (0, LANES - own_heads)))
    cx = wide(conv_x, 1)
    gain_in = norm_gain[None, :]
    gain_gate = wide(gate_gain, 0)[None, :]
    at_head = lax.axis_index("head")
    place = jnp.stack([at_head & 1, head_start, at_head, lax.axis_index("tok")]).astype(jnp.int32)
    hidden_in, place, w_z, w_x, w_o, w_dt_here, per_head, cx, gain_in, gain_gate = lax.optimization_barrier(
        (hidden_in, place, w_z, w_x, w_o, w_dt_here, per_head, cx, gain_in, gain_gate)
    )
    w_outs = head_gathered(w_o)

    def rows(a, at=None):
        return (a, row_block(a.shape, GROUP, at))

    def full(a):
        return (a, whole(a.shape))

    def kept(a, at=None):
        return (a, Kept(GROUP, at))

    def per_chunk(a, at=None):
        return (a, Kept(PARTS, at))

    def out_rows(cols, dtype, at=None):
        return ((tokens, cols), dtype, row_block((tokens, cols), GROUP, at))

    def out_kept(cols, dtype, at=None):
        return ((tokens, cols), dtype, Kept(GROUP, at))

    def out_full(shape, dtype):
        return (shape, dtype, whole(shape))

    def out_chunk(shape, dtype, at=None):
        return ((chunks,) + shape, dtype, Kept(PARTS, at))

    carry = (N + 8, width)
    h, v, pre = call(
        k_project,
        groups,
        [rows(hidden_in), full(gain_in), full(w_x), full(w_bc), full(w_dt_here), full(per_head)],
        [out_kept(dim, BF16), out_kept(conv_width, F32), out_kept(LANES, F32)],
        [],
        4 * 10**9,
        "project",
    )
    cv, xs, bc, dt, cum, ent, pd, fin = call(
        k_conv,
        groups,
        [
            (group_first, SMEM), (group_valid, SMEM), kept(v), kept(pre), full(rim), full(gain_in),
            full(w_x), full(w_bc), full(per_head), full(cx), full(conv_bc),
        ],
        [
            out_kept(conv_width, F32), out_kept(width, BF16), out_kept(2 * N, BF16),
            out_kept(LANES, F32), out_kept(LANES, F32), out_chunk((N, width), F32),
            out_chunk((1, width), F32), out_full(carry, F32),
        ],
        [
            pltpu.VMEM((GROUP + 8, conv_width), F32), pltpu.VMEM((N, width), F32),
            pltpu.VMEM((8, width), F32),
        ],
        4 * 10**9,
        "conv",
    )
    prev, _ = carried_in(fin, False, place)
    z, gyn = call(
        k_proj,
        groups,
        [kept(h), rows(after(out_grad, fin)), full(w_z), full(w_o)],
        [out_kept(width, F32), out_kept(width, F32)],
        [],
        5 * 10**9,
        "proj",
    )
    (yw,) = call(
        k_within,
        groups,
        [kept(xs), kept(bc), kept(dt), kept(cum)],
        [out_kept(width, F32)],
        [],
        5 * 10**9,
        "within",
    )
    mix, entry, sums = call(
        k_gate,
        groups,
        [
            per_chunk(ent), per_chunk(pd), full(after(prev, *w_outs)), kept(bc), kept(cum), kept(yw), kept(xs),
            kept(z), kept(gyn), full(gain_gate), full(per_head),
        ],
        [
            out_kept(width, F32), out_chunk((N, width), F32),
            ((2, tokens), F32, pl.BlockSpec((2, GROUP), lambda i: (0, i))),
        ],
        [],
        3 * 10**9,
        "gate",
    )
    sums = [sums] + [swap(sums, "head", mask) for mask in range(1, head_count)]

    def back(i):
        return groups - 1 - i

    yn, gm, gz, ds, qd, acc_gain, acc_skip, fin_back = call(
        functools.partial(k_gate_back, float(heads * P_SIZE), head_count),
        groups,
        [
            (group_first, SMEM), kept(mix, back), kept(z, back), kept(gyn, back), full(gain_gate), kept(xs, back),
            kept(bc, back), kept(cum, back),
        ]
        + [(a, pl.BlockSpec((2, GROUP), lambda i: (0, groups - 1 - i))) for a in sums],
        [
            out_kept(width, BF16, back), out_kept(width, BF16, back), out_kept(width, BF16, back),
            out_chunk((N, width), F32, back), out_chunk((1, width), F32, back),
            out_full((8, width), F32), out_full((8, width), F32), out_full(carry, F32),
        ],
        [pltpu.VMEM((N, width), F32), pltpu.VMEM((8, width), F32)],
        3 * 10**9,
        "gate_back",
    )
    end_grad, first_grad = carried_in(fin_back, True, place)
    yns = head_gathered(yn)
    rows_z, rows_o = dim // tok_count, width // tok_count
    piece_a = (rows_z * width + rows_o * dim) // LANES
    sides = tok_count // 2
    keep_a, send_a = call(
        k_weights,
        groups,
        [kept(yn), rows(out_grad), kept(h), kept(gz)],
        [out_full((sides, piece_a, LANES), F32)] * 2,
        [pltpu.VMEM((dim, width), F32), pltpu.VMEM((width, dim), F32)],
        3 * 10**9,
        "weights",
        place,
    )
    arrived_a = swap(after(send_a, first_grad), "tok", 1)
    per_token = [
        out_kept(width, F32), out_kept(2 * N, F32), out_kept(LANES, F32), out_kept(LANES, F32)
    ]
    inner = [kept(xs), kept(bc), kept(after(gm, keep_a)), kept(dt), kept(cum), kept(mix), per_chunk(entry), full(per_head)]
    dxw, dbc, rq, qw = call(
        k_within_back, groups, inner, per_token, [], 10 * 10**9, "within_back"
    )

    def leading(a):
        per = GROUP // 16
        return (a, Kept(16, lambda i: i * per))

    rims, lead = call(
        k_rim,
        groups,
        [
            (group_first, SMEM), leading(xs), leading(bc), leading(gm), leading(dt), leading(cum),
            (cum, Kept(8, lambda i: i * (GROUP // 8) + CHUNK // 8 - 1)),
            leading(dxw), leading(dbc), leading(cv),
            (ds, Kept(1, lambda i: i * PARTS)),
            (qd, Kept(1, lambda i: i * PARTS)),
            full(end_grad), full(per_head),
        ],
        [((groups, 16, conv_width), F32, Kept(1)), out_full((8, conv_width), F32)],
        [],
        10**9,
        "rim",
    )
    rim_in = lax.ppermute(lead, "tok", [(i, i - 1) for i in range(1, tok_count)])
    at_head = lax.axis_index("head")
    place = jnp.stack([at_head & 1, head_start, at_head, lax.axis_index("tok")]).astype(jnp.int32)
    pairs_a = call(
        k_pair,
        1,
        [full(after(keep_a, end_grad)), full(arrived_a)],
        [out_full((piece_a, LANES), BF16)] * sides,
        [],
        10**6,
        "pair",
        place,
    )
    arrived_a = [pairs_a[0]] + [swap(pairs_a[k], "tok", 2 * k) for k in range(1, sides)]
    half = groups // 2
    piece_b = rows_z * width // LANES
    tiles = width // LANES
    small_rows = 2 * dim + heads * dim // LANES + 16 + head_count * 8 * tiles
    unit = head_count * tok_count * 8
    small_rows = -(-small_rows // unit) * unit
    gx, gbc, gpre, grads_b, small_keep, small_send = call(
        k_back,
        groups,
        [
            (group_valid, SMEM),
            kept(h), kept(xs), kept(bc), kept(gm), kept(pre), kept(dt), kept(cum), kept(v), kept(cv),
            kept(dxw), kept(dbc), kept(rq), kept(qw), per_chunk(entry), per_chunk(ds), per_chunk(qd),
            full(end_grad),
            (rims, row_block(rims.shape, 1, lambda i, s: jnp.minimum(i + 1, groups - 1))),
            full(after(rim_in, pairs_a[0], yns[1])), full(cx), full(conv_bc), full(per_head), full(acc_gain), full(acc_skip),
        ],
        [
            out_kept(width, BF16), out_kept(4 * N, BF16), out_kept(LANES, BF16),
            out_full((tok_count, piece_b, LANES), BF16), out_full((small_rows // 2, LANES), F32),
            out_full((small_rows // 2, LANES), F32),
        ],
        [
            pltpu.VMEM((GROUP + 8, conv_width), F32), pltpu.VMEM((small_rows, LANES), F32),
            pltpu.VMEM((dim, width), F32), pltpu.VMEM((dim, 2 * N), F32), pltpu.VMEM((heads, dim), F32),
            pltpu.VMEM((8 * KCONV + 8, conv_width), F32), pltpu.VMEM((16, LANES), F32),
        ],
        10 * 10**9,
        "back",
        place,
    )

    (total_a,) = call(
        k_reduce, 1, [full(a) for a in arrived_a], [out_full((piece_a, LANES), BF16)], [], 10**6, "reduce"
    )

    small_arrived = swap(small_send, "head", 1)
    for mask in powers(head_count)[1:]:
        shape = (small_keep.shape[0] // 2, LANES)
        small_keep, small_send = call(
            functools.partial(k_halve, mask), 1, [full(small_keep), full(small_arrived)],
            [out_full(shape, F32)] * 2, [], 10**6, "halve", place,
        )
        small_arrived = swap(small_send, "head", mask)
    shape = (tokens // 2, dim)

    def input_ins(own):
        def turned(i, s):
            return i + half * (s[0] if own else 1 - s[0])

        return [rows(hidden_in, turned)] + [
            kept(a, turned) for a in (gz, gx, gbc, after(gpre, total_a))
        ] + [
            full(a) for a in (w_z, w_x, w_bc, w_dt_here)
        ]

    sent, norm = call(
        k_input_sent, half, input_ins(False),
        [(shape, F32, row_block(shape, GROUP)), out_full((8, dim), F32)], [], 3 * 10**9,
        "input_sent", place,
    )
    arrived = after(swap(sent, "head", 1), small_keep)
    part, norm = call(
        k_input_own, half, input_ins(True) + [rows(arrived), full(norm)],
        [(shape, BF16, row_block(shape, GROUP)), out_full((8, LANES), F32)],
        [pltpu.VMEM((8, dim), F32)], 3 * 10**9, "input_own", place,
    )
    parts = [after(part, small_arrived)]
    for mask in powers(head_count)[1:]:
        parts = parts + [swap(a, "head", mask) for a in parts]
    others = [swap(a, "head", 1) for a in parts]

    (block_out,) = call(
        k_out,
        groups,
        [rows(hidden_in)] + [rows(a) for a in yns] + [full(a) for a in w_outs],
        [out_rows(dim, BF16)],
        [],
        5 * 10**9,
        "out",
    )
    arrived_b = exchange(grads_b, "tok")
    joined = total_a[None]
    shape = joined.shape
    joins = []
    for mask in powers(sides):
        shape = (2 * shape[0],) + shape[1:]
        (joined,) = call(
            functools.partial(k_join, 2 * mask), 1, [full(joined), full(swap(joined, "tok", 2 * mask))],
            [out_full(shape, BF16)], [], 10**6, "join", place,
        )
        joins.append(joined)
    mine_a = joined
    other_a = swap(mine_a, "tok", 1)
    shape = (tok_count, small_keep.shape[0] // tok_count + 8, LANES)
    (pieces,) = call(
        k_pieces, 1, [full(small_keep), full(small_arrived), full(norm)], [out_full(shape, F32)], [],
        10**6, "pieces",
    )
    pieces = exchange(pieces, "tok")
    shape = (tok_count, piece_b + 2 * pieces.shape[1], LANES)
    (copies,) = call(
        k_reduce_both, 1, [full(after(arrived_b, mine_a)), full(pieces)], [out_full(shape, BF16)], [], 10**6,
        "reduce_both",
    )
    sum_b = exchange(copies, "tok")
    shape = (small_rows // head_count + tok_count, LANES)
    (quarter,) = call(
        functools.partial(k_quarter, piece_b), 1, [full(after(sum_b, block_out))], [out_full(shape, F32)],
        [], 10**6, "quarter",
    )
    quarters = [(quarter, 0)]
    for mask in powers(head_count):
        quarters = quarters + [(swap(a, "head", mask), k | mask) for a, k in quarters]
    quarters = [a for a, _ in sorted(quarters, key=lambda item: item[1])]

    grad_w_zx, grad_w_out = call(
        k_unpack,
        1,
        [full(mine_a), full(other_a), full(sum_b)],
        [out_full((dim, 2, real), F32), out_full((width, dim), F32)],
        [],
        10**6,
        "unpack",
        place,
    )
    grad_w_bc, grad_w_dt, grad_taps, grad_bias, grad_alog, grad_skip, grad_norm, own = call(
        k_small,
        1,
        [full(a) for a in quarters],
        [
            out_full((dim, 2 * N), F32), out_full((heads, dim), F32), out_full((KCONV + 1, 2 * N), F32),
            out_full((1, heads), F32), out_full((1, heads), F32), out_full((1, heads), F32),
            out_full((1, dim), F32), out_full((8, real), F32),
        ],
        [pltpu.VMEM((small_rows, LANES), F32)],
        10**6,
        "small",
        place,
    )

    def turned_back(i, s):
        return lax.rem(i + half * s[0], groups)

    def first_half(a):
        return (a, row_block(a.shape, GROUP, lambda i, s: jnp.minimum(i, half - 1)))

    def second_half(a):
        return (a, row_block(a.shape, GROUP, lambda i, s: jnp.maximum(i - half, 0)))

    (grad_in,) = call(
        k_in_back,
        groups,
        [rows(hidden_in, turned_back), rows(out_grad, turned_back), full(gain_in)]
        + [first_half(a) for a in parts]
        + [second_half(a) for a in others],
        [out_rows(dim, F32, turned_back)],
        [],
        10**9,
        "in_back",
        place,
    )
    return (
        block_out,
        grad_in,
        grad_norm[0],
        grad_w_zx,
        grad_w_bc,
        grad_w_dt.T,
        grad_bias[0],
        grad_alog[0],
        own[: KCONV + 1],
        grad_taps,
        grad_skip[0],
        own[KCONV + 1],
        grad_w_out[:real],
    )


def solution(mesh):
    return jax.shard_map(
        on_device,
        mesh=mesh,
        in_specs=(
            P("tok", None), P(), P(None, None, "head"), P(), P(), P(), P(), P(None, "head"), P(), P(),
            P("head"), P("head", None), P("tok", None), P("tok"), P("tok"),
        ),
        out_specs=(
            P("tok", None), P("tok", None), P(), P(None, None, "head"), P(), P(), P(), P(),
            P(None, "head"), P(), P(), P("head"), P("head", None),
        ),
        check_vma=False,
    )
```

time: 973 us -> 303 us (0.31)
  waiting for transfers between devices: 394 us -> 70.1 us
  other arithmetic: 176 us -> 0.7 us
  Pallas kernels: 0 us -> 142 us
  matrix products: 134 us -> 0 us
  blocking collectives: 129 us -> 0 us
  local copies, waits for them, and re-layouts: 96.4 us -> 35.5 us
  starting transfers between devices: 6.96 us -> 51.6 us
  between operations: 16.4 us -> 1.28 us
  loops' own time: 12 us -> 0 us
    psum x3 -> x0, waiting for transfers between devices: 383 us -> none  [the longest x1 253 us: on_device(): block_out = (upcast + lax.psum(partial_value, 'head')).astype(jnp.bfloat16)]
    pallas_call x0 -> x30, Pallas kernels: none -> 142 us  [call(): pl.pallas_call(body, grid_spec=pltpu.PrefetchScalarGridSpec(num_scalar_pr...]
    dot_general x24 -> x0, matrix products: 134 us -> none  [the longest x3 45.7 us: group_inner(): within = jnp.einsum('khls,kshp->klhp', weights, x_scaled, precision=PRECISE)]
    psum x4 -> x0, blocking collectives: 88.6 us -> none  [the longest x1 39.5 us: on_device(): lax.psum((grad_norm_gain, grad_w_bc, grad_w_dt, place_heads(grad_bias_her...]
    ppermute x2 -> x33, waiting for transfers between devices: 0.01 us -> 66 us  [the longest x31 62.6 us: swap(): lax.ppermute(value, axis, [(i, i ^ mask) for i in range(lax.axis_size(axi...]
    unnamed x2 -> x0, blocking collectives: 40 us -> none
    add x27 -> x0, other arithmetic: 37.5 us -> none  [the longest x1 11.4 us: on_device(): inv_rms * norm_gain * grad_hidden - upcast * inv_rms ** 3 * row_dot / D]
    reduce_sum x15 -> x0, other arithmetic: 35.1 us -> none  [the longest x1 10.8 us: conv_silu(): conv_taps[tap_index] * extended[tap_index:tap_index + row_count]]
  transfers between devices with their start and end apart: 7 -> 36, of which waited for: 4 -> 14; matrix products, arithmetic and copies ran while one was open for 14% -> 4% of each run, Pallas kernels for 0% -> 28%
where the time goes in v1:
time: 303 us; the launch traced here: 301 us
  Pallas kernels  142 us (47%)
  waiting for transfers between devices  70.1 us (23%)
  starting transfers between devices  51.6 us (17%)
  local copies, waits for them, and re-layouts  35.5 us (12%)
    pallas_call x30, Pallas kernels, call(): pl.pallas_call(body, grid_spec=pltpu.PrefetchScalarGridSpec(num_scalar_pr...  142 us
    ppermute x31, waiting for transfers between devices, swap(): lax.ppermute(value, axis, [(i, i ^ mask) for i in range(lax.axis_size(axi...  62.6 us
    ppermute x31, starting transfers between devices, swap(): lax.ppermute(value, axis, [(i, i ^ mask) for i in range(lax.axis_size(axi...  31.7 us
    unnamed x95, local copies, waits for them, and re-layouts  25.1 us
    all_to_all x3, starting transfers between devices, exchange(): return lax.all_to_all(pieces, axis, 0, 0, tiled=True)  13.5 us
  transfers between devices with their start and end apart: 36, of which 14 were waited for; matrix products, arithmetic and copies ran while one was open for 4% of the time, Pallas kernels for 28%

profile of v1, /device:TPU:0, one launch (start us, length us, event | category | flops | bytes accessed | tf_op | source)
XLA Modules:
  0.0 301.3 jit_solution(8986269056301430591)
XLA Ops:
  1.4 4.9 %collective-permute-start = (bf16[16,768]{1,0:T(8,128)(2,1)S(1)}, bf16[16,768]{1,0:T(8,128)(2,1)S(1)}, u32[]{:S(2)}, u32[]{:S(2)}) collective-permute-start(bf16[16,768]{1,0:T(8,128)(2,1)S(1)} %slice.17), channel_id=1, source_target_pairs={{0,4},{4,8},{8,12},{12,16},{16,20},{20,24},{24,28},{1,5},{5,9},{9,... | collective-permute-start | bytes 73736 | tf_op jit(solution)/shard_map/ppermute | solution.py:835
  6.3 5.1 %fusion = (bf16[768,1,384]{2,1,0:T(2,128)(2,1)}, bf16[768,1,384]{2,1,0:T(2,128)(2,1)}) fusion(bf16[768,2,384]{2,1,0:T(2,128)(2,1)} %param.17), kind=kLoop, calls=%fused_computation.7 | loop fusion | bytes 2359296 | tf_op jit(solution)/shard_map/slice | solution.py:837
  17.3 5.4 %project.1 = (bf16[2048,768]{1,0:T(8,128)(2,1)S(1)}, f32[2048,640]{1,0:T(8,128)S(1)}, f32[2048,128]{1,0:T(8,128)S(1)}) custom-call(bf16[2048,768]{1,0:T(8,128)(2,1)S(1)} %copy-done.2, f32[1,768]{1,0:T(1,128)S(1)} %broadcast_in_dim.9.refs_1_.refs_5_.refs_3_, bf16[768,384]{1,0:T(8,128)(2,1)S(1)} %get-tuple-element.102.refs_2_.refs_6_.refs_7_, ...), custom_call_target="tpu_custom_call" | custom-call | flops 4000000000 | bytes 13769728 | tf_op jit(solution)/shard_map/project/pallas_call | solution.py:714
  22.8 12.8 %conv.1 = (f32[2048,640]{1,0:T(8,128)S(1)}, bf16[2048,384]{1,0:T(8,128)(2,1)S(1)}, bf16[2048,256]{1,0:T(8,128)(2,1)S(1)}, f32[2048,128]{1,0:T(8,128)S(1)}, f32[2...) custom-call(s32[8]{0:T(128)S(1)} %copy-done.28, ...), custom_call_target="tpu_custom_call" | custom-call | flops 4000000000 | bytes 20659776 | tf_op jit(solution)/shard_map/conv/pallas_call | solution.py:714
  37.2 4.8 %collective-permute-done.1.refs_2_ = f32[136,384]{1,0:T(8,128)S(1)} collective-permute-done((f32[136,384]{1,0:T(8,128)S(1)}, f32[136,384]{1,0:T(8,128)S(1)}, u32[]{:S(2)}, u32[]{:S(2)}) %collective-permute-start.1) | collective-permute-done | bytes 208928 | tf_op jit(solution)/shard_map/ppermute | solution.py:733
  44.3 4.5 %proj.1 = (f32[2048,384]{1,0:T(8,128)S(1)}, f32[2048,384]{1,0:T(8,128)S(1)}) custom-call(bf16[2048,768]{1,0:T(8,128)(2,1)S(1)} %get-tuple-element.122.refs_0_.refs_3_.refs_2_, bf16[2048,768]{1,0:T(8,128)(2,1)S(1)} %copy-done.5, bf16[768,384]{1,0:T(8,128)(2,1)S(1)} %get-tuple-element.124.refs_2_.refs_6_, bf16[384,768]{1,0:T(8,128)(2,1)S(1)} %copy-done.29), custom_call_target="tpu_custom_call" | custom-call | flops 5000000000 | bytes 13762560 | tf_op jit(solution)/shard_map/proj/pallas_call | solution.py:714
  49.4 2.7 collective-permute-start.3
  52.1 5.5 %within.1.refs_5_ = f32[2048,384]{1,0:T(8,128)S(1)} custom-call(bf16[2048,384]{1,0:T(8,128)(2,1)S(1)} %get-tuple-element.120.refs_0_.refs_6_.refs_5_.refs_1_.refs_3_, bf16[2048,256]{1,0:T(8,128)(2,1)S(1)} %get-tuple-element.118.refs_1_.refs_3_.refs_6_.refs_2_.refs_4_, f32[2048,128]{1,0:T(8,128)S(1)} %get-tuple-element.121.refs_2_.refs_3_.refs_4_.refs_7_, ...), custom_call_target="tpu_custom_call" | custom-call | flops 5000000000 | bytes 7864320 | tf_op jit(solution)/shard_map/within/pallas_call | solution.py:714
  57.5 4.7 %collective-permute-done.3.refs_2_ = f32[136,384]{1,0:T(8,128)S(1)} collective-permute-done((f32[136,384]{1,0:T(8,128)S(1)}, f32[136,384]{1,0:T(8,128)S(1)}, u32[]{:S(2)}, u32[]{:S(2)}) %collective-permute-start.3) | collective-permute-done | bytes 208928 | tf_op jit(solution)/shard_map/ppermute | solution.py:733
  64.5 4.4 %gate.1 = (f32[2048,384]{1,0:T(8,128)S(1)}, f32[16,128,384]{2,1,0:T(8,128)S(1)}, f32[2,2048]{1,0:T(2,128)S(1)}) custom-call(f32[16,128,384]{2,1,0:T(8,128)S(1)} %get-tuple-element.108.refs_0_, f32[16,1,384]{2,1,0:T(1,128)S(1)} %get-tuple-element.109.refs_1_, f32[136,384]{1,0:T(8,128)S(1)} %merge.8.refs_2_, ...), custom_call_target="tpu_custom_call" | custom-call | flops 3000000000 | bytes 22799872 | tf_op jit(solution)/shard_map/gate/pallas_call | solution.py:714
  72.9 9.3 %gate_back.1 = (bf16[2048,384]{1,0:T(8,128)(2,1)}, bf16[2048,384]{1,0:T(8,128)(2,1)S(1)}, bf16[2048,384]{1,0:T(8,128)(2,1)S(1)}, f32[16,128,384]{2,1,0:T(8,128)S...) custom-call(s32[8]{0:T(128)S(1)} %copy-done.28, ...), custom_call_target="tpu_custom_call" | custom-call | flops 3000000000 | bytes 21296672 | tf_op jit(solution)/shard_map/gate_back/pallas_call | solution.py:714
  83.7 7.1 %weights.1 = (f32[4,576,128]{2,1,0:T(8,128)S(1)}, f32[4,576,128]{2,1,0:T(8,128)S(1)}) custom-call(s32[4]{0:T(128)S(1)} %pad_add_fusion.refs_0_, bf16[2048,384]{1,0:T(8,128)(2,1)} %get-tuple-element.130.refs_1_, bf16[2048,768]{1,0:T(8,128)(2,1)S(1)} %copy-done.5, bf16[2048,768]{1,0:T(8,128)(2,1)S(1)} %get-tuple-element.122.refs_0_.refs_3_.refs_2_, ...), custom_call_target="tpu_custom_call" | custom-call | flops 3000000000 | bytes 11796480 | tf_op jit(solution)/shard_map/weights/pallas_call | solution.py:714
  93.2 6.4 %collective-permute-done.14.refs_2_ = f32[136,384]{1,0:T(8,128)S(1)} collective-permute-done((f32[136,384]{1,0:T(8,128)S(1)}, f32[136,384]{1,0:T(8,128)S(1)}, u32[]{:S(2)}, u32[]{:S(2)}) %collective-permute-start.14) | collective-permute-done | bytes 208928 | tf_op jit(solution)/shard_map/ppermute | solution.py:733
  101.7 9.5 %collective-permute-done.15.refs_2_ = f32[136,384]{1,0:T(8,128)S(1)} collective-permute-done((f32[136,384]{1,0:T(8,128)S(1)}, f32[136,384]{1,0:T(8,128)S(1)}, u32[]{:S(2)}, u32[]{:S(2)}) %collective-permute-start.15) | collective-permute-done | bytes 208928 | tf_op jit(solution)/shard_map/ppermute | solution.py:733
  111.8 7.3 %collective-permute-done.17.refs_2_ = f32[4,576,128]{2,1,0:T(8,128)S(1)} collective-permute-done((f32[4,576,128]{2,1,0:T(8,128)S(1)}, f32[4,576,128]{2,1,0:T(8,128)S(1)}, u32[]{:S(2)}, u32[]{:S(2)}) %collective-permute-start.17) | collective-permute-done | bytes 1179680 | tf_op jit(solution)/shard_map/ppermute | solution.py:733
  119.9 2.9 collective-permute-start.19
  124.2 12.9 %within_back.1 = (f32[2048,384]{1,0:T(8,128)S(1)}, f32[2048,256]{1,0:T(8,128)S(1)}, f32[2048,128]{1,0:T(8,128)S(1)}, f32[2048,128]{1,0:T(8,128)S(1)}) custom-call(bf16[2048,384]{1,0:T(8,128)(2,1)S(1)} %get-tuple-element.120.refs_0_.refs_6_.refs_5_.refs_1_.refs_3_, bf16[2048,256]{1,0:T(8,128)(2,1)S(1)} %get-tuple-element.118.refs_1_.refs_3_.refs_6_.refs_2_.refs_4_, ...), custom_call_target="tpu_custom_call" | custom-call | flops 10000000000 | bytes 19927040 | tf_op jit(solution)/shard_map/within_back/pallas_call | solution.py:714
  137.2 3.0 rim.1
  142.5 3.4 %collective-permute-done.16.refs_20_ = f32[8,640]{1,0:T(8,128)S(1)} collective-permute-done((f32[8,640]{1,0:T(8,128)S(1)}, f32[8,640]{1,0:T(8,128)S(1)}, u32[]{:S(2)}, u32[]{:S(2)}) %collective-permute-start.16) | collective-permute-done | bytes 20512 | tf_op jit(solution)/shard_map/ppermute | solution.py:1006
  148.4 29.5 %back.1 = (bf16[2048,384]{1,0:T(8,128)(2,1)S(1)}, bf16[2048,512]{1,0:T(8,128)(2,1)S(1)}, bf16[2048,128]{1,0:T(8,128)(2,1)S(1)}, bf16[8,288,128]{2,1,0:T(8,128)(2...) custom-call(s32[4]{0:T(128)S(1)} %pad_add_fusion.refs_0_, s32[8]{0:T(128)S(1)} %copy-done.39, ...), custom_call_target="tpu_custom_call" | custom-call | flops 10000000000 | bytes 40927776 | tf_op jit(solution)/shard_map/back/pallas_call | solution.py:714
  177.9 5.2 %input_sent.1 = (f32[1024,768]{1,0:T(8,128)}, f32[8,768]{1,0:T(8,128)S(1)}) custom-call(s32[4]{0:T(128)S(1)} %pad_add_fusion.refs_0_, bf16[2048,768]{1,0:T(8,128)(2,1)S(1)} %copy-done.2, bf16[2048,384]{1,0:T(8,128)(2,1)S(1)} %get-tuple-element.131.refs_4_.refs_2_, bf16[2048,384]{1,0:T(8,128)(2,1)S(1)} %get-tuple-element.157.refs_3_, ...), custom_call_target="tpu_custom_call" | custom-call | flops 3000000000 | bytes 13852672 | tf_op jit(solution)/shard_map/input_sent/pallas_call | solution.py:714
  183.7 4.2 %all-to-all-start = ((bf16[8,288,128]{2,1,0:T(8,128)(2,1)}), bf16[8,288,128]{2,1,0:T(8,128)(2,1)}, u32[]{:S(2)}, u32[]{:S(2)}) async-start(bf16[8,288,128]{2,1,0:T(8,128)(2,1)} %copy-done.19), calls=%async_computation | async-start | bytes 1179648 | tf_op jit(solution)/shard_map/all_to_all | solution.py:799
  202.5 6.6 %input_own.1 = (bf16[1024,768]{1,0:T(8,128)(2,1)}, f32[8,128]{1,0:T(8,128)S(1)}) custom-call(s32[4]{0:T(128)S(1)} %pad_add_fusion.refs_0_, bf16[2048,768]{1,0:T(8,128)(2,1)S(1)} %copy-done.2, bf16[2048,384]{1,0:T(8,128)(2,1)S(1)} %copy-done.16, bf16[2048,384]{1,0:T(8,128)(2,1)S(1)} %copy-done.18, bf16[2048,512]{1,0:T(8,128)(2,1)S(1)} %copy-done.14, ...), custom_call_target="tpu_custom_call" | custom-call | flops 3000000000 | bytes 15429632 | tf_op jit(solution)/shard_map/input_own/pallas_call | solution.py:714
  211.0 4.0 %all-to-all-start.1 = ((f32[8,64,128]{2,1,0:T(8,128)}), f32[8,64,128]{2,1,0:T(8,128)S(1)}, u32[]{:S(2)}, u32[]{:S(2)}) async-start(f32[8,64,128]{2,1,0:T(8,128)} %pieces.1), calls=%async_computation.1 | async-start | bytes 524288 | tf_op jit(solution)/shard_map/all_to_all | solution.py:799
  217.0 7.9 %collective-permute-done.27.refs_2_ = bf16[1,576,128]{2,1,0:T(8,128)(2,1)S(1)} collective-permute-done((bf16[1,576,128]{2,1,0:T(8,128)(2,1)}, bf16[1,576,128]{2,1,0:T(8,128)(2,1)S(1)}, u32[]{:S(2)}, u32[]{:S(2)}) %collective-permute-start.27) | collective-permute-done | bytes 147488 | tf_op jit(solution)/shard_map/ppermute | solution.py:733
  228.8 12.7 %collective-permute-done.28.refs_2_ = bf16[2,576,128]{2,1,0:T(8,128)(2,1)S(1)} collective-permute-done((bf16[2,576,128]{2,1,0:T(8,128)(2,1)S(1)}, bf16[2,576,128]{2,1,0:T(8,128)(2,1)S(1)}, u32[]{:S(2)}, u32[]{:S(2)}) %collective-permute-start.28) | collective-permute-done | bytes 294944 | tf_op jit(solution)/shard_map/ppermute | solution.py:733
  245.0 5.3 %all-to-all-start.2 = ((bf16[8,416,128]{2,1,0:T(8,128)(2,1)}), bf16[8,416,128]{2,1,0:T(8,128)(2,1)}, u32[]{:S(2)}, u32[]{:S(2)}) async-start(bf16[8,416,128]{2,1,0:T(8,128)(2,1)} %copy-done.4), calls=%async_computation.2 | async-start | bytes 1703936 | tf_op jit(solution)/shard_map/all_to_all | solution.py:799
  257.1 11.0 %out.1 = bf16[2048,768]{1,0:T(8,128)(2,1)} custom-call(bf16[2048,768]{1,0:T(8,128)(2,1)S(1)} %copy-done.2, bf16[2048,384]{1,0:T(8,128)(2,1)} %get-tuple-element.130.refs_1_, bf16[2048,384]{1,0:T(8,128)(2,1)} %collective-permute-done.10.refs_2_, bf16[2048,384]{1,0:T(8,128)(2,1)} %collective-permute-done.11.refs_3_, ...), custom_call_target="tpu_custom_call" | custom-call | flops 5000000000 | bytes 14942208 | tf_op jit(solution)/shard_map/out/pallas_call | solution.py:714
  268.1 4.0 %all-to-all-done.2.refs_0_.refs_3_ = bf16[8,416,128]{2,1,0:T(8,128)(2,1)} async-done(((bf16[8,416,128]{2,1,0:T(8,128)(2,1)}), bf16[8,416,128]{2,1,0:T(8,128)(2,1)}, u32[]{:S(2)}, u32[]{:S(2)}) %all-to-all-start.2) | async-done | bytes 852000 | tf_op jit(solution)/shard_map/all_to_all | solution.py:799
  277.3 4.0 %unpack.1 = (f32[768,2,384]{2,1,0:T(2,128)}, f32[384,768]{1,0:T(8,128)}) custom-call(s32[4]{0:T(128)S(1)} %pad_add_fusion.refs_0_, bf16[4,576,128]{2,1,0:T(8,128)(2,1)S(1)} %copy-done.12, bf16[4,576,128]{2,1,0:T(8,128)(2,1)} %collective-permute-done.32.refs_2_, bf16[8,416,128]{2,1,0:T(8,128)(2,1)} %all-to-all-done.2.refs_0_.refs_3_), custom_call_target="tpu_custom_call" | custom-call | flops 1000000 | bytes 5570560 | tf_op jit(solution)/shard_map/unpack/pallas_call | solution.py:714
  282.0 4.6 %collective-permute-done.31.refs_4_ = f32[456,128]{1,0:T(8,128)S(1)} collective-permute-done((f32[456,128]{1,0:T(8,128)S(1)}, f32[456,128]{1,0:T(8,128)S(1)}, u32[]{:S(2)}, u32[]{:S(2)}) %collective-permute-start.31) | collective-permute-done | bytes 233504 | tf_op jit(solution)/shard_map/ppermute | solution.py:733
  291.9 9.4 %in_back.1 = f32[2048,768]{1,0:T(8,128)} custom-call(s32[4]{0:T(128)S(1)} %pad_add_fusion.refs_0_, bf16[2048,768]{1,0:T(8,128)(2,1)S(1)} %copy-done.2, bf16[2048,768]{1,0:T(8,128)(2,1)S(1)} %copy-done.6, f32[1,768]{1,0:T(1,128)S(1)} %broadcast_in_dim.9.refs_1_.refs_5_.refs_3_, bf16[1024,768]{1,0:T(8,128)(2,1)} %get-tuple-element.172.refs_4_, ...), custom_call_target="tpu_custom_call" | custom-call | flops 1000000000 | bytes 18877440 | tf_op jit(solution)/shard_map/in_back/pallas_call | solution.py:714
  (178 shorter events, 75.2 us)
Async XLA Ops:
  1.4 21.3 %collective-permute-start = (bf16[16,768]{1,0:T(8,128)(2,1)S(1)}, bf16[16,768]{1,0:T(8,128)(2,1)S(1)}, u32[]{:S(2)}, u32[]{:S(2)}) collective-permute-start(bf16[16,768]{1,0:T(8,128)(2,1)S(1)} %slice.17), channel_id=1, source_target_pairs={{0,4},{4,8},{8,12},{12,16},{16,20},{20,24},{24,28},{1,5},{5,9},{9,... | collective-permute-start | bytes 73736 | tf_op jit(solution)/shard_map/ppermute | solution.py:835
  15.7 28.5 %collective-permute-start.4 = (bf16[384,768]{1,0:T(8,128)(2,1)}, bf16[384,768]{1,0:T(8,128)(2,1)S(1)}, u32[]{:S(2)}, u32[]{:S(2)}) collective-permute-start(bf16[384,768]{1,0:T(8,128)(2,1)} %refs_5_), channel_id=1, source_target_pairs={{0,2},{1,3},{2,0},{3,1},{4,6},{5,7},{6,4},{7,5},{8,10},{9,11},{10,... | collective-permute-start | bytes 1769480 | tf_op jit(solution)/shard_map/ppermute | solution.py:733
  35.6 6.4 %collective-permute-start.1 = (f32[136,384]{1,0:T(8,128)S(1)}, f32[136,384]{1,0:T(8,128)S(1)}, u32[]{:S(2)}, u32[]{:S(2)}) collective-permute-start(f32[136,384]{1,0:T(8,128)S(1)} %get-tuple-element.111.refs_1_), channel_id=1, source_target_pairs={{0,4},{4,0},{8,12},{12,8},{16,20},{20,16},{24,28},{28,24},{1,5},{5... | collective-permute-start | bytes 626696 | tf_op jit(solution)/shard_map/ppermute | solution.py:733
  37.2 25.7 %collective-permute-start.5 = (bf16[384,768]{1,0:T(8,128)(2,1)S(1)}, bf16[384,768]{1,0:T(8,128)(2,1)S(1)}, u32[]{:S(2)}, u32[]{:S(2)}) collective-permute-start(bf16[384,768]{1,0:T(8,128)(2,1)S(1)} %copy-done.29), channel_id=1, source_target_pairs={{0,1},{1,0},{2,3},{3,2},{4,5},{5,4},{6,7},{7,6},{8,9},{9,8},{10,11... | collective-permute-start | bytes 1769480 | tf_op jit(solution)/shard_map/ppermute | solution.py:733
  42.6 6.2 %collective-permute-start.2 = (f32[136,384]{1,0:T(8,128)S(1)}, f32[136,384]{1,0:T(8,128)S(1)}, u32[]{:S(2)}, u32[]{:S(2)}) collective-permute-start(f32[136,384]{1,0:T(8,128)S(1)} %get-tuple-element.112.refs_1_), channel_id=1, source_target_pairs={{0,8},{4,12},{8,0},{12,4},{16,24},{20,28},{24,16},{28,20},{1,9},{5... | collective-permute-start | bytes 626696 | tf_op jit(solution)/shard_map/ppermute | solution.py:733
  44.2 19.5 %collective-permute-start.6 = (bf16[384,768]{1,0:T(8,128)(2,1)S(1)}, bf16[384,768]{1,0:T(8,128)(2,1)S(1)}, u32[]{:S(2)}, u32[]{:S(2)}) collective-permute-start(bf16[384,768]{1,0:T(8,128)(2,1)S(1)} %collective-permute-done.4.refs_6_), channel_id=1, source_target_pairs={{0,1},{1,0},{2,3},{3,2},{4,5},{5,4},{6,7},{7,6},{8,9},{9,8},{10,11... | collective-permute-start | bytes 1769480 | tf_op jit(solution)/shard_map/ppermute | solution.py:733
  49.4 12.9 %collective-permute-start.3 = (f32[136,384]{1,0:T(8,128)S(1)}, f32[136,384]{1,0:T(8,128)S(1)}, u32[]{:S(2)}, u32[]{:S(2)}) collective-permute-start(f32[136,384]{1,0:T(8,128)S(1)} %get-tuple-element.114.refs_1_), channel_id=1, source_target_pairs={{0,16},{4,20},{8,24},{12,28},{16,0},{20,4},{24,8},{28,12},{1,17},{... | collective-permute-start | bytes 626696 | tf_op jit(solution)/shard_map/ppermute | solution.py:733
  82.2 8.6 %collective-permute-start.13 = (f32[136,384]{1,0:T(8,128)S(1)}, f32[136,384]{1,0:T(8,128)S(1)}, u32[]{:S(2)}, u32[]{:S(2)}) collective-permute-start(f32[136,384]{1,0:T(8,128)S(1)} %get-tuple-element.143.refs_1_), channel_id=1, source_target_pairs={{0,4},{4,0},{8,12},{12,8},{16,20},{20,16},{24,28},{28,24},{1,5},{5... | collective-permute-start | bytes 626696 | tf_op jit(solution)/shard_map/ppermute | solution.py:733
  91.4 27.7 %collective-permute-start.17 = (f32[4,576,128]{2,1,0:T(8,128)S(1)}, f32[4,576,128]{2,1,0:T(8,128)S(1)}, u32[]{:S(2)}, u32[]{:S(2)}) collective-permute-start(f32[4,576,128]{2,1,0:T(8,128)S(1)} %get-tuple-element.152), channel_id=1, source_target_pairs={{0,4},{4,0},{8,12},{12,8},{16,20},{20,16},{24,28},{28,24},{1,5},{5... | collective-permute-start | bytes 3538952 | tf_op jit(solution)/shard_map/ppermute | solution.py:733
  91.9 54.0 %collective-permute-start.10 = (bf16[2048,384]{1,0:T(8,128)(2,1)}, bf16[2048,384]{1,0:T(8,128)(2,1)}, u32[]{:S(2)}, u32[]{:S(2)}) collective-permute-start(bf16[2048,384]{1,0:T(8,128)(2,1)} %get-tuple-element.130.refs_1_), channel_id=1, source_target_pairs={{0,2},{1,3},{2,0},{3,1},{4,6},{5,7},{6,4},{7,5},{8,10},{9,11},{10,... | collective-permute-start | bytes 4718600 | tf_op jit(solution)/shard_map/ppermute | solution.py:733
  93.2 6.4 %collective-permute-start.14 = (f32[136,384]{1,0:T(8,128)S(1)}, f32[136,384]{1,0:T(8,128)S(1)}, u32[]{:S(2)}, u32[]{:S(2)}) collective-permute-start(f32[136,384]{1,0:T(8,128)S(1)} %get-tuple-element.144.refs_1_), channel_id=1, source_target_pairs={{0,8},{4,12},{8,0},{12,4},{16,24},{20,28},{24,16},{28,20},{1,9},{5... | collective-permute-start | bytes 626696 | tf_op jit(solution)/shard_map/ppermute | solution.py:733
  100.2 11.0 %collective-permute-start.15 = (f32[136,384]{1,0:T(8,128)S(1)}, f32[136,384]{1,0:T(8,128)S(1)}, u32[]{:S(2)}, u32[]{:S(2)}) collective-permute-start(f32[136,384]{1,0:T(8,128)S(1)} %get-tuple-element.146.refs_1_), channel_id=1, source_target_pairs={{0,16},{4,20},{8,24},{12,28},{16,0},{20,4},{24,8},{28,12},{1,17},{... | collective-permute-start | bytes 626696 | tf_op jit(solution)/shard_map/ppermute | solution.py:733
  119.8 21.9 %collective-permute-start.18 = (bf16[576,128]{1,0:T(8,128)(2,1)S(1)}, bf16[576,128]{1,0:T(8,128)(2,1)S(1)}, u32[]{:S(2)}, u32[]{:S(2)}) collective-permute-start(bf16[576,128]{1,0:T(8,128)(2,1)S(1)} %get-tuple-element.160), channel_id=1, source_target_pairs={{0,8},{4,12},{8,0},{12,4},{16,24},{20,28},{24,16},{28,20},{1,9},{5... | collective-permute-start | bytes 442376 | tf_op jit(solution)/shard_map/ppermute | solution.py:733
  119.9 21.8 %collective-permute-start.19 = (bf16[576,128]{1,0:T(8,128)(2,1)S(1)}, bf16[576,128]{1,0:T(8,128)(2,1)S(1)}, u32[]{:S(2)}, u32[]{:S(2)}) collective-permute-start(bf16[576,128]{1,0:T(8,128)(2,1)S(1)} %get-tuple-element.161), channel_id=1, source_target_pairs={{0,16},{4,20},{8,24},{12,28},{16,0},{20,4},{24,8},{28,12},{1,17},{... | collective-permute-start | bytes 442376 | tf_op jit(solution)/shard_map/ppermute | solution.py:733
  122.8 18.9 %collective-permute-start.20 = (bf16[576,128]{1,0:T(8,128)(2,1)S(1)}, bf16[576,128]{1,0:T(8,128)(2,1)S(1)}, u32[]{:S(2)}, u32[]{:S(2)}) collective-permute-start(bf16[576,128]{1,0:T(8,128)(2,1)S(1)} %get-tuple-element.162), channel_id=1, source_target_pairs={{0,24},{4,28},{8,16},{12,20},{16,8},{20,12},{24,0},{28,4},{1,25},{... | collective-permute-start | bytes 442376 | tf_op jit(solution)/shard_map/ppermute | solution.py:733
  140.2 5.7 %collective-permute-start.16 = (f32[8,640]{1,0:T(8,128)S(1)}, f32[8,640]{1,0:T(8,128)S(1)}, u32[]{:S(2)}, u32[]{:S(2)}) collective-permute-start(f32[8,640]{1,0:T(8,128)S(1)} %get-tuple-element.149), channel_id=1, source_target_pairs={{4,0},{8,4},{12,8},{16,12},{20,16},{24,20},{28,24},{5,1},{9,5},{13... | collective-permute-start | bytes 61448 | tf_op jit(solution)/shard_map/ppermute | solution.py:1006
  183.1 10.8 %collective-permute-start.21 = (f32[1024,768]{1,0:T(8,128)}, f32[1024,768]{1,0:T(8,128)}, u32[]{:S(2)}, u32[]{:S(2)}) collective-permute-start(f32[1024,768]{1,0:T(8,128)} %get-tuple-element.164), channel_id=1, source_target_pairs={{0,1},{1,0},{2,3},{3,2},{4,5},{5,4},{6,7},{7,6},{8,9},{9,8},{10,11... | collective-permute-start | bytes 9437192 | tf_op jit(solution)/shard_map/ppermute | solution.py:733
  183.2 6.6 %collective-permute-start.22 = (f32[896,128]{1,0:T(8,128)}, f32[896,128]{1,0:T(8,128)}, u32[]{:S(2)}, u32[]{:S(2)}) collective-permute-start(f32[896,128]{1,0:T(8,128)} %get-tuple-element.166), channel_id=1, source_target_pairs={{0,1},{1,0},{2,3},{3,2},{4,5},{5,4},{6,7},{7,6},{8,9},{9,8},{10,11... | collective-permute-start | bytes 1376264 | tf_op jit(solution)/shard_map/ppermute | solution.py:733
  183.7 27.3 %all-to-all-start = ((bf16[8,288,128]{2,1,0:T(8,128)(2,1)}), bf16[8,288,128]{2,1,0:T(8,128)(2,1)}, u32[]{:S(2)}, u32[]{:S(2)}) async-start(bf16[8,288,128]{2,1,0:T(8,128)(2,1)} %copy-done.19), calls=%async_computation | async-start | bytes 1179648 | tf_op jit(solution)/shard_map/all_to_all | solution.py:799
  192.5 16.6 %collective-permute-start.23 = (f32[448,128]{1,0:T(8,128)S(1)}, f32[448,128]{1,0:T(8,128)S(1)}, u32[]{:S(2)}, u32[]{:S(2)}) collective-permute-start(f32[448,128]{1,0:T(8,128)S(1)} %get-tuple-element.171), channel_id=1, source_target_pairs={{0,2},{1,3},{2,0},{3,1},{4,6},{5,7},{6,4},{7,5},{8,10},{9,11},{10,... | collective-permute-start | bytes 688136 | tf_op jit(solution)/shard_map/ppermute | solution.py:733
  209.1 41.3 %collective-permute-start.24 = (bf16[1024,768]{1,0:T(8,128)(2,1)}, bf16[1024,768]{1,0:T(8,128)(2,1)}, u32[]{:S(2)}, u32[]{:S(2)}) collective-permute-start(bf16[1024,768]{1,0:T(8,128)(2,1)} %get-tuple-element.172.refs_4_), channel_id=1, source_target_pairs={{0,2},{1,3},{2,0},{3,1},{4,6},{5,7},{6,4},{7,5},{8,10},{9,11},{10,... | collective-permute-start | bytes 4718600 | tf_op jit(solution)/shard_map/ppermute | solution.py:733
  209.7 43.1 %collective-permute-start.11 = (bf16[2048,384]{1,0:T(8,128)(2,1)}, bf16[2048,384]{1,0:T(8,128)(2,1)}, u32[]{:S(2)}, u32[]{:S(2)}) collective-permute-start(bf16[2048,384]{1,0:T(8,128)(2,1)} %get-tuple-element.130.refs_1_), channel_id=1, source_target_pairs={{0,1},{1,0},{2,3},{3,2},{4,5},{5,4},{6,7},{7,6},{8,9},{9,8},{10,11... | collective-permute-start | bytes 4718600 | tf_op jit(solution)/shard_map/ppermute | solution.py:733
  209.7 43.1 %collective-permute-start.12 = (bf16[2048,384]{1,0:T(8,128)(2,1)}, bf16[2048,384]{1,0:T(8,128)(2,1)}, u32[]{:S(2)}, u32[]{:S(2)}) collective-permute-start(bf16[2048,384]{1,0:T(8,128)(2,1)} %collective-permute-done.10.refs_2_), channel_id=1, source_target_pairs={{0,1},{1,0},{2,3},{3,2},{4,5},{5,4},{6,7},{7,6},{8,9},{9,8},{10,11... | collective-permute-start | bytes 4718600 | tf_op jit(solution)/shard_map/ppermute | solution.py:733
  211.0 31.9 %all-to-all-start.1 = ((f32[8,64,128]{2,1,0:T(8,128)}), f32[8,64,128]{2,1,0:T(8,128)S(1)}, u32[]{:S(2)}, u32[]{:S(2)}) async-start(f32[8,64,128]{2,1,0:T(8,128)} %pieces.1), calls=%async_computation.1 | async-start | bytes 524288 | tf_op jit(solution)/shard_map/all_to_all | solution.py:799
  215.0 9.9 %collective-permute-start.27 = (bf16[1,576,128]{2,1,0:T(8,128)(2,1)}, bf16[1,576,128]{2,1,0:T(8,128)(2,1)S(1)}, u32[]{:S(2)}, u32[]{:S(2)}) collective-permute-start(bf16[1,576,128]{2,1,0:T(8,128)(2,1)} %bitcast.17), channel_id=1, source_target_pairs={{0,8},{4,12},{8,0},{12,4},{16,24},{20,28},{24,16},{28,20},{1,9},{5... | collective-permute-start | bytes 442376 | tf_op jit(solution)/shard_map/ppermute | solution.py:733
  226.4 15.1 %collective-permute-start.28 = (bf16[2,576,128]{2,1,0:T(8,128)(2,1)S(1)}, bf16[2,576,128]{2,1,0:T(8,128)(2,1)S(1)}, u32[]{:S(2)}, u32[]{:S(2)}) collective-permute-start(bf16[2,576,128]{2,1,0:T(8,128)(2,1)S(1)} %join.2.refs_1_), channel_id=1, source_target_pairs={{0,16},{4,20},{8,24},{12,28},{16,0},{20,4},{24,8},{28,12},{1,17},{... | collective-permute-start | bytes 884744 | tf_op jit(solution)/shard_map/ppermute | solution.py:733
  245.0 27.1 %all-to-all-start.2 = ((bf16[8,416,128]{2,1,0:T(8,128)(2,1)}), bf16[8,416,128]{2,1,0:T(8,128)(2,1)}, u32[]{:S(2)}, u32[]{:S(2)}) async-start(bf16[8,416,128]{2,1,0:T(8,128)(2,1)} %copy-done.4), calls=%async_computation.2 | async-start | bytes 1703936 | tf_op jit(solution)/shard_map/all_to_all | solution.py:799
  250.3 39.7 %collective-permute-start.25 = (bf16[1024,768]{1,0:T(8,128)(2,1)}, bf16[1024,768]{1,0:T(8,128)(2,1)}, u32[]{:S(2)}, u32[]{:S(2)}) collective-permute-start(bf16[1024,768]{1,0:T(8,128)(2,1)} %get-tuple-element.172.refs_4_), channel_id=1, source_target_pairs={{0,1},{1,0},{2,3},{3,2},{4,5},{5,4},{6,7},{7,6},{8,9},{9,8},{10,11... | collective-permute-start | bytes 4718600 | tf_op jit(solution)/shard_map/ppermute | solution.py:733
  250.3 39.6 %collective-permute-start.26 = (bf16[1024,768]{1,0:T(8,128)(2,1)}, bf16[1024,768]{1,0:T(8,128)(2,1)}, u32[]{:S(2)}, u32[]{:S(2)}) collective-permute-start(bf16[1024,768]{1,0:T(8,128)(2,1)} %collective-permute-done.24.refs_5_), channel_id=1, source_target_pairs={{0,1},{1,0},{2,3},{3,2},{4,5},{5,4},{6,7},{7,6},{8,9},{9,8},{10,11... | collective-permute-start | bytes 4718600 | tf_op jit(solution)/shard_map/ppermute | solution.py:733
  250.8 25.4 %collective-permute-start.32 = (bf16[4,576,128]{2,1,0:T(8,128)(2,1)}, bf16[4,576,128]{2,1,0:T(8,128)(2,1)}, u32[]{:S(2)}, u32[]{:S(2)}) collective-permute-start(bf16[4,576,128]{2,1,0:T(8,128)(2,1)} %copy-done.11), channel_id=1, source_target_pairs={{0,4},{4,0},{8,12},{12,8},{16,20},{20,16},{24,28},{28,24},{1,5},{5... | collective-permute-start | bytes 1769480 | tf_op jit(solution)/shard_map/ppermute | solution.py:733
  273.4 8.6 %collective-permute-start.30 = (f32[456,128]{1,0:T(8,128)S(1)}, f32[456,128]{1,0:T(8,128)S(1)}, u32[]{:S(2)}, u32[]{:S(2)}) collective-permute-start(f32[456,128]{1,0:T(8,128)S(1)} %quarter.1.refs_1_), channel_id=1, source_target_pairs={{0,2},{1,3},{2,0},{3,1},{4,6},{5,7},{6,4},{7,5},{8,10},{9,11},{10,... | collective-permute-start | bytes 700424 | tf_op jit(solution)/shard_map/ppermute | solution.py:733
  274.9 11.6 %collective-permute-start.31 = (f32[456,128]{1,0:T(8,128)S(1)}, f32[456,128]{1,0:T(8,128)S(1)}, u32[]{:S(2)}, u32[]{:S(2)}) collective-permute-start(f32[456,128]{1,0:T(8,128)S(1)} %collective-permute-done.29.refs_2_), channel_id=1, source_target_pairs={{0,2},{1,3},{2,0},{3,1},{4,6},{5,7},{6,4},{7,5},{8,10},{9,11},{10,... | collective-permute-start | bytes 700424 | tf_op jit(solution)/shard_map/ppermute | solution.py:733
  (51 other events, 727.0 us)

commit v2 on v1

--- a/solution.py
+++ b/solution.py
@@ -1,4 +1,5 @@
 import functools
+import math
 
 import jax
 import jax.numpy as jnp
@@ -15,7 +16,7 @@
 LANES = 128
 PARTS = GROUP // CHUNK
 EPS = 1e-05
-VMEM_LIMIT = 16 * 1024 * 1024
+VMEM_LIMIT = 10 * 1024 * 1024
 F32 = jnp.float32
 BF16 = jnp.bfloat16
 
@@ -297,11 +298,10 @@
         out[...] = (keep[at] + arrived[at]).astype(BF16)
 
 
-def k_join(mask, place, mine, other, out):
-    count = mine.shape[0]
-    upper = (place[3] // mask) % 2
-    out[pl.ds(upper * count, count)] = mine[...]
-    out[pl.ds((1 - upper) * count, count)] = other[...]
+def k_join(place, *refs):
+    out = refs[-1]
+    for k, part in enumerate(refs[:-1]):
+        out[(place[3] // 2) ^ k] = part[...]
 
 
 def k_within_back(
@@ -367,23 +367,31 @@
         lead_o[...] = out[0, 0:8, :]
 
 
-def k_back(
-    place, valid, h, xs, bc, g, pre, dt, cum, v, cv, dxw, dbc, rq, qw, ent, ds, qd, endg,
-    rims, rim_in, cx, cb, hp, acc_gain, acc_skip,
-    gx_o, gbc_o, gpre_o, grads_o, keep_o, send_o,
-    gbuf, small_o, acc_x, acc_bc, acc_dt, acc_taps, acc_heads,
-):
+def k_back(final, place, *refs):
+    (
+        valid, h, xs, bc, g, pre, dt, cum, v, cv, dxw, dbc, rq, qw, ent, ds, qd, endg, rims, cx, cb, hp,
+    ) = refs[:22]
+    if final:
+        rim_in, acc_gain, acc_skip = refs[22:25]
+        gx_o, gbc_o, gpre_o = refs[33:36]
+        acc_x, acc_bc, acc_dt, acc_taps, acc_heads = refs[36:41]
+        grads_o, keep_o, send_o, gbuf, small_o = refs[41:]
+    else:
+        gx_o, gbc_o, gpre_o, acc_x, acc_bc, acc_dt, acc_taps, acc_heads, gbuf = refs[22:]
     i = pl.program_id(0)
     last = pl.num_programs(0) - 1
+    group = i + pl.num_programs(0) if final else i
     width = xs.shape[1]
     heads = gather_heads(width)
     skip = spread(hp[2:3, :], width)
     rate = -jnp.exp(hp[1:2, :])
 
-    @pl.when(i == 0)
-    def _():
-        for ref in (acc_x, acc_bc, acc_dt, acc_taps, acc_heads):
-            ref[...] = jnp.zeros_like(ref)
+    if not final:
+
+        @pl.when(i == 0)
+        def _():
+            for ref in (acc_x, acc_bc, acc_dt, acc_taps, acc_heads):
+                ref[...] = jnp.zeros_like(ref)
 
     upper, below = tri("ge").astype(BF16), tri("lt").astype(BF16)
     both = jnp.concatenate([upper, upper, below, below], axis=1)
@@ -410,7 +418,7 @@
         g_ld = mm(both, jnp.concatenate(split2(rq[rows, :]) + split2(qs), axis=0)) + ends
         step = dt[rows, :]
         direct = jnp.where(step > 0.0, (qw[rows, :] + qs) / jnp.where(step > 0.0, step, 1.0), 0.0)
-        live = iota((CHUNK, LANES), 0) + c * CHUNK < valid[i]
+        live = iota((CHUNK, LANES), 0) + c * CHUNK < valid[group]
         own = iota((CHUNK, LANES), 1) < width // P_SIZE
         g_pre = jnp.where(
             live & own, (direct + g_ld * rate) * jax.nn.sigmoid(pre[rows, :]), 0.0
@@ -421,13 +429,12 @@
         gpre_o[rows, :] = low
         acc_dt[...] += mm(pltpu.roll(low.astype(F32), place[1], 1).astype(BF16), h[rows, :], 0, 0)[0 : acc_dt.shape[0]]
 
-    @pl.when(i < last)
-    def _():
-        gbuf[GROUP:, :] = rims[0, 0:8, :]
-
-    @pl.when(i == last)
-    def _():
-        gbuf[GROUP:, :] = rim_in[0:8, :]
+    gbuf[GROUP:, :] = rims[0, 0:8, :]
+    if final:
+
+        @pl.when(i == last)
+        def _():
+            gbuf[GROUP:, :] = rim_in[0:8, :]
 
     taps = jnp.concatenate([cx[...], cb[...]], axis=1)
     vv = v[...]
@@ -445,6 +452,8 @@
     hh = h[...]
     acc_x[...] += mm(hh, gx_low, 0, 0)
     acc_bc[...] += mm(hh, bc_high, 0, 0) + mm(hh, bc_low, 0, 0)
+    if not final:
+        return
 
     @pl.when(i == last)
     def _():
@@ -512,35 +521,26 @@
     return gh, fold_rows(gh * (u * rms_inv(u)))
 
 
-def k_input_sent(place, *refs):
-    out, norm_o = refs[9:]
-
-    @pl.when(pl.program_id(0) == 0)
-    def _():
-        norm_o[...] = jnp.zeros_like(norm_o)
-
-    gh, norm = input_grad(*refs[:9])
-    out[...] = gh
-    norm_o[...] += norm
-
-
-def k_input_own(place, *refs):
-    arrived, before, out, norm_o, acc = refs[9:]
+def k_input(begins, own, ends, place, *refs):
+    refs, (out, norm_o, acc) = refs[:-3], refs[-3:]
     i = pl.program_id(0)
 
     @pl.when(i == 0)
     def _():
-        acc[...] = before[...]
+        acc[...] = jnp.zeros_like(acc) if begins else refs[-1][...]
 
     gh, norm = input_grad(*refs[:9])
-    out[...] = (gh + arrived[...]).astype(BF16)
+    out[...] = (gh + refs[9][...]).astype(BF16) if own else gh
     acc[...] += norm
 
     @pl.when(i == pl.num_programs(0) - 1)
     def _():
-        rows = acc.shape[1] // LANES
-        norm_o[0:rows, :] = stacked(jnp.sum(acc[...], axis=0, keepdims=True))
-        norm_o[rows:, :] = jnp.zeros((8 - rows, LANES), F32)
+        if ends:
+            rows = acc.shape[1] // LANES
+            norm_o[0:rows, :] = stacked(jnp.sum(acc[...], axis=0, keepdims=True))
+            norm_o[rows:, :] = jnp.zeros((8 - rows, LANES), F32)
+        else:
+            norm_o[...] = acc[...]
 
 
 def k_reduce(*refs):
@@ -556,22 +556,26 @@
         out[...] = kept[pl.ds(at, rows), :] + arrived[pl.ds(at, rows), :]
 
 
-def k_pieces(kept, arrived, norm, out):
+def k_pieces(kept, arrived, norm, large, out):
     count = out.shape[0]
     rows = kept.shape[0] // count
+    cut = large.shape[1]
     spare = jnp.zeros((7, LANES), F32)
     for k in range(count):
         own = slice(k * rows, (k + 1) * rows)
-        out[k, 0:rows, :] = kept[own, :] + arrived[own, :]
         line = norm[k : k + 1, :] if k < 8 else spare[0:1]
-        out[k, rows:, :] = jnp.concatenate([line, spare], axis=0)
-
-
-def k_reduce_both(large, small, out):
+        small = jnp.concatenate([kept[own, :] + arrived[own, :], line, spare], axis=0)
+        out[k, 0:cut, :] = large[k]
+        out[k, cut:, :] = jnp.concatenate(split2(small), axis=0)
+
+
+def k_reduce_both(cut, parts, out):
     count = out.shape[0]
-    total = tree([large[k].astype(F32) for k in range(count)]).astype(BF16)
-    rest = tree([small[k] for k in range(count)])
-    joined = jnp.concatenate([total, *split2(rest)], axis=0)
+    rows = (out.shape[1] - cut) // 2
+    terms = [parts[k].astype(F32) for k in range(count)]
+    small = tree([term[cut : cut + rows] + term[cut + rows :] for term in terms])
+    large = tree([term[:cut] for term in terms]).astype(BF16)
+    joined = jnp.concatenate([large, *split2(small)], axis=0)
     for k in range(count):
         out[k] = joined
 
@@ -592,27 +596,35 @@
     )
 
 
-def k_unpack(place, mine, other, b, w_zx_o, w_out_o):
+def k_unpack_out(place, mine, other, w_out_o):
+    count = 2 * mine.shape[0]
+    ro = w_out_o.shape[0] // count
+    rows = ro * w_out_o.shape[1] // LANES
+    side = place[3] % 2
+    for k in range(count // 2):
+        for part, at in ((mine, 2 * k + side), (other, 2 * k + 1 - side)):
+            piece = part[k].astype(F32)
+            w_out_o[pl.ds(pl.multiple_of(at * ro, 8), ro), :] = unstack(piece[piece.shape[0] - rows :], ro)
+
+
+def k_unpack(place, mine, other, b, w_zx_o):
     count = b.shape[0]
     dim, _, real = w_zx_o.shape
     rz = dim // count
-    width = -(-real // LANES) * LANES
-    cut = rz * width // LANES
-    ro = width // count
+    cut = rz * -(-real // LANES)
     side = place[3] % 2
     for k in range(count // 2):
         for part, at in ((mine, 2 * k + side), (other, 2 * k + 1 - side)):
             piece = part[k].astype(F32)
             w_zx_o[pl.ds(at * rz, rz), 0, :] = unstack(piece[0:cut], rz)[:, :real]
-            w_out_o[pl.ds(pl.multiple_of(at * ro, 8), ro), :] = unstack(piece[cut:], ro)
     for k in range(count):
         own = unstack(b[k, 0:cut, :].astype(F32), rz)[:, :real]
         w_zx_o[k * rz : (k + 1) * rz, 1, :] = own
 
 
 def k_small(place, *refs):
-    count = len(refs) - 9
-    w_bc_o, w_dt_o, bc_taps_o, bias_o, alog_o, skip_o, norm_o, own_o, buf = refs[count:]
+    count = len(refs) - 10
+    w_bc_o, w_dt_o, bc_taps_o, bias_o, alog_o, skip_o, norm_o, taps_o, gain_o, buf = refs[count:]
     quarter = buf.shape[0] // count
     norms = []
     for k in range(count):
@@ -634,9 +646,12 @@
     bc_taps_o[...] = unstack(buf[at : at + 16, :], 8)[0 : KCONV + 1]
     for k, out in enumerate((bias_o, alog_o, skip_o)):
         out[...] = buf[at + KCONV + 1 + k : at + KCONV + 2 + k, 0 : out.shape[1]]
-    tiles = -(-own_o.shape[1] // LANES)
+    real = taps_o.shape[1]
+    tiles = -(-real // LANES)
     own = buf[pl.ds(pl.multiple_of(at + 16 + place[2] * (8 * tiles), 8), 8 * tiles), :]
-    own_o[...] = unstack(own, 8)[:, 0 : own_o.shape[1]]
+    own = unstack(own, 8)[:, 0:real]
+    taps_o[...] = own[0 : KCONV + 1]
+    gain_o[...] = own[KCONV + 1 : KCONV + 2]
 
 
 def k_out(hid, *refs):
@@ -646,11 +661,11 @@
     out[...] = (hid[...].astype(F32) + total).astype(BF16)
 
 
-def k_in_back(place, hid, og, gain, *refs):
+def k_in_back(steps, place, hid, og, gain, *refs):
     i = pl.program_id(0)
-    half = pl.num_programs(0) // 2
-    count = (len(refs) - 1) // 2
+    cuts = pl.num_programs(0) // steps
     out = refs[-1]
+    count = (len(refs) - 1) // cuts
 
     def finish(parts):
         gh = tree([part[...].astype(F32) for part in parts])
@@ -660,13 +675,8 @@
         dot = jnp.sum(scaled * u, axis=1, keepdims=True) / u.shape[1]
         out[...] = inv * scaled - u * (inv * inv * inv * dot) + og[...].astype(F32)
 
-    @pl.when(i < half)
-    def _():
-        finish(refs[:count])
-
-    @pl.when(i >= half)
-    def _():
-        finish(refs[count : 2 * count])
+    for k in range(cuts):
+        pl.when(i // steps == k)(functools.partial(finish, refs[k * count : (k + 1) * count]))
 
 
 def row_block(shape, rows, at=None):
@@ -680,6 +690,7 @@
 
 
 SMEM = pl.BlockSpec(memory_space=pltpu.SMEM)
+VMEM = pl.BlockSpec(memory_space=pltpu.VMEM)
 
 
 class Kept:
@@ -692,7 +703,7 @@
         return ref.at[pl.ds(start, self.rows)]
 
 
-def call(kernel, steps, ins, outs, scratch, flops, name, place=None):
+def call(kernel, steps, ins, outs, scratch, flops, name, place=None, weight=1, alias=()):
     moved = sum(a.size * a.dtype.itemsize for a, _ in ins)
     for shape, dtype, _ in outs:
         moved += functools.reduce(lambda x, y: x * y, shape) * jnp.dtype(dtype).itemsize
@@ -711,6 +722,16 @@
     places = [
         pl.BlockSpec(memory_space=pltpu.VMEM) if isinstance(spec, Kept) else spec for spec in specs
     ]
+    held = 4 * 1024 * 1024
+    for (shape, dtype), spec in zip(
+        [(a.shape, a.dtype) for a, _ in ins] + [(shape, dtype) for shape, dtype, _ in outs], places
+    ):
+        if spec.block_shape is not None:
+            padded = list(spec.block_shape)
+            padded[-1] = -(-padded[-1] // LANES) * LANES
+            held += 2 * math.prod(padded) * jnp.dtype(dtype).itemsize
+    for buffer in scratch:
+        held += math.prod(buffer.shape) * jnp.dtype(buffer.dtype).itemsize
     return pl.pallas_call(
         body,
         grid_spec=pltpu.PrefetchScalarGridSpec(
@@ -722,9 +743,12 @@
         ),
         out_shape=[jax.ShapeDtypeStruct(s, d) for s, d, _ in outs],
         compiler_params=pltpu.CompilerParams(
-            dimension_semantics=("arbitrary",), vmem_limit_bytes=VMEM_LIMIT
+            dimension_semantics=("arbitrary",), vmem_limit_bytes=max(VMEM_LIMIT, held)
         ),
-        cost_estimate=pl.CostEstimate(flops=flops, bytes_accessed=moved, transcendentals=0),
+        cost_estimate=pl.CostEstimate(
+            flops=flops * weight, bytes_accessed=moved * weight, transcendentals=0
+        ),
+        input_output_aliases={first + k: j for k, j in alias},
         name=name,
     )(*scalars, *[a for a, _ in ins])
 
@@ -773,12 +797,13 @@
             merge(total, other, outs[1])
 
 
-def carried_in(total, backward, place):
+def carried_in(total, backward, place, beside=()):
     before, firsts = [], []
     shape = total.shape
     masks = powers(lax.axis_size("tok"))
     for mask in masks:
-        ins = [total, swap(total, "tok", mask)] + before
+        other = swap(total, "tok", mask)
+        ins = [total, other if before else after(other, *beside), *before]
         last = mask == masks[-1]
         found = call(
             functools.partial(k_merge, mask, backward, not before),
@@ -959,8 +984,9 @@
         3 * 10**9,
         "gate_back",
     )
-    end_grad, first_grad = carried_in(fin_back, True, place)
-    yns = head_gathered(yn)
+    yns = [yn]
+    for mask in powers(head_count)[1:]:
+        yns = yns + [swap(a, "head", mask) for a in yns]
     rows_z, rows_o = dim // tok_count, width // tok_count
     piece_a = (rows_z * width + rows_o * dim) // LANES
     sides = tok_count // 2
@@ -973,14 +999,16 @@
         3 * 10**9,
         "weights",
         place,
-    )
+        4,
+    )
+    end_grad, first_grad = carried_in(fin_back, True, place, (keep_a,))
     arrived_a = swap(after(send_a, first_grad), "tok", 1)
     per_token = [
         out_kept(width, F32), out_kept(2 * N, F32), out_kept(LANES, F32), out_kept(LANES, F32)
     ]
     inner = [kept(xs), kept(bc), kept(after(gm, keep_a)), kept(dt), kept(cum), kept(mix), per_chunk(entry), full(per_head)]
     dxw, dbc, rq, qw = call(
-        k_within_back, groups, inner, per_token, [], 10 * 10**9, "within_back"
+        k_within_back, groups, inner, per_token, [], 10 * 10**9, "within_back", None, 4
     )
 
     def leading(a):
@@ -1009,7 +1037,7 @@
     pairs_a = call(
         k_pair,
         1,
-        [full(after(keep_a, end_grad)), full(arrived_a)],
+        [full(after(keep_a, lead)), full(arrived_a)],
         [out_full((piece_a, LANES), BF16)] * sides,
         [],
         10**6,
@@ -1023,109 +1051,159 @@
     small_rows = 2 * dim + heads * dim // LANES + 16 + head_count * 8 * tiles
     unit = head_count * tok_count * 8
     small_rows = -(-small_rows // unit) * unit
-    gx, gbc, gpre, grads_b, small_keep, small_send = call(
-        k_back,
-        groups,
+    acc_shapes = [(dim, width), (dim, 2 * N), (heads, dim), (8 * KCONV + 8, conv_width), (16, LANES)]
+
+    def back_call(final, more_in, more_out, more_scratch, alias, ready):
+        def at(i, *s):
+            return i + half if final else i
+
+        return call(
+            functools.partial(k_back, final),
+            half,
+            [(group_valid, SMEM)]
+            + [
+                kept(a, at)
+                for a in (after(h, *ready), xs, bc, gm, pre, dt, cum, v, cv, dxw, dbc, rq, qw)
+            ]
+            + [per_chunk(entry, at), per_chunk(ds, at), per_chunk(qd, at), full(end_grad)]
+            + [(rims, Kept(1, lambda i, s: jnp.minimum(at(i) + 1, groups - 1)))]
+            + [full(cx), full(conv_bc), full(per_head)]
+            + more_in,
+            [out_kept(width, BF16, at), out_kept(4 * N, BF16, at), out_kept(LANES, BF16, at)]
+            + [(a, F32, VMEM) for a in acc_shapes]
+            + more_out,
+            [pltpu.VMEM((GROUP + 8, conv_width), F32)] + more_scratch,
+            5 * 10**9,
+            "back_end" if final else "back_start",
+            place,
+            4,
+            alias,
+        )
+
+    partial = back_call(False, [], [], [], (), (pairs_a[0],))
+    (total_a,) = call(
+        k_reduce, 1, [full(after(a, partial[0])) for a in arrived_a], [out_full((piece_a, LANES), BF16)],
+        [], 10**6, "reduce",
+    )
+    found = back_call(
+        True,
+        [full(rim_in), full(acc_gain), full(acc_skip)] + [(a, VMEM) for a in partial],
         [
-            (group_valid, SMEM),
-            kept(h), kept(xs), kept(bc), kept(gm), kept(pre), kept(dt), kept(cum), kept(v), kept(cv),
-            kept(dxw), kept(dbc), kept(rq), kept(qw), per_chunk(entry), per_chunk(ds), per_chunk(qd),
-            full(end_grad),
-            (rims, row_block(rims.shape, 1, lambda i, s: jnp.minimum(i + 1, groups - 1))),
-            full(after(rim_in, pairs_a[0], yns[1])), full(cx), full(conv_bc), full(per_head), full(acc_gain), full(acc_skip),
-        ],
-        [
-            out_kept(width, BF16), out_kept(4 * N, BF16), out_kept(LANES, BF16),
             out_full((tok_count, piece_b, LANES), BF16), out_full((small_rows // 2, LANES), F32),
             out_full((small_rows // 2, LANES), F32),
         ],
-        [
-            pltpu.VMEM((GROUP + 8, conv_width), F32), pltpu.VMEM((small_rows, LANES), F32),
-            pltpu.VMEM((dim, width), F32), pltpu.VMEM((dim, 2 * N), F32), pltpu.VMEM((heads, dim), F32),
-            pltpu.VMEM((8 * KCONV + 8, conv_width), F32), pltpu.VMEM((16, LANES), F32),
-        ],
-        10 * 10**9,
-        "back",
-        place,
-    )
-
-    (total_a,) = call(
-        k_reduce, 1, [full(a) for a in arrived_a], [out_full((piece_a, LANES), BF16)], [], 10**6, "reduce"
-    )
-
-    small_arrived = swap(small_send, "head", 1)
+        [pltpu.VMEM((small_rows, LANES), F32)],
+        [(25 + k, k) for k in range(8)],
+        (total_a, yns[1]),
+    )
+    gx, gbc, gpre = found[:3]
+    grads_b, small_keep, small_send = found[8:]
+    parts_a = distances(total_a, "tok", 2)
+    (mine_a,) = call(
+        k_join, 1, [full(after(a, gx)) for a in parts_a], [out_full((sides, piece_a, LANES), BF16)], [],
+        10**6, "join", place,
+    )
+
+    cuts = 2
+    steps = half // cuts
+    shape = (tokens // 2 // cuts, dim)
+
+    def input_call(own, k, norm, more, ready):
+        def turned(i, s):
+            return i + k * steps + half * (s[0] if own else 1 - s[0])
+
+        ends = own and k == cuts - 1
+        return call(
+            functools.partial(k_input, norm is None, own, ends),
+            steps,
+            [rows(hidden_in, turned)]
+            + [kept(a, turned) for a in (gz, gx, gbc, after(gpre, *ready))]
+            + [full(a) for a in (w_z, w_x, w_bc, w_dt_here)]
+            + [rows(a) for a in more]
+            + ([] if norm is None else [full(norm)]),
+            [
+                (shape, BF16 if own else F32, row_block(shape, GROUP)),
+                out_full((8, LANES if ends else dim), F32),
+            ],
+            [pltpu.VMEM((8, dim), F32)],
+            10**9,
+            "input_own" if own else "input_sent",
+            place,
+        )
+
+    sent, norm = input_call(False, 0, None, [], (mine_a,))
+    arrived = [swap(sent, "head", 1)]
+    small_arrived = after(swap(after(small_send, mine_a), "head", 1), sent)
     for mask in powers(head_count)[1:]:
-        shape = (small_keep.shape[0] // 2, LANES)
+        small_shape = (small_keep.shape[0] // 2, LANES)
         small_keep, small_send = call(
             functools.partial(k_halve, mask), 1, [full(small_keep), full(small_arrived)],
-            [out_full(shape, F32)] * 2, [], 10**6, "halve", place,
+            [out_full(small_shape, F32)] * 2, [], 10**6, "halve", place,
         )
         small_arrived = swap(small_send, "head", mask)
-    shape = (tokens // 2, dim)
-
-    def input_ins(own):
-        def turned(i, s):
-            return i + half * (s[0] if own else 1 - s[0])
-
-        return [rows(hidden_in, turned)] + [
-            kept(a, turned) for a in (gz, gx, gbc, after(gpre, total_a))
-        ] + [
-            full(a) for a in (w_z, w_x, w_bc, w_dt_here)
-        ]
-
-    sent, norm = call(
-        k_input_sent, half, input_ins(False),
-        [(shape, F32, row_block(shape, GROUP)), out_full((8, dim), F32)], [], 3 * 10**9,
-        "input_sent", place,
-    )
-    arrived = after(swap(sent, "head", 1), small_keep)
-    part, norm = call(
-        k_input_own, half, input_ins(True) + [rows(arrived), full(norm)],
-        [(shape, BF16, row_block(shape, GROUP)), out_full((8, LANES), F32)],
-        [pltpu.VMEM((8, dim), F32)], 3 * 10**9, "input_own", place,
-    )
-    parts = [after(part, small_arrived)]
-    for mask in powers(head_count)[1:]:
-        parts = parts + [swap(a, "head", mask) for a in parts]
-    others = [swap(a, "head", 1) for a in parts]
-
+    for k in range(1, cuts):
+        sent, norm = input_call(False, k, norm, [], (mine_a, small_keep))
+        arrived.append(swap(sent, "head", 1))
+    parts = []
+    for k in range(cuts):
+        part, norm = input_call(True, k, norm, [arrived[k]], (mine_a,))
+        found = [part]
+        for mask in powers(head_count)[1:]:
+            found = found + [swap(a, "head", mask) for a in found]
+        parts.append(found)
+
+    shape = (tok_count, piece_b + 2 * (small_keep.shape[0] // tok_count + 8), LANES)
+    (pieces,) = call(
+        k_pieces, 1, [full(small_keep), full(small_arrived), full(norm), full(grads_b)],
+        [out_full(shape, BF16)], [], 10**6, "pieces",
+    )
+    other_a = swap(after(mine_a, pieces), "tok", 1)
+    yns = yns + [swap(after(a, pieces), "head", 1) for a in yns]
     (block_out,) = call(
         k_out,
         groups,
-        [rows(hidden_in)] + [rows(a) for a in yns] + [full(a) for a in w_outs],
+        [rows(after(hidden_in, pieces))] + [rows(a) for a in yns] + [full(a) for a in w_outs],
         [out_rows(dim, BF16)],
         [],
         5 * 10**9,
         "out",
     )
-    arrived_b = exchange(grads_b, "tok")
-    joined = total_a[None]
-    shape = joined.shape
-    joins = []
-    for mask in powers(sides):
-        shape = (2 * shape[0],) + shape[1:]
-        (joined,) = call(
-            functools.partial(k_join, 2 * mask), 1, [full(joined), full(swap(joined, "tok", 2 * mask))],
-            [out_full(shape, BF16)], [], 10**6, "join", place,
-        )
-        joins.append(joined)
-    mine_a = joined
-    other_a = swap(mine_a, "tok", 1)
-    shape = (tok_count, small_keep.shape[0] // tok_count + 8, LANES)
-    (pieces,) = call(
-        k_pieces, 1, [full(small_keep), full(small_arrived), full(norm)], [out_full(shape, F32)], [],
-        10**6, "pieces",
-    )
-    pieces = exchange(pieces, "tok")
-    shape = (tok_count, piece_b + 2 * pieces.shape[1], LANES)
+
     (copies,) = call(
-        k_reduce_both, 1, [full(after(arrived_b, mine_a)), full(pieces)], [out_full(shape, BF16)], [], 10**6,
-        "reduce_both",
+        functools.partial(k_reduce_both, piece_b), 1,
+        [full(after(exchange(pieces, "tok"), block_out, other_a))],
+        [out_full(shape, BF16)], [], 10**6, "reduce_both",
     )
     sum_b = exchange(copies, "tok")
+    (grad_w_out,) = call(
+        k_unpack_out, 1, [full(after(mine_a, copies)), full(other_a)], [out_full((width, dim), F32)],
+        [], 10**6, "unpack_out", place,
+    )
+    others = [
+        [swap(found[0], "head", 1)] + [swap(after(a, grad_w_out), "head", 1) for a in found[1:]]
+        for found in parts
+    ]
+
+    def turned_back(i, s):
+        return lax.rem(i + half * s[0], groups)
+
+    def in_cut(a, k):
+        return (a, row_block(a.shape, GROUP, lambda i, s: jnp.clip(i - k * steps, 0, steps - 1)))
+
+    (grad_in,) = call(
+        functools.partial(k_in_back, steps),
+        groups,
+        [rows(hidden_in, turned_back), rows(out_grad, turned_back), full(gain_in)]
+        + [in_cut(a, k) for k, found in enumerate(parts + others) for a in found],
+        [out_rows(dim, F32, turned_back)],
+        [],
+        10**9,
+        "in_back",
+        place,
+    )
     shape = (small_rows // head_count + tok_count, LANES)
     (quarter,) = call(
-        functools.partial(k_quarter, piece_b), 1, [full(after(sum_b, block_out))], [out_full(shape, F32)],
+        functools.partial(k_quarter, piece_b), 1, [full(after(sum_b, grad_in))], [out_full(shape, F32)],
         [], 10**6, "quarter",
     )
     quarters = [(quarter, 0)]
@@ -1133,24 +1211,24 @@
         quarters = quarters + [(swap(a, "head", mask), k | mask) for a, k in quarters]
     quarters = [a for a, _ in sorted(quarters, key=lambda item: item[1])]
 
-    grad_w_zx, grad_w_out = call(
+    (grad_w_zx,) = call(
         k_unpack,
         1,
         [full(mine_a), full(other_a), full(sum_b)],
-        [out_full((dim, 2, real), F32), out_full((width, dim), F32)],
+        [out_full((dim, 2, real), F32)],
         [],
         10**6,
         "unpack",
         place,
     )
-    grad_w_bc, grad_w_dt, grad_taps, grad_bias, grad_alog, grad_skip, grad_norm, own = call(
+    grad_w_bc, grad_w_dt, grad_taps, grad_bias, grad_alog, grad_skip, grad_norm, own_taps, own_gain = call(
         k_small,
         1,
         [full(a) for a in quarters],
         [
             out_full((dim, 2 * N), F32), out_full((heads, dim), F32), out_full((KCONV + 1, 2 * N), F32),
             out_full((1, heads), F32), out_full((1, heads), F32), out_full((1, heads), F32),
-            out_full((1, dim), F32), out_full((8, real), F32),
+            out_full((1, dim), F32), out_full((KCONV + 1, real), F32), out_full((1, real), F32),
         ],
         [pltpu.VMEM((small_rows, LANES), F32)],
         10**6,
@@ -1158,27 +1236,6 @@
         place,
     )
 
-    def turned_back(i, s):
-        return lax.rem(i + half * s[0], groups)
-
-    def first_half(a):
-        return (a, row_block(a.shape, GROUP, lambda i, s: jnp.minimum(i, half - 1)))
-
-    def second_half(a):
-        return (a, row_block(a.shape, GROUP, lambda i, s: jnp.maximum(i - half, 0)))
-
-    (grad_in,) = call(
-        k_in_back,
-        groups,
-        [rows(hidden_in, turned_back), rows(out_grad, turned_back), full(gain_in)]
-        + [first_half(a) for a in parts]
-        + [second_half(a) for a in others],
-        [out_rows(dim, F32, turned_back)],
-        [],
-        10**9,
-        "in_back",
-        place,
-    )
     return (
         block_out,
         grad_in,
@@ -1188,10 +1245,10 @@
         grad_w_dt.T,
         grad_bias[0],
         grad_alog[0],
-        own[: KCONV + 1],
+        own_taps,
         grad_taps,
         grad_skip[0],
-        own[KCONV + 1],
+        own_gain[0],
         grad_w_out[:real],
     )
 

time: 303 us -> 247 us (0.82)
  waiting for transfers between devices: 70.1 us -> 37.4 us
  local copies, waits for them, and re-layouts: 35.5 us -> 23.2 us
  Pallas kernels: 142 us -> 134 us
  starting transfers between devices: 51.6 us -> 48.4 us
    ppermute x31 -> x36, waiting for transfers between devices: 62.6 us -> 34.9 us  [swap(): lax.ppermute(value, axis, [(i, i ^ mask) for i in range(lax.axis_size(axi...]
    pallas_call x30 -> x33, Pallas kernels: 142 us -> 134 us  [call(): pl.pallas_call(body, grid_spec=pltpu.PrefetchScalarGridSpec(num_scalar_pr...]
    unnamed x95 -> x77, local copies, waits for them, and re-layouts: 25.1 us -> 17.1 us
    all_to_all x3 -> x2, starting transfers between devices: 13.5 us -> 8.8 us  [exchange(): return lax.all_to_all(pieces, axis, 0, 0, tiled=True)]
    ppermute x1, waiting for transfers between devices: 3.42 us -> 0.01 us  [on_device(): lax.ppermute(lead, 'tok', [(i, i - 1) for i in range(1, tok_count)])]
    ppermute x31 -> x36, starting transfers between devices: 31.7 us -> 33.1 us  [swap(): lax.ppermute(value, axis, [(i, i ^ mask) for i in range(lax.axis_size(axi...]
  transfers between devices with their start and end apart: 36 -> 40, of which waited for: 14 -> 13; matrix products, arithmetic and copies ran while one was open for 4% -> 3% of each run, Pallas kernels for 28% -> 47%
where the time goes in v2:
time: 247 us; the launch traced here: 246 us
  Pallas kernels  134 us (54%)
  starting transfers between devices  48.4 us (20%)
  waiting for transfers between devices  37.4 us (15%)
  local copies, waits for them, and re-layouts  23.2 us (9%)
    pallas_call x33, Pallas kernels, call(): pl.pallas_call(body, grid_spec=pltpu.PrefetchScalarGridSpec(num_scalar_pr...  134 us
    ppermute x36, waiting for transfers between devices, swap(): lax.ppermute(value, axis, [(i, i ^ mask) for i in range(lax.axis_size(axi...  34.9 us
    ppermute x36, starting transfers between devices, swap(): lax.ppermute(value, axis, [(i, i ^ mask) for i in range(lax.axis_size(axi...  33.1 us
    unnamed x77, local copies, waits for them, and re-layouts  17.1 us
    all_to_all x2, starting transfers between devices, exchange(): return lax.all_to_all(pieces, axis, 0, 0, tiled=True)  8.8 us
  transfers between devices with their start and end apart: 40, of which 13 were waited for; matrix products, arithmetic and copies ran while one was open for 3% of the time, Pallas kernels for 47%

profile of v2, /device:TPU:0, one launch (start us, length us, event | category | flops | bytes accessed | tf_op | source)
XLA Modules:
  0.0 245.8 jit_solution(568784890425360178)
XLA Ops:
  1.4 4.9 %collective-permute-start = (bf16[16,768]{1,0:T(8,128)(2,1)S(1)}, bf16[16,768]{1,0:T(8,128)(2,1)S(1)}, u32[]{:S(2)}, u32[]{:S(2)}) collective-permute-start(bf16[16,768]{1,0:T(8,128)(2,1)S(1)} %slice.11), channel_id=1, source_target_pairs={{0,4},{4,8},{8,12},{12,16},{16,20},{20,24},{24,28},{1,5},{5,9},{9,... | collective-permute-start | bytes 73736 | tf_op jit(solution)/shard_map/ppermute | solution.py:860
  8.6 3.7 %fusion = (bf16[768,1,384]{2,1,0:T(2,128)(2,1)S(1)}, bf16[768,1,384]{2,1,0:T(2,128)(2,1)S(1)}) fusion(bf16[768,2,384]{2,1,0:T(2,128)(2,1)} %param.17), kind=kLoop, calls=%fused_computation.6 | loop fusion | bytes 2359296 | tf_op jit(solution)/shard_map/slice | solution.py:862
  14.4 5.4 %project.1 = (bf16[2048,768]{1,0:T(8,128)(2,1)S(1)}, f32[2048,640]{1,0:T(8,128)S(1)}, f32[2048,128]{1,0:T(8,128)S(1)}) custom-call(bf16[2048,768]{1,0:T(8,128)(2,1)S(1)} %copy-done.2, f32[1,768]{1,0:T(1,128)S(1)} %broadcast_in_dim.6.refs_1_.refs_5_.refs_3_, bf16[768,384]{1,0:T(8,128)(2,1)S(1)} %get-tuple-element.131.refs_2_.refs_6_.refs_7_, ...), custom_call_target="tpu_custom_call" | custom-call | flops 4000000000 | bytes 13769728 | tf_op jit(solution)/shard_map/project/pallas_call | solution.py:735
  19.9 12.8 %conv.1 = (f32[2048,640]{1,0:T(8,128)S(1)}, bf16[2048,384]{1,0:T(8,128)(2,1)S(1)}, bf16[2048,256]{1,0:T(8,128)(2,1)S(1)}, f32[2048,128]{1,0:T(8,128)S(1)}, f32[2...) custom-call(s32[8]{0:T(128)S(1)} %copy-done.20, ...), custom_call_target="tpu_custom_call" | custom-call | flops 4000000000 | bytes 20659776 | tf_op jit(solution)/shard_map/conv/pallas_call | solution.py:735
  34.3 5.1 %collective-permute-done.1.refs_2_ = f32[136,384]{1,0:T(8,128)S(1)} collective-permute-done((f32[136,384]{1,0:T(8,128)S(1)}, f32[136,384]{1,0:T(8,128)S(1)}, u32[]{:S(2)}, u32[]{:S(2)}) %collective-permute-start.1) | collective-permute-done | bytes 208928 | tf_op jit(solution)/shard_map/ppermute | solution.py:757
  41.7 4.5 %proj.1 = (f32[2048,384]{1,0:T(8,128)S(1)}, f32[2048,384]{1,0:T(8,128)S(1)}) custom-call(bf16[2048,768]{1,0:T(8,128)(2,1)S(1)} %get-tuple-element.193.refs_0_.refs_3_.refs_2_, bf16[2048,768]{1,0:T(8,128)(2,1)S(1)} %copy-done.11, bf16[768,384]{1,0:T(8,128)(2,1)S(1)} %get-tuple-element.153.refs_2_.refs_6_, bf16[384,768]{1,0:T(8,128)(2,1)S(1)} %copy-done.21), custom_call_target="tpu_custom_call" | custom-call | flops 5000000000 | bytes 13762560 | tf_op jit(solution)/shard_map/proj/pallas_call | solution.py:735
  46.8 2.6 %collective-permute-start.3 = (f32[136,384]{1,0:T(8,128)S(1)}, f32[136,384]{1,0:T(8,128)S(1)}, u32[]{:S(2)}, u32[]{:S(2)}) collective-permute-start(f32[136,384]{1,0:T(8,128)S(1)} %get-tuple-element.144.refs_1_), channel_id=1, source_target_pairs={{0,16},{4,20},{8,24},{12,28},{16,0},{20,4},{24,8},{28,12},{1,17},{... | collective-permute-start | bytes 626696 | tf_op jit(solution)/shard_map/ppermute | solution.py:757
  49.5 5.5 %within.1.refs_5_ = f32[2048,384]{1,0:T(8,128)S(1)} custom-call(bf16[2048,384]{1,0:T(8,128)(2,1)S(1)} %get-tuple-element.150.refs_0_.refs_6_.refs_5_.refs_1_.refs_3_, bf16[2048,256]{1,0:T(8,128)(2,1)S(1)} %get-tuple-element.148.refs_1_.refs_3_.refs_6_.refs_2_.refs_4_, f32[2048,128]{1,0:T(8,128)S(1)} %get-tuple-element.151.refs_2_.refs_3_.refs_4_.refs_7_, ...), custom_call_target="tpu_custom_call" | custom-call | flops 5000000000 | bytes 7864320 | tf_op jit(solution)/shard_map/within/pallas_call | solution.py:735
  54.9 4.7 %collective-permute-done.3.refs_2_ = f32[136,384]{1,0:T(8,128)S(1)} collective-permute-done((f32[136,384]{1,0:T(8,128)S(1)}, f32[136,384]{1,0:T(8,128)S(1)}, u32[]{:S(2)}, u32[]{:S(2)}) %collective-permute-start.3) | collective-permute-done | bytes 208928 | tf_op jit(solution)/shard_map/ppermute | solution.py:757
  60.3 4.3 %gate.1 = (f32[2048,384]{1,0:T(8,128)S(1)}, f32[16,128,384]{2,1,0:T(8,128)S(1)}, f32[2,2048]{1,0:T(2,128)S(1)}) custom-call(f32[16,128,384]{2,1,0:T(8,128)S(1)} %get-tuple-element.139.refs_0_, f32[16,1,384]{2,1,0:T(1,128)S(1)} %get-tuple-element.140.refs_1_, f32[136,384]{1,0:T(8,128)S(1)} %merge.8.refs_2_, ...), custom_call_target="tpu_custom_call" | custom-call | flops 3000000000 | bytes 22799872 | tf_op jit(solution)/shard_map/gate/pallas_call | solution.py:735
  69.7 9.3 %gate_back.1 = (bf16[2048,384]{1,0:T(8,128)(2,1)}, bf16[2048,384]{1,0:T(8,128)(2,1)S(1)}, bf16[2048,384]{1,0:T(8,128)(2,1)S(1)}, f32[16,128,384]{2,1,0:T(8,128)S...) custom-call(s32[8]{0:T(128)S(1)} %copy-done.20, ...), custom_call_target="tpu_custom_call" | custom-call | flops 3000000000 | bytes 21296672 | tf_op jit(solution)/shard_map/gate_back/pallas_call | solution.py:735
  80.5 7.0 %weights.1 = (f32[4,576,128]{2,1,0:T(8,128)S(1)}, f32[4,576,128]{2,1,0:T(8,128)S(1)}) custom-call(s32[4]{0:T(128)S(1)} %pad_add_fusion.refs_0_, bf16[2048,384]{1,0:T(8,128)(2,1)} %get-tuple-element.226.refs_1_, bf16[2048,768]{1,0:T(8,128)(2,1)S(1)} %copy-done.11, bf16[2048,768]{1,0:T(8,128)(2,1)S(1)} %get-tuple-element.193.refs_0_.refs_3_.refs_2_, ...), custom_call_target="tpu_custom_call" | custom-call | flops 12000000000 | bytes 47185920 | tf_op jit(solution)/shard_map/weights/pallas_call | solution.py:735
  89.3 5.0 %collective-permute-done.11.refs_2_ = f32[136,384]{1,0:T(8,128)S(1)} collective-permute-done((f32[136,384]{1,0:T(8,128)S(1)}, f32[136,384]{1,0:T(8,128)S(1)}, u32[]{:S(2)}, u32[]{:S(2)}) %collective-permute-start.11) | collective-permute-done | bytes 208928 | tf_op jit(solution)/shard_map/ppermute | solution.py:757
  96.2 13.0 %within_back.1 = (f32[2048,384]{1,0:T(8,128)S(1)}, f32[2048,256]{1,0:T(8,128)S(1)}, f32[2048,128]{1,0:T(8,128)S(1)}, f32[2048,128]{1,0:T(8,128)S(1)}) custom-call(bf16[2048,384]{1,0:T(8,128)(2,1)S(1)} %get-tuple-element.150.refs_0_.refs_6_.refs_5_.refs_1_.refs_3_, bf16[2048,256]{1,0:T(8,128)(2,1)S(1)} %get-tuple-element.148.refs_1_.refs_3_.refs_6_.refs_2_.refs_4_, ...), custom_call_target="tpu_custom_call" | custom-call | flops 40000000000 | bytes 79708160 | tf_op jit(solution)/shard_map/within_back/pallas_call | solution.py:735
  109.8 3.0 %rim.1 = (f32[8,16,640]{2,1,0:T(8,128)S(1)}, f32[8,640]{1,0:T(8,128)S(1)}) custom-call(s32[8]{0:T(128)S(1)} %copy-done.20, bf16[2048,384]{1,0:T(8,128)(2,1)S(1)} %get-tuple-element.150.refs_0_.refs_6_.refs_5_.refs_1_.refs_3_, bf16[2048,256]{1,0:T(8,128)(2,1)S(1)} %get-tuple-element.148.refs_1_.refs_3_.refs_6_.refs_2_.refs_4_, ...), custom_call_target="tpu_custom_call" | custom-call | flops 1000000000 | bytes 21557280 | tf_op jit(solution)/shard_map/rim/pallas_call | solution.py:735
  120.7 2.5 %copy-done.33 = f32[2048,640]{1,0:T(8,128)S(1)} copy-done((f32[2048,640]{1,0:T(8,128)S(1)}, f32[2048,640]{1,0:T(8,128)}, u32[]{:S(2)}) %copy-start.33) | copy-done | bytes 5242904
  123.2 11.4 %back_start.1 = (bf16[2048,384]{1,0:T(8,128)(2,1)S(1)}, bf16[2048,512]{1,0:T(8,128)(2,1)S(1)}, bf16[2048,128]{1,0:T(8,128)(2,1)S(1)}, f32[768,384]{1,0:T(8,128)S...) custom-call(s32[4]{0:T(128)S(1)} %pad_add_fusion.refs_0_, ...), custom_call_target="tpu_custom_call" | custom-call | flops 20000000000 | bytes 166103168 | tf_op jit(solution)/shard_map/back_start/pallas_call | solution.py:735
  134.7 2.7 %collective-permute-start.21 = (bf16[576,128]{1,0:T(8,128)(2,1)S(1)}, bf16[576,128]{1,0:T(8,128)(2,1)S(1)}, u32[]{:S(2)}, u32[]{:S(2)}) collective-permute-start(bf16[576,128]{1,0:T(8,128)(2,1)S(1)} %reduce.3.refs_1_), channel_id=1, source_target_pairs={{0,24},{4,28},{8,16},{12,20},{16,8},{20,12},{24,0},{28,4},{1,25},{... | collective-permute-start | bytes 442376 | tf_op jit(solution)/shard_map/ppermute | solution.py:757
  140.4 13.9 %back_end.1 = (bf16[2048,384]{1,0:T(8,128)(2,1)S(1)}, bf16[2048,512]{1,0:T(8,128)(2,1)S(1)}, bf16[2048,128]{1,0:T(8,128)(2,1)S(1)}, f32[768,384]{1,0:T(8,128)S(1...) custom-call(s32[4]{0:T(128)S(1)} %pad_add_fusion.refs_0_, ...), custom_call_target="tpu_custom_call", output_to_operand_aliasing={{0}: (26, {}), {1}: (27, {}), {2}: (28, {}), {3}: (29, {}),... | custom-call | flops 20000000000 | bytes 197691520 | tf_op jit(solution)/shard_map/back_end/pallas_call | solution.py:735
  155.0 2.4 input_sent.2
  158.6 2.4 input_sent.3
  162.7 2.4 input_own.2
  165.2 2.4 input_own.3
  170.6 4.2 %all-to-all-start = ((bf16[8,416,128]{2,1,0:T(8,128)(2,1)}), bf16[8,416,128]{2,1,0:T(8,128)(2,1)}, u32[]{:S(2)}, u32[]{:S(2)}) async-start(bf16[8,416,128]{2,1,0:T(8,128)(2,1)} %copy-done.10), calls=%async_computation | async-start | bytes 1703936 | tf_op jit(solution)/shard_map/all_to_all | solution.py:824
  183.1 11.0 %out.1 = bf16[2048,768]{1,0:T(8,128)(2,1)} custom-call(bf16[2048,768]{1,0:T(8,128)(2,1)S(1)} %copy-done.2, bf16[2048,384]{1,0:T(8,128)(2,1)} %get-tuple-element.226.refs_1_, bf16[2048,384]{1,0:T(8,128)(2,1)} %collective-permute-done.17.refs_2_, bf16[2048,384]{1,0:T(8,128)(2,1)} %collective-permute-done.26.refs_3_, ...), custom_call_target="tpu_custom_call" | custom-call | flops 5000000000 | bytes 14942208 | tf_op jit(solution)/shard_map/out/pallas_call | solution.py:735
  194.0 5.3 %collective-permute-done.31.refs_2_ = bf16[4,576,128]{2,1,0:T(8,128)(2,1)S(1)} collective-permute-done((bf16[4,576,128]{2,1,0:T(8,128)(2,1)}, bf16[4,576,128]{2,1,0:T(8,128)(2,1)S(1)}, u32[]{:S(2)}, u32[]{:S(2)}) %collective-permute-start.31) | collective-permute-done | bytes 589856 | tf_op jit(solution)/shard_map/ppermute | solution.py:757
  202.3 4.6 %all-to-all-start.1 = ((bf16[8,416,128]{2,1,0:T(8,128)(2,1)}), bf16[8,416,128]{2,1,0:T(8,128)(2,1)}, u32[]{:S(2)}, u32[]{:S(2)}) async-start(bf16[8,416,128]{2,1,0:T(8,128)(2,1)} %copy-done.9), calls=%async_computation.1 | async-start | bytes 1703936 | tf_op jit(solution)/shard_map/all_to_all | solution.py:824
  213.3 2.0 collective-permute-done.32.refs_9_
  218.3 7.9 %in_back.1 = f32[2048,768]{1,0:T(8,128)} custom-call(s32[4]{0:T(128)S(1)} %pad_add_fusion.refs_0_, bf16[2048,768]{1,0:T(8,128)(2,1)S(1)} %copy-done.2, bf16[2048,768]{1,0:T(8,128)(2,1)S(1)} %copy-done.12, f32[1,768]{1,0:T(1,128)S(1)} %broadcast_in_dim.6.refs_1_.refs_5_.refs_3_, bf16[512,768]{1,0:T(8,128)(2,1)S(1)} %copy-done.17, ...), custom_call_target="tpu_custom_call" | custom-call | flops 1000000000 | bytes 18877440 | tf_op jit(solution)/shard_map/in_back/pallas_call | solution.py:735
  226.2 2.5 %all-to-all-done.1.refs_0_.refs_3_ = bf16[8,416,128]{2,1,0:T(8,128)(2,1)} async-done(((bf16[8,416,128]{2,1,0:T(8,128)(2,1)}), bf16[8,416,128]{2,1,0:T(8,128)(2,1)}, u32[]{:S(2)}, u32[]{:S(2)}) %all-to-all-start.1) | async-done | bytes 852000 | tf_op jit(solution)/shard_map/all_to_all | solution.py:824
  235.1 3.7 %unpack.1 = f32[768,2,384]{2,1,0:T(2,128)} custom-call(s32[4]{0:T(128)S(1)} %pad_add_fusion.refs_0_, bf16[4,576,128]{2,1,0:T(8,128)(2,1)S(1)} %copy-done.8, bf16[4,576,128]{2,1,0:T(8,128)(2,1)S(1)} %copy-done.15, bf16[8,416,128]{2,1,0:T(8,128)(2,1)} %all-to-all-done.1.refs_0_.refs_3_), custom_call_target="tpu_custom_call" | custom-call | flops 1000000 | bytes 4390912 | tf_op jit(solution)/shard_map/unpack/pallas_call | solution.py:735
  238.8 4.3 %collective-permute-done.37.refs_4_ = f32[456,128]{1,0:T(8,128)S(1)} collective-permute-done((f32[456,128]{1,0:T(8,128)S(1)}, f32[456,128]{1,0:T(8,128)S(1)}, u32[]{:S(2)}, u32[]{:S(2)}) %collective-permute-start.37) | collective-permute-done | bytes 233504 | tf_op jit(solution)/shard_map/ppermute | solution.py:757
  (171 shorter events, 68.2 us)
Async XLA Ops:
  1.4 18.4 %collective-permute-start = (bf16[16,768]{1,0:T(8,128)(2,1)S(1)}, bf16[16,768]{1,0:T(8,128)(2,1)S(1)}, u32[]{:S(2)}, u32[]{:S(2)}) collective-permute-start(bf16[16,768]{1,0:T(8,128)(2,1)S(1)} %slice.11), channel_id=1, source_target_pairs={{0,4},{4,8},{8,12},{12,16},{16,20},{20,24},{24,28},{1,5},{5,9},{9,... | collective-permute-start | bytes 73736 | tf_op jit(solution)/shard_map/ppermute | solution.py:860
  12.8 28.9 %collective-permute-start.4 = (bf16[384,768]{1,0:T(8,128)(2,1)S(1)}, bf16[384,768]{1,0:T(8,128)(2,1)S(1)}, u32[]{:S(2)}, u32[]{:S(2)}) collective-permute-start(bf16[384,768]{1,0:T(8,128)(2,1)S(1)} %copy-done.21), channel_id=1, source_target_pairs={{0,2},{1,3},{2,0},{3,1},{4,6},{5,7},{6,4},{7,5},{8,10},{9,11},{10,... | collective-permute-start | bytes 1769480 | tf_op jit(solution)/shard_map/ppermute | solution.py:757
  32.7 6.7 %collective-permute-start.1 = (f32[136,384]{1,0:T(8,128)S(1)}, f32[136,384]{1,0:T(8,128)S(1)}, u32[]{:S(2)}, u32[]{:S(2)}) collective-permute-start(f32[136,384]{1,0:T(8,128)S(1)} %get-tuple-element.141.refs_1_), channel_id=1, source_target_pairs={{0,4},{4,0},{8,12},{12,8},{16,20},{20,16},{24,28},{28,24},{1,5},{5... | collective-permute-start | bytes 626696 | tf_op jit(solution)/shard_map/ppermute | solution.py:757
  34.3 26.0 %collective-permute-start.5 = (bf16[384,768]{1,0:T(8,128)(2,1)S(1)}, bf16[384,768]{1,0:T(8,128)(2,1)S(1)}, u32[]{:S(2)}, u32[]{:S(2)}) collective-permute-start(bf16[384,768]{1,0:T(8,128)(2,1)S(1)} %copy-done.21), channel_id=1, source_target_pairs={{0,1},{1,0},{2,3},{3,2},{4,5},{5,4},{6,7},{7,6},{8,9},{9,8},{10,11... | collective-permute-start | bytes 1769480 | tf_op jit(solution)/shard_map/ppermute | solution.py:757
  40.0 6.2 %collective-permute-start.2 = (f32[136,384]{1,0:T(8,128)S(1)}, f32[136,384]{1,0:T(8,128)S(1)}, u32[]{:S(2)}, u32[]{:S(2)}) collective-permute-start(f32[136,384]{1,0:T(8,128)S(1)} %get-tuple-element.142.refs_1_), channel_id=1, source_target_pairs={{0,8},{4,12},{8,0},{12,4},{16,24},{20,28},{24,16},{28,20},{1,9},{5... | collective-permute-start | bytes 626696 | tf_op jit(solution)/shard_map/ppermute | solution.py:757
  41.6 18.6 %collective-permute-start.6 = (bf16[384,768]{1,0:T(8,128)(2,1)S(1)}, bf16[384,768]{1,0:T(8,128)(2,1)S(1)}, u32[]{:S(2)}, u32[]{:S(2)}) collective-permute-start(bf16[384,768]{1,0:T(8,128)(2,1)S(1)} %collective-permute-done.4.refs_6_), channel_id=1, source_target_pairs={{0,1},{1,0},{2,3},{3,2},{4,5},{5,4},{6,7},{7,6},{8,9},{9,8},{10,11... | collective-permute-start | bytes 1769480 | tf_op jit(solution)/shard_map/ppermute | solution.py:757
  46.8 12.9 %collective-permute-start.3 = (f32[136,384]{1,0:T(8,128)S(1)}, f32[136,384]{1,0:T(8,128)S(1)}, u32[]{:S(2)}, u32[]{:S(2)}) collective-permute-start(f32[136,384]{1,0:T(8,128)S(1)} %get-tuple-element.144.refs_1_), channel_id=1, source_target_pairs={{0,16},{4,20},{8,24},{12,28},{16,0},{20,4},{24,8},{28,12},{1,17},{... | collective-permute-start | bytes 626696 | tf_op jit(solution)/shard_map/ppermute | solution.py:757
  79.0 8.6 %collective-permute-start.10 = (f32[136,384]{1,0:T(8,128)S(1)}, f32[136,384]{1,0:T(8,128)S(1)}, u32[]{:S(2)}, u32[]{:S(2)}) collective-permute-start(f32[136,384]{1,0:T(8,128)S(1)} %get-tuple-element.170.refs_1_), channel_id=1, source_target_pairs={{0,4},{4,0},{8,12},{12,8},{16,20},{20,16},{24,28},{28,24},{1,5},{5... | collective-permute-start | bytes 626696 | tf_op jit(solution)/shard_map/ppermute | solution.py:757
  88.1 6.2 %collective-permute-start.11 = (f32[136,384]{1,0:T(8,128)S(1)}, f32[136,384]{1,0:T(8,128)S(1)}, u32[]{:S(2)}, u32[]{:S(2)}) collective-permute-start(f32[136,384]{1,0:T(8,128)S(1)} %get-tuple-element.172.refs_1_), channel_id=1, source_target_pairs={{0,8},{4,12},{8,0},{12,4},{16,24},{20,28},{24,16},{28,20},{1,9},{5... | collective-permute-start | bytes 626696 | tf_op jit(solution)/shard_map/ppermute | solution.py:757
  88.2 51.0 %collective-permute-start.17 = (bf16[2048,384]{1,0:T(8,128)(2,1)}, bf16[2048,384]{1,0:T(8,128)(2,1)}, u32[]{:S(2)}, u32[]{:S(2)}) collective-permute-start(bf16[2048,384]{1,0:T(8,128)(2,1)} %get-tuple-element.226.refs_1_), channel_id=1, source_target_pairs={{0,2},{1,3},{2,0},{3,1},{4,6},{5,7},{6,4},{7,5},{8,10},{9,11},{10,... | collective-permute-start | bytes 4718600 | tf_op jit(solution)/shard_map/ppermute | solution.py:757
  88.8 26.8 %collective-permute-start.13 = (f32[4,576,128]{2,1,0:T(8,128)S(1)}, f32[4,576,128]{2,1,0:T(8,128)S(1)}, u32[]{:S(2)}, u32[]{:S(2)}) collective-permute-start(f32[4,576,128]{2,1,0:T(8,128)S(1)} %get-tuple-element.179), channel_id=1, source_target_pairs={{0,4},{4,0},{8,12},{12,8},{16,20},{20,16},{24,28},{28,24},{1,5},{5... | collective-permute-start | bytes 3538952 | tf_op jit(solution)/shard_map/ppermute | solution.py:757
  94.9 14.3 %collective-permute-start.12 = (f32[136,384]{1,0:T(8,128)S(1)}, f32[136,384]{1,0:T(8,128)S(1)}, u32[]{:S(2)}, u32[]{:S(2)}) collective-permute-start(f32[136,384]{1,0:T(8,128)S(1)} %get-tuple-element.174.refs_1_), channel_id=1, source_target_pairs={{0,16},{4,20},{8,24},{12,28},{16,0},{20,4},{24,8},{28,12},{1,17},{... | collective-permute-start | bytes 626696 | tf_op jit(solution)/shard_map/ppermute | solution.py:757
  112.8 26.4 %collective-permute-start.18 = (f32[8,640]{1,0:T(8,128)S(1)}, f32[8,640]{1,0:T(8,128)S(1)}, u32[]{:S(2)}, u32[]{:S(2)}) collective-permute-start(f32[8,640]{1,0:T(8,128)S(1)} %get-tuple-element.176), channel_id=1, source_target_pairs={{4,0},{8,4},{12,8},{16,12},{20,16},{24,20},{28,24},{5,1},{9,5},{13... | collective-permute-start | bytes 61448 | tf_op jit(solution)/shard_map/ppermute | solution.py:1034
  116.3 18.4 %collective-permute-start.14 = (bf16[576,128]{1,0:T(8,128)(2,1)S(1)}, bf16[576,128]{1,0:T(8,128)(2,1)S(1)}, u32[]{:S(2)}, u32[]{:S(2)}) collective-permute-start(bf16[576,128]{1,0:T(8,128)(2,1)S(1)} %get-tuple-element.187), channel_id=1, source_target_pairs={{0,8},{4,12},{8,0},{12,4},{16,24},{20,28},{24,16},{28,20},{1,9},{5... | collective-permute-start | bytes 442376 | tf_op jit(solution)/shard_map/ppermute | solution.py:757
  118.1 16.5 %collective-permute-start.15 = (bf16[576,128]{1,0:T(8,128)(2,1)S(1)}, bf16[576,128]{1,0:T(8,128)(2,1)S(1)}, u32[]{:S(2)}, u32[]{:S(2)}) collective-permute-start(bf16[576,128]{1,0:T(8,128)(2,1)S(1)} %get-tuple-element.189), channel_id=1, source_target_pairs={{0,16},{4,20},{8,24},{12,28},{16,0},{20,4},{24,8},{28,12},{1,17},{... | collective-permute-start | bytes 442376 | tf_op jit(solution)/shard_map/ppermute | solution.py:757
  119.5 15.1 %collective-permute-start.16 = (bf16[576,128]{1,0:T(8,128)(2,1)S(1)}, bf16[576,128]{1,0:T(8,128)(2,1)S(1)}, u32[]{:S(2)}, u32[]{:S(2)}) collective-permute-start(bf16[576,128]{1,0:T(8,128)(2,1)S(1)} %get-tuple-element.191), channel_id=1, source_target_pairs={{0,24},{4,28},{8,16},{12,20},{16,8},{20,12},{24,0},{28,4},{1,25},{... | collective-permute-start | bytes 442376 | tf_op jit(solution)/shard_map/ppermute | solution.py:757
  134.7 19.6 %collective-permute-start.21 = (bf16[576,128]{1,0:T(8,128)(2,1)S(1)}, bf16[576,128]{1,0:T(8,128)(2,1)S(1)}, u32[]{:S(2)}, u32[]{:S(2)}) collective-permute-start(bf16[576,128]{1,0:T(8,128)(2,1)S(1)} %reduce.3.refs_1_), channel_id=1, source_target_pairs={{0,24},{4,28},{8,16},{12,20},{16,8},{20,12},{24,0},{28,4},{1,25},{... | collective-permute-start | bytes 442376 | tf_op jit(solution)/shard_map/ppermute | solution.py:757
  137.4 16.9 %collective-permute-start.20 = (bf16[576,128]{1,0:T(8,128)(2,1)S(1)}, bf16[576,128]{1,0:T(8,128)(2,1)S(1)}, u32[]{:S(2)}, u32[]{:S(2)}) collective-permute-start(bf16[576,128]{1,0:T(8,128)(2,1)S(1)} %reduce.3.refs_1_), channel_id=1, source_target_pairs={{0,16},{4,20},{8,24},{12,28},{16,0},{20,4},{24,8},{28,12},{1,17},{... | collective-permute-start | bytes 442376 | tf_op jit(solution)/shard_map/ppermute | solution.py:757
  137.4 16.9 %collective-permute-start.19 = (bf16[576,128]{1,0:T(8,128)(2,1)S(1)}, bf16[576,128]{1,0:T(8,128)(2,1)S(1)}, u32[]{:S(2)}, u32[]{:S(2)}) collective-permute-start(bf16[576,128]{1,0:T(8,128)(2,1)S(1)} %reduce.3.refs_1_), channel_id=1, source_target_pairs={{0,8},{4,12},{8,0},{12,4},{16,24},{20,28},{24,16},{28,20},{1,9},{5... | collective-permute-start | bytes 442376 | tf_op jit(solution)/shard_map/ppermute | solution.py:757
  157.4 5.3 %collective-permute-start.25 = (f32[512,768]{1,0:T(8,128)S(1)}, f32[512,768]{1,0:T(8,128)S(1)}, u32[]{:S(2)}, u32[]{:S(2)}) collective-permute-start(f32[512,768]{1,0:T(8,128)S(1)} %get-tuple-element.214), channel_id=1, source_target_pairs={{0,1},{1,0},{2,3},{3,2},{4,5},{5,4},{6,7},{7,6},{8,9},{9,8},{10,11... | collective-permute-start | bytes 4718600 | tf_op jit(solution)/shard_map/ppermute | solution.py:757
  161.1 8.0 %collective-permute-start.23 = (f32[448,128]{1,0:T(8,128)S(1)}, f32[448,128]{1,0:T(8,128)S(1)}, u32[]{:S(2)}, u32[]{:S(2)}) collective-permute-start(f32[448,128]{1,0:T(8,128)S(1)} %get-tuple-element.217), channel_id=1, source_target_pairs={{0,2},{1,3},{2,0},{3,1},{4,6},{5,7},{6,4},{7,5},{8,10},{9,11},{10,... | collective-permute-start | bytes 688136 | tf_op jit(solution)/shard_map/ppermute | solution.py:757
  170.1 8.7 %collective-permute-start.26 = (bf16[2048,384]{1,0:T(8,128)(2,1)}, bf16[2048,384]{1,0:T(8,128)(2,1)}, u32[]{:S(2)}, u32[]{:S(2)}) collective-permute-start(bf16[2048,384]{1,0:T(8,128)(2,1)} %get-tuple-element.226.refs_1_), channel_id=1, source_target_pairs={{0,1},{1,0},{2,3},{3,2},{4,5},{5,4},{6,7},{7,6},{8,9},{9,8},{10,11... | collective-permute-start | bytes 4718600 | tf_op jit(solution)/shard_map/ppermute | solution.py:757
  170.1 8.7 %collective-permute-start.27 = (bf16[2048,384]{1,0:T(8,128)(2,1)}, bf16[2048,384]{1,0:T(8,128)(2,1)}, u32[]{:S(2)}, u32[]{:S(2)}) collective-permute-start(bf16[2048,384]{1,0:T(8,128)(2,1)} %collective-permute-done.17.refs_2_), channel_id=1, source_target_pairs={{0,1},{1,0},{2,3},{3,2},{4,5},{5,4},{6,7},{7,6},{8,9},{9,8},{10,11... | collective-permute-start | bytes 4718600 | tf_op jit(solution)/shard_map/ppermute | solution.py:757
  170.6 29.5 %all-to-all-start = ((bf16[8,416,128]{2,1,0:T(8,128)(2,1)}), bf16[8,416,128]{2,1,0:T(8,128)(2,1)}, u32[]{:S(2)}, u32[]{:S(2)}) async-start(bf16[8,416,128]{2,1,0:T(8,128)(2,1)} %copy-done.10), calls=%async_computation | async-start | bytes 1703936 | tf_op jit(solution)/shard_map/all_to_all | solution.py:824
  174.9 24.4 %collective-permute-start.31 = (bf16[4,576,128]{2,1,0:T(8,128)(2,1)}, bf16[4,576,128]{2,1,0:T(8,128)(2,1)S(1)}, u32[]{:S(2)}, u32[]{:S(2)}) collective-permute-start(bf16[4,576,128]{2,1,0:T(8,128)(2,1)} %copy-done.6), channel_id=1, source_target_pairs={{0,4},{4,0},{8,12},{12,8},{16,20},{20,16},{24,28},{28,24},{1,5},{5... | collective-permute-start | bytes 1769480 | tf_op jit(solution)/shard_map/ppermute | solution.py:757
  176.8 36.1 %collective-permute-start.28 = (bf16[512,768]{1,0:T(8,128)(2,1)}, bf16[512,768]{1,0:T(8,128)(2,1)}, u32[]{:S(2)}, u32[]{:S(2)}) collective-permute-start(bf16[512,768]{1,0:T(8,128)(2,1)} %copy-done.16), channel_id=1, source_target_pairs={{0,2},{1,3},{2,0},{3,1},{4,6},{5,7},{6,4},{7,5},{8,10},{9,11},{10,... | collective-permute-start | bytes 2359304 | tf_op jit(solution)/shard_map/ppermute | solution.py:757
  178.3 34.5 %collective-permute-start.29 = (bf16[512,768]{1,0:T(8,128)(2,1)}, bf16[512,768]{1,0:T(8,128)(2,1)}, u32[]{:S(2)}, u32[]{:S(2)}) collective-permute-start(bf16[512,768]{1,0:T(8,128)(2,1)} %copy-done.18), channel_id=1, source_target_pairs={{0,2},{1,3},{2,0},{3,1},{4,6},{5,7},{6,4},{7,5},{8,10},{9,11},{10,... | collective-permute-start | bytes 2359304 | tf_op jit(solution)/shard_map/ppermute | solution.py:757
  202.3 26.4 %all-to-all-start.1 = ((bf16[8,416,128]{2,1,0:T(8,128)(2,1)}), bf16[8,416,128]{2,1,0:T(8,128)(2,1)}, u32[]{:S(2)}, u32[]{:S(2)}) async-start(bf16[8,416,128]{2,1,0:T(8,128)(2,1)} %copy-done.9), calls=%async_computation.1 | async-start | bytes 1703936 | tf_op jit(solution)/shard_map/all_to_all | solution.py:824
  206.9 6.5 %collective-permute-start.30 = (bf16[512,768]{1,0:T(8,128)(2,1)}, bf16[512,768]{1,0:T(8,128)(2,1)S(1)}, u32[]{:S(2)}, u32[]{:S(2)}) collective-permute-start(bf16[512,768]{1,0:T(8,128)(2,1)} %copy-done.16), channel_id=1, source_target_pairs={{0,1},{1,0},{2,3},{3,2},{4,5},{5,4},{6,7},{7,6},{8,9},{9,8},{10,11... | collective-permute-start | bytes 2359304 | tf_op jit(solution)/shard_map/ppermute | solution.py:757
  206.9 6.4 %collective-permute-start.33 = (bf16[512,768]{1,0:T(8,128)(2,1)}, bf16[512,768]{1,0:T(8,128)(2,1)S(1)}, u32[]{:S(2)}, u32[]{:S(2)}) collective-permute-start(bf16[512,768]{1,0:T(8,128)(2,1)} %copy-done.18), channel_id=1, source_target_pairs={{0,1},{1,0},{2,3},{3,2},{4,5},{5,4},{6,7},{7,6},{8,9},{9,8},{10,11... | collective-permute-start | bytes 2359304 | tf_op jit(solution)/shard_map/ppermute | solution.py:757
  229.9 8.8 %collective-permute-start.36 = (f32[456,128]{1,0:T(8,128)S(1)}, f32[456,128]{1,0:T(8,128)S(1)}, u32[]{:S(2)}, u32[]{:S(2)}) collective-permute-start(f32[456,128]{1,0:T(8,128)S(1)} %quarter.1.refs_1_), channel_id=1, source_target_pairs={{0,2},{1,3},{2,0},{3,1},{4,6},{5,7},{6,4},{7,5},{8,10},{9,11},{10,... | collective-permute-start | bytes 700424 | tf_op jit(solution)/shard_map/ppermute | solution.py:757
  231.5 11.5 %collective-permute-start.37 = (f32[456,128]{1,0:T(8,128)S(1)}, f32[456,128]{1,0:T(8,128)S(1)}, u32[]{:S(2)}, u32[]{:S(2)}) collective-permute-start(f32[456,128]{1,0:T(8,128)S(1)} %collective-permute-done.35.refs_2_), channel_id=1, source_target_pairs={{0,2},{1,3},{2,0},{3,1},{4,6},{5,7},{6,4},{7,5},{8,10},{9,11},{10,... | collective-permute-start | bytes 700424 | tf_op jit(solution)/shard_map/ppermute | solution.py:757
  (46 other events, 345.6 us)

commit v3 on v2

--- a/solution.py
+++ b/solution.py
@@ -101,28 +101,21 @@
     return lax.rsqrt(jnp.mean(u * u, axis=1, keepdims=True) + EPS)
 
 
-def k_project(hid, gain, w_x, w_bc, w_dt, hp, h_o, v_o, pre_o):
-    width = w_x.shape[1]
-    u = hid[...].astype(F32)
-    h = (u * rms_inv(u) * gain[...]).astype(BF16)
-    h_o[...] = h
-    v_o[:, :width] = mm(h, w_x[...])
-    v_o[:, width:] = mm(h, w_bc[...])
-    pre_o[...] = mm(h, w_dt[...]) + hp[0:1, :]
-
-
-def k_conv(
-    first, valid, v, pre, rim, gain, w_x, w_bc, hp, cx, cb,
-    cv_o, xs_o, bc_o, dt_o, cum_o, ent_o, pd_o, fin_o,
+def k_front(
+    first, valid, hid, rim, gain, w_x, w_bc, w_dt, hp, cx, cb,
+    h_o, v_o, pre_o, prev_o, lead_o, xs_o, bc_o, dt_o, cum_o, ent_o, pd_o, fin_o,
     vbuf, state, decay,
 ):
     g = pl.program_id(0)
     width = w_x.shape[1]
 
+    def normed(block):
+        u = block.astype(F32)
+        return (u * rms_inv(u) * gain[...]).astype(BF16)
+
     @pl.when(g == 0)
     def _():
-        u = rim[...].astype(F32)
-        hr = (u * rms_inv(u) * gain[...]).astype(BF16)
+        hr = normed(rim[...])
         vbuf[0:8, :width] = mm(hr, w_x[...])[8:16]
         vbuf[0:8, width:] = mm(hr, w_bc[...])[8:16]
         state[...] = jnp.zeros_like(state)
@@ -132,17 +125,23 @@
     vbuf[0:8, :] = vbuf[0:8, :] * keep
     state[...] = state[...] * keep
     decay[...] = decay[...] * keep
-    vbuf[8:, :] = v[...]
+    h = normed(hid[...])
+    h_o[...] = h
+    raw = mm(h, w_dt[...]) + hp[0:1, :]
+    pre_o[...] = raw
+    vbuf[8:, :width] = mm(h, w_x[...])
+    vbuf[8:, width:] = mm(h, w_bc[...])
+    v_o[...] = vbuf[8:, :]
     taps = jnp.concatenate([cx[...], cb[...]], axis=1)
     conv = taps[KCONV : KCONV + 1, :] + taps[0:1, :] * vbuf[5 : 5 + GROUP, :]
     for k in range(1, KCONV):
         conv = conv + taps[k : k + 1, :] * vbuf[5 + k : 5 + k + GROUP, :]
-    cv_o[...] = conv
+    prev_o[0] = vbuf[0:8, :]
+    lead_o[0] = conv[0:16, :]
     act = (conv * jax.nn.sigmoid(conv)).astype(BF16)
     xs_o[...] = act[:, :width]
     bc_o[...] = act[:, width:]
     vbuf[0:8, :] = vbuf[GROUP : GROUP + 8, :]
-    raw = pre[...]
     live = iota((GROUP, LANES), 0) < valid[g]
     soft = jnp.maximum(raw, 0.0) + jnp.log1p(jnp.exp(-jnp.abs(raw)))
     dt = jnp.where(live, soft, 0.0)
@@ -170,18 +169,22 @@
         fin_o[N:, :] = decay[...]
 
 
-def k_proj(h, og, w_z, w_out, z_o, gyn_o):
-    z_o[...] = mm(h[...], w_z[...])
+def k_proj(h, og, w_z, w_out, silu_o, slope_o, gyn_o):
+    z = mm(h[...], w_z[...])
+    sig = jax.nn.sigmoid(z)
+    silu_o[...] = z * sig
+    slope_o[...] = sig * (1.0 + z * (1.0 - sig))
     gyn_o[...] = mm(og[...], w_out[...], 1, 1)
 
 
-def k_within(xs, bc, dt, cum, y_o):
+def k_within(xs, bc, dt, cum, y_o, ecum_o):
     width = xs.shape[1]
     mask = tri("le")
     for c in range(PARTS):
         rows = slice(c * CHUNK, (c + 1) * CHUNK)
         scores = mm(bc[rows, N:], bc[rows, :N], 1, 1)
         a = cum[rows, :]
+        ecum_o[rows, :] = spread(jnp.exp(a), width)
         b = jnp.transpose(a - jnp.log(dt[rows, :]))
         for p in range(width // LANES):
             lanes = slice(p * LANES, (p + 1) * LANES)
@@ -192,17 +195,16 @@
             y_o[rows, lanes] = mm_left(jnp.concatenate(weights, axis=1), pair_rows(xs[rows, lanes]))
 
 
-def k_gate(ent, pd, prev, bc, cum, yw, xs, z, gyn, gain, hp, mix_o, ent_o, sums_o):
+def k_gate(ent, pd, prev, bc, ecum, yw, xs, silu, gyn, gain, hp, mix_o, ent_o, sums_o):
     width = xs.shape[1]
     skip = spread(hp[2:3, :], width)
     for c in range(PARTS):
         rows = slice(c * CHUNK, (c + 1) * CHUNK)
         entry = ent[c] + pd[c] * prev[0:N, :]
         ent_o[c] = entry
-        across = mm_right(bc[rows, N:], entry) * spread(jnp.exp(cum[rows, :]), width)
+        across = mm_right(bc[rows, N:], entry) * ecum[rows, :]
         mix_o[rows, :] = yw[rows, :] + across + skip * xs[rows, :].astype(F32)
-    zz = z[...]
-    gated = mix_o[...] * (zz * jax.nn.sigmoid(zz))
+    gated = mix_o[...] * silu[...]
     square = jnp.sum(gated * gated, axis=1, keepdims=True)
     inner = jnp.sum(gyn[...] * gain[...] * gated, axis=1, keepdims=True)
     lane = iota((GROUP, LANES), 1)
@@ -211,7 +213,7 @@
 
 
 def k_gate_back(
-    total, count, first, mix, z, gyn, gain, xs, bc, cum, *rest,
+    total, count, first, mix, silu, slope, gyn, gain, xs, bc, ecum, *rest,
 ):
     sums = rest[:count]
     yn_o, g_o, gz_o, ds_o, qd_o, again_o, askip_o, fin_o, state, decay = rest[count:]
@@ -230,9 +232,7 @@
     both = jnp.transpose(jnp.concatenate([rows2, jnp.zeros((LANES - 2, GROUP), F32)], axis=0))
     inv = lax.rsqrt(both[:, 0:1] / total + EPS)
     inner = both[:, 1:2] / total
-    zz = z[...]
-    sig = jax.nn.sigmoid(zz)
-    silu = zz * sig
+    silu = silu[...]
     mixer = mix[...]
     gated = mixer * silu
     scaled = gated * inv
@@ -243,16 +243,15 @@
     gg = inv * gn * gy - gated * (inv * inv * inv * inner)
     gm = (gg * silu).astype(BF16)
     g_o[...] = gm
-    gz_o[...] = (gg * mixer * sig * (1.0 + zz * (1.0 - sig))).astype(BF16)
+    gz_o[...] = (gg * mixer * slope[...]).astype(BF16)
     gmf = gm.astype(F32)
     askip_o[...] += fold_rows(gmf * xs[...].astype(F32))
     for c in reversed(range(PARTS)):
         rows = slice(c * CHUNK, (c + 1) * CHUNK)
-        ecum = spread(jnp.exp(cum[rows, :]), width)
         ds_o[c] = state[...]
         qd_o[c] = decay[0:1]
-        new = mm_right(bc[rows, N:], gmf[rows] * ecum, 0, 0)
-        ec = ecum[CHUNK - 1 : CHUNK, :]
+        new = mm_right(bc[rows, N:], gmf[rows] * ecum[rows, :], 0, 0)
+        ec = ecum[(c + 1) * CHUNK - 1 : (c + 1) * CHUNK, :]
         state[...] = state[...] * ec + new
         decay[...] = decay[...] * ec
     keep = 1.0 - first[g].astype(F32)
@@ -357,7 +356,7 @@
     xd = xs[...].astype(F32) * factor
     gx = dxw[...] + factor * mm_right(bc[:, :N], d_state) + g[...].astype(F32) * skip
     gb = dbc[:, :N] + mm_both(xd, d_state, 1, 1)
-    slope = silu_slope(cv[...]) * (1.0 - first[i].astype(F32))
+    slope = silu_slope(cv[0]) * (1.0 - first[i].astype(F32))
     out[0, :, :width] = gx * slope[:, :width]
     out[0, :, width : width + N] = gb * slope[:, width : width + N]
     out[0, :, width + N :] = dbc[:, N:] * slope[:, width + N :]
@@ -367,17 +366,17 @@
         lead_o[...] = out[0, 0:8, :]
 
 
-def k_back(final, place, *refs):
+def k_back(final, slots, place, *refs):
     (
-        valid, h, xs, bc, g, pre, dt, cum, v, cv, dxw, dbc, rq, qw, ent, ds, qd, endg, rims, cx, cb, hp,
+        valid, h, xs, bc, g, pre, dt, cum, v, vprev, dxw, dbc, rq, qw, ent, ds, qd, endg, rims, cx, cb, hp,
     ) = refs[:22]
     if final:
         rim_in, acc_gain, acc_skip = refs[22:25]
         gx_o, gbc_o, gpre_o = refs[33:36]
         acc_x, acc_bc, acc_dt, acc_taps, acc_heads = refs[36:41]
-        grads_o, keep_o, send_o, gbuf, small_o = refs[41:]
+        grads_o, keep_o, send_o, gbuf, vbuf, small_o = refs[41:]
     else:
-        gx_o, gbc_o, gpre_o, acc_x, acc_bc, acc_dt, acc_taps, acc_heads, gbuf = refs[22:]
+        gx_o, gbc_o, gpre_o, acc_x, acc_bc, acc_dt, acc_taps, acc_heads, gbuf, vbuf = refs[22:]
     i = pl.program_id(0)
     last = pl.num_programs(0) - 1
     group = i + pl.num_programs(0) if final else i
@@ -395,6 +394,9 @@
 
     upper, below = tri("ge").astype(BF16), tri("lt").astype(BF16)
     both = jnp.concatenate([upper, upper, below, below], axis=1)
+    taps = jnp.concatenate([cx[...], cb[...]], axis=1)
+    vbuf[0:8, :] = vprev[0]
+    vbuf[8:, :] = v[...]
     for c in range(PARTS):
         rows = slice(c * CHUNK, (c + 1) * CHUNK)
         d_state = ds[c] + qd[c] * endg[0:N, :]
@@ -408,7 +410,11 @@
         x_high, x_low = split2(xf * factor)
         gb = dbc[rows, :N] + (mm(x_high, d_high, 1, 1) + mm(x_low, d_high, 1, 1) + mm(x_high, d_low, 1, 1))
         gx = dxw[rows, :] + dxs + g[rows, :].astype(F32) * skip
-        slope = silu_slope(cv[rows, :])
+        conv = taps[KCONV : KCONV + 1, :]
+        for k in range(KCONV):
+            start = 5 + k + c * CHUNK
+            conv = conv + taps[k : k + 1, :] * vbuf[start : start + CHUNK, :]
+        slope = silu_slope(conv)
         gbuf[rows, :width] = gx * slope[:, :width]
         gbuf[rows, width : width + N] = gb * slope[:, width : width + N]
         gbuf[rows, width + N :] = dbc[rows, N:] * slope[:, width + N :]
@@ -436,7 +442,6 @@
         def _():
             gbuf[GROUP:, :] = rim_in[0:8, :]
 
-    taps = jnp.concatenate([cx[...], cb[...]], axis=1)
     vv = v[...]
     gv = jnp.zeros_like(vv)
     for k in range(KCONV):
@@ -471,6 +476,9 @@
 
         put(acc_bc[:, :LANES])
         put(acc_bc[:, LANES:])
+        count, each, rest = slots
+        if at < count * each:
+            put(jnp.zeros((count * each - at, LANES), F32))
         put(stacked(acc_dt[...]))
 
         def line(value):
@@ -504,9 +512,13 @@
             axis=0,
         )
         small_o[pl.ds(pl.multiple_of(at + place[2] * (8 * tiles), 8), 8 * tiles), :] = own_rows
-        rows = keep_o.shape[0]
-        keep_o[...] = small_o[pl.ds(pl.multiple_of(place[0] * rows, 8), rows), :]
-        send_o[...] = small_o[pl.ds(pl.multiple_of((1 - place[0]) * rows, 8), rows), :]
+        for k in range(count // 2):
+            for out, side in ((keep_o, place[0]), (send_o, 1 - place[0])):
+                slot = side * (count // 2) + k
+                to = k * (each + rest)
+                out[to : to + each, :] = small_o[pl.ds(pl.multiple_of(slot * each, 8), each), :]
+                start = pl.multiple_of(count * each + slot * rest, 8)
+                out[to + each : to + each + rest, :] = small_o[pl.ds(start, rest), :]
 
 
 def input_grad(hid, gz, gx, gbc, gpre, w_z, w_x, w_bc, w_dt):
@@ -556,17 +568,20 @@
         out[...] = kept[pl.ds(at, rows), :] + arrived[pl.ds(at, rows), :]
 
 
-def k_pieces(kept, arrived, norm, large, out):
+def k_pieces(slots, kept, arrived, norm, large, out):
     count = out.shape[0]
-    rows = kept.shape[0] // count
+    _, each, rest = slots
+    rows = each + rest
     cut = large.shape[1]
     spare = jnp.zeros((7, LANES), F32)
     for k in range(count):
         own = slice(k * rows, (k + 1) * rows)
+        value = kept[own, :] + arrived[own, :]
         line = norm[k : k + 1, :] if k < 8 else spare[0:1]
-        small = jnp.concatenate([kept[own, :] + arrived[own, :], line, spare], axis=0)
+        small = jnp.concatenate([value[each:], line, spare], axis=0)
         out[k, 0:cut, :] = large[k]
-        out[k, cut:, :] = jnp.concatenate(split2(small), axis=0)
+        out[k, cut : cut + each, :] = value[:each].astype(BF16)
+        out[k, cut + each :, :] = jnp.concatenate(split2(small), axis=0)
 
 
 def k_reduce_both(cut, parts, out):
@@ -580,14 +595,20 @@
         out[k] = joined
 
 
-def k_quarter(cut, parts, out):
+def k_tick(value, out):
+    out[...] = value[0, 0:16, :]
+
+
+def k_quarter(cut, slots, parts, out):
     count = parts.shape[0]
-    rows = out.shape[0] // count - 1
+    _, each, rest = slots
+    rows = each + rest
     for k in range(count):
         value = parts[k, cut:, :].astype(F32)
-        value = value[: rows + 8] + value[rows + 8 :]
-        out[k * rows : (k + 1) * rows, :] = value[:rows]
-        out[count * rows + k : count * rows + k + 1, :] = value[rows : rows + 1]
+        small = value[each : each + rest + 8] + value[each + rest + 8 :]
+        out[k * rows : k * rows + each, :] = value[:each]
+        out[k * rows + each : (k + 1) * rows, :] = small[:rest]
+        out[count * rows + k : count * rows + k + 1, :] = small[rest : rest + 1]
 
 
 def unstack(value, rows):
@@ -622,24 +643,29 @@
         w_zx_o[k * rz : (k + 1) * rz, 1, :] = own
 
 
-def k_small(place, *refs):
+def k_small(slots, place, *refs):
     count = len(refs) - 10
     w_bc_o, w_dt_o, bc_taps_o, bias_o, alog_o, skip_o, norm_o, taps_o, gain_o, buf = refs[count:]
-    quarter = buf.shape[0] // count
+    total, each, rest = slots
+    steps = total // count
     norms = []
     for k in range(count):
         from_head, at = place[2] ^ k, 0
         for mask in powers(count):
             at = 2 * at + (from_head // mask) % 2
-        buf[pl.ds(pl.multiple_of(at * quarter, 8), quarter), :] = refs[k][0:quarter, :]
-        norms.append(refs[k][quarter : quarter + 8, :])
+        for t in range(steps):
+            slot = at * steps + t
+            value = refs[k][t * (each + rest) : (t + 1) * (each + rest), :]
+            buf[pl.ds(pl.multiple_of(slot * each, 8), each), :] = value[:each]
+            buf[pl.ds(pl.multiple_of(total * each + slot * rest, 8), rest), :] = value[each:]
+        norms.append(refs[k][steps * (each + rest) : steps * (each + rest) + 8, :])
     norm = tree(norms)
     dim = w_bc_o.shape[0]
     for k in range(dim // LANES):
         norm_o[:, k * LANES : (k + 1) * LANES] = norm[k : k + 1, :]
     w_bc_o[:, :LANES] = buf[0:dim, :]
     w_bc_o[:, LANES:] = buf[dim : 2 * dim, :]
-    at = 2 * dim
+    at = total * each
     heads = w_dt_o.shape[0]
     w_dt_o[...] = unstack(buf[at : at + heads * dim // LANES, :], heads)
     at += heads * dim // LANES
@@ -858,8 +884,7 @@
 
     route = [(i - 1, i) for i in range(1, tok_count)]
     rim = lax.ppermute(hidden_in[tokens - 16 :], "tok", route)
-    w_z = wide(w_zx[:, 0], 1)
-    w_x = wide(w_zx[:, 1], 1)
+    flat_zx = wide(w_zx, 2).reshape(dim, 2 * width)
     w_o = wide(w_out, 0)
     w_dt_here = wide(lax.dynamic_slice_in_dim(w_dt, head_start, own_heads, 1), 1, LANES - own_heads)
     per_head = jnp.stack([dt_bias, a_log, d_skip])
@@ -870,9 +895,12 @@
     gain_gate = wide(gate_gain, 0)[None, :]
     at_head = lax.axis_index("head")
     place = jnp.stack([at_head & 1, head_start, at_head, lax.axis_index("tok")]).astype(jnp.int32)
-    hidden_in, place, w_z, w_x, w_o, w_dt_here, per_head, cx, gain_in, gain_gate = lax.optimization_barrier(
-        (hidden_in, place, w_z, w_x, w_o, w_dt_here, per_head, cx, gain_in, gain_gate)
-    )
+    hidden_in, place, flat_zx, w_o, w_dt_here, per_head, cx, gain_in, gain_gate = lax.optimization_barrier(
+        (hidden_in, place, flat_zx, w_o, w_dt_here, per_head, cx, gain_in, gain_gate)
+    )
+    part_z, part_x = [
+        (flat_zx, pl.BlockSpec((dim, width), lambda i, *s, side=side: (0, side))) for side in range(2)
+    ]
     w_outs = head_gathered(w_o)
 
     def rows(a, at=None):
@@ -900,24 +928,16 @@
         return ((chunks,) + shape, dtype, Kept(PARTS, at))
 
     carry = (N + 8, width)
-    h, v, pre = call(
-        k_project,
-        groups,
-        [rows(hidden_in), full(gain_in), full(w_x), full(w_bc), full(w_dt_here), full(per_head)],
-        [out_kept(dim, BF16), out_kept(conv_width, F32), out_kept(LANES, F32)],
-        [],
-        4 * 10**9,
-        "project",
-    )
-    cv, xs, bc, dt, cum, ent, pd, fin = call(
-        k_conv,
+    h, v, pre, vprev, cvlead, xs, bc, dt, cum, ent, pd, fin = call(
+        k_front,
         groups,
         [
-            (group_first, SMEM), (group_valid, SMEM), kept(v), kept(pre), full(rim), full(gain_in),
-            full(w_x), full(w_bc), full(per_head), full(cx), full(conv_bc),
+            (group_first, SMEM), (group_valid, SMEM), rows(hidden_in), full(rim), full(gain_in),
+            part_x, full(w_bc), full(w_dt_here), full(per_head), full(cx), full(conv_bc),
         ],
         [
-            out_kept(conv_width, F32), out_kept(width, BF16), out_kept(2 * N, BF16),
+            out_kept(dim, BF16), out_kept(conv_width, F32), out_kept(LANES, F32),
+            ((groups, 8, conv_width), F32, Kept(1)), ((groups, 16, conv_width), F32, Kept(1)), out_kept(width, BF16), out_kept(2 * N, BF16),
             out_kept(LANES, F32), out_kept(LANES, F32), out_chunk((N, width), F32),
             out_chunk((1, width), F32), out_full(carry, F32),
         ],
@@ -926,23 +946,23 @@
             pltpu.VMEM((8, width), F32),
         ],
         4 * 10**9,
-        "conv",
+        "front",
     )
     prev, _ = carried_in(fin, False, place)
-    z, gyn = call(
+    silu, slope, gyn = call(
         k_proj,
         groups,
-        [kept(h), rows(after(out_grad, fin)), full(w_z), full(w_o)],
-        [out_kept(width, F32), out_kept(width, F32)],
+        [kept(h), rows(after(out_grad, fin)), part_z, full(w_o)],
+        [out_kept(width, F32)] * 3,
         [],
         5 * 10**9,
         "proj",
     )
-    (yw,) = call(
+    yw, ecum = call(
         k_within,
         groups,
         [kept(xs), kept(bc), kept(dt), kept(cum)],
-        [out_kept(width, F32)],
+        [out_kept(width, F32)] * 2,
         [],
         5 * 10**9,
         "within",
@@ -951,8 +971,8 @@
         k_gate,
         groups,
         [
-            per_chunk(ent), per_chunk(pd), full(after(prev, *w_outs)), kept(bc), kept(cum), kept(yw), kept(xs),
-            kept(z), kept(gyn), full(gain_gate), full(per_head),
+            per_chunk(ent), per_chunk(pd), full(after(prev, *w_outs)), kept(bc), kept(ecum), kept(yw), kept(xs),
+            kept(silu), kept(gyn), full(gain_gate), full(per_head),
         ],
         [
             out_kept(width, F32), out_chunk((N, width), F32),
@@ -971,8 +991,8 @@
         functools.partial(k_gate_back, float(heads * P_SIZE), head_count),
         groups,
         [
-            (group_first, SMEM), kept(mix, back), kept(z, back), kept(gyn, back), full(gain_gate), kept(xs, back),
-            kept(bc, back), kept(cum, back),
+            (group_first, SMEM), kept(mix, back), kept(silu, back), kept(slope, back), kept(gyn, back), full(gain_gate),
+            kept(xs, back), kept(bc, back), kept(ecum, back),
         ]
         + [(a, pl.BlockSpec((2, GROUP), lambda i: (0, groups - 1 - i))) for a in sums],
         [
@@ -1021,7 +1041,7 @@
         [
             (group_first, SMEM), leading(xs), leading(bc), leading(gm), leading(dt), leading(cum),
             (cum, Kept(8, lambda i: i * (GROUP // 8) + CHUNK // 8 - 1)),
-            leading(dxw), leading(dbc), leading(cv),
+            leading(dxw), leading(dbc), (cvlead, Kept(1)),
             (ds, Kept(1, lambda i: i * PARTS)),
             (qd, Kept(1, lambda i: i * PARTS)),
             full(end_grad), full(per_head),
@@ -1048,9 +1068,11 @@
     half = groups // 2
     piece_b = rows_z * width // LANES
     tiles = width // LANES
-    small_rows = 2 * dim + heads * dim // LANES + 16 + head_count * 8 * tiles
-    unit = head_count * tok_count * 8
-    small_rows = -(-small_rows // unit) * unit
+    count = head_count * tok_count
+    each = -(-2 * dim // (16 * count)) * 16
+    rest = -(-(heads * dim // LANES + 16 + head_count * 8 * tiles) // (8 * count)) * 8
+    slots = (count, each, rest)
+    small_rows = count * (each + rest)
     acc_shapes = [(dim, width), (dim, 2 * N), (heads, dim), (8 * KCONV + 8, conv_width), (16, LANES)]
 
     def back_call(final, more_in, more_out, more_scratch, alias, ready):
@@ -1058,12 +1080,17 @@
             return i + half if final else i
 
         return call(
-            functools.partial(k_back, final),
+            functools.partial(k_back, final, slots),
             half,
             [(group_valid, SMEM)]
             + [
                 kept(a, at)
-                for a in (after(h, *ready), xs, bc, gm, pre, dt, cum, v, cv, dxw, dbc, rq, qw)
+                for a in (after(h, *ready), xs, bc, gm, pre, dt, cum, v)
+            ]
+            + [(vprev, Kept(1, at))]
+            + [
+                kept(a, at)
+                for a in (dxw, dbc, rq, qw)
             ]
             + [per_chunk(entry, at), per_chunk(ds, at), per_chunk(qd, at), full(end_grad)]
             + [(rims, Kept(1, lambda i, s: jnp.minimum(at(i) + 1, groups - 1)))]
@@ -1072,7 +1099,7 @@
             [out_kept(width, BF16, at), out_kept(4 * N, BF16, at), out_kept(LANES, BF16, at)]
             + [(a, F32, VMEM) for a in acc_shapes]
             + more_out,
-            [pltpu.VMEM((GROUP + 8, conv_width), F32)] + more_scratch,
+            [pltpu.VMEM((GROUP + 8, conv_width), F32)] * 2 + more_scratch,
             5 * 10**9,
             "back_end" if final else "back_start",
             place,
@@ -1118,7 +1145,7 @@
             steps,
             [rows(hidden_in, turned)]
             + [kept(a, turned) for a in (gz, gx, gbc, after(gpre, *ready))]
-            + [full(a) for a in (w_z, w_x, w_bc, w_dt_here)]
+            + [part_z, part_x, full(w_bc), full(w_dt_here)]
             + [rows(a) for a in more]
             + ([] if norm is None else [full(norm)]),
             [
@@ -1152,12 +1179,11 @@
             found = found + [swap(a, "head", mask) for a in found]
         parts.append(found)
 
-    shape = (tok_count, piece_b + 2 * (small_keep.shape[0] // tok_count + 8), LANES)
+    shape = (tok_count, piece_b + each + 2 * (rest + 8), LANES)
     (pieces,) = call(
-        k_pieces, 1, [full(small_keep), full(small_arrived), full(norm), full(grads_b)],
+        functools.partial(k_pieces, slots), 1, [full(small_keep), full(small_arrived), full(norm), full(grads_b)],
         [out_full(shape, BF16)], [], 10**6, "pieces",
     )
-    other_a = swap(after(mine_a, pieces), "tok", 1)
     yns = yns + [swap(after(a, pieces), "head", 1) for a in yns]
     (block_out,) = call(
         k_out,
@@ -1170,17 +1196,21 @@
     )
 
     (copies,) = call(
-        functools.partial(k_reduce_both, piece_b), 1,
-        [full(after(exchange(pieces, "tok"), block_out, other_a))],
+        functools.partial(k_reduce_both, piece_b + each), 1,
+        [full(after(exchange(pieces, "tok"), block_out))],
         [out_full(shape, BF16)], [], 10**6, "reduce_both",
     )
     sum_b = exchange(copies, "tok")
+    other_a = swap(after(mine_a, copies), "tok", 1)
+    (tick,) = call(
+        k_tick, 1, [(copies, row_block(copies.shape, 1))], [out_full((16, LANES), BF16)], [], 1, "tick"
+    )
     (grad_w_out,) = call(
-        k_unpack_out, 1, [full(after(mine_a, copies)), full(other_a)], [out_full((width, dim), F32)],
+        k_unpack_out, 1, [full(mine_a), full(other_a)], [out_full((width, dim), F32)],
         [], 10**6, "unpack_out", place,
     )
     others = [
-        [swap(found[0], "head", 1)] + [swap(after(a, grad_w_out), "head", 1) for a in found[1:]]
+        [swap(found[0], "head", 1)] + [swap(after(a, tick), "head", 1) for a in found[1:]]
         for found in parts
     ]
 
@@ -1203,7 +1233,7 @@
     )
     shape = (small_rows // head_count + tok_count, LANES)
     (quarter,) = call(
-        functools.partial(k_quarter, piece_b), 1, [full(after(sum_b, grad_in))], [out_full(shape, F32)],
+        functools.partial(k_quarter, piece_b, slots), 1, [full(after(sum_b, grad_in))], [out_full(shape, F32)],
         [], 10**6, "quarter",
     )
     quarters = [(quarter, 0)]
@@ -1222,7 +1252,7 @@
         place,
     )
     grad_w_bc, grad_w_dt, grad_taps, grad_bias, grad_alog, grad_skip, grad_norm, own_taps, own_gain = call(
-        k_small,
+        functools.partial(k_small, slots),
         1,
         [full(a) for a in quarters],
         [

time: 247 us -> 238 us (0.964)
  local copies, waits for them, and re-layouts: 23.2 us -> 18 us
  starting transfers between devices: 48.4 us -> 45.5 us
    slice x1 -> x0, local copies, waits for them, and re-layouts: 3.71 us -> none  [on_device(): w_x = wide(w_zx[:, 1], 1)]
    ppermute x36, starting transfers between devices: 33.1 us -> 30.4 us  [swap(): lax.ppermute(value, axis, [(i, i ^ mask) for i in range(lax.axis_size(axi...]
    unnamed x77 -> x82, local copies, waits for them, and re-layouts: 17.1 us -> 15.7 us
    pallas_call x33 -> x32, Pallas kernels: 134 us -> 133 us  [call(): pl.pallas_call(body, grid_spec=pltpu.PrefetchScalarGridSpec(num_scalar_pr...]
  transfers between devices with their start and end apart: 40 -> 40, of which waited for: 13 -> 14; matrix products, arithmetic and copies ran while one was open for 3% -> 2% of each run, Pallas kernels for 47% -> 50%
where the time goes in v3:
time: 238 us; the launch traced here: 237 us
  Pallas kernels  133 us (56%)
  starting transfers between devices  45.5 us (19%)
  waiting for transfers between devices  37 us (16%)
  local copies, waits for them, and re-layouts  18 us (8%)
    pallas_call x32, Pallas kernels, call(): pl.pallas_call(body, grid_spec=pltpu.PrefetchScalarGridSpec(num_scalar_pr...  133 us
    ppermute x36, waiting for transfers between devices, swap(): lax.ppermute(value, axis, [(i, i ^ mask) for i in range(lax.axis_size(axi...  34.1 us
    ppermute x36, starting transfers between devices, swap(): lax.ppermute(value, axis, [(i, i ^ mask) for i in range(lax.axis_size(axi...  30.4 us
    unnamed x82, local copies, waits for them, and re-layouts  15.7 us
    all_to_all x2, starting transfers between devices, exchange(): return lax.all_to_all(pieces, axis, 0, 0, tiled=True)  8.64 us
    ppermute x1, starting transfers between devices, on_device(): rim = lax.ppermute(hidden_in[tokens - 16:], 'tok', route)  4.86 us
  transfers between devices with their start and end apart: 40, of which 14 were waited for; matrix products, arithmetic and copies ran while one was open for 2% of the time, Pallas kernels for 50%

profile of v3, /device:TPU:0, one launch (start us, length us, event | category | flops | bytes accessed | tf_op | source)
XLA Modules:
  0.0 236.8 jit_solution(15850332045069005363)
XLA Ops:
  1.5 4.9 %collective-permute-start = (bf16[16,768]{1,0:T(8,128)(2,1)S(1)}, bf16[16,768]{1,0:T(8,128)(2,1)S(1)}, u32[]{:S(2)}, u32[]{:S(2)}) collective-permute-start(bf16[16,768]{1,0:T(8,128)(2,1)S(1)} %slice.3), channel_id=1, source_target_pairs={{0,4},{4,8},{8,12},{12,16},{16,20},{20,24},{24,28},{1,5},{5,9},{9,... | collective-permute-start | bytes 73736 | tf_op jit(solution)/shard_map/ppermute | solution.py:886
  12.0 1.9 copy-done.2
  13.9 14.0 %front.1 = (bf16[2048,768]{1,0:T(8,128)(2,1)S(1)}, f32[2048,640]{1,0:T(8,128)S(1)}, f32[2048,128]{1,0:T(8,128)S(1)}, f32[8,8,640]{2,1,0:T(8,128)S(1)}, f32[8,16,...) custom-call(s32[8]{0:T(128)S(1)} %copy-done.16, ...), custom_call_target="tpu_custom_call" | custom-call | flops 4000000000 | bytes 22986304 | tf_op jit(solution)/shard_map/front/pallas_call | solution.py:761
  29.5 4.8 %collective-permute-done.1.refs_2_ = f32[136,384]{1,0:T(8,128)S(1)} collective-permute-done((f32[136,384]{1,0:T(8,128)S(1)}, f32[136,384]{1,0:T(8,128)S(1)}, u32[]{:S(2)}, u32[]{:S(2)}) %collective-permute-start.1) | collective-permute-done | bytes 208928 | tf_op jit(solution)/shard_map/ppermute | solution.py:783
  36.6 4.7 %proj.1 = (f32[2048,384]{1,0:T(8,128)S(1)}, f32[2048,384]{1,0:T(8,128)S(1)}, f32[2048,384]{1,0:T(8,128)S(1)}) custom-call(bf16[2048,768]{1,0:T(8,128)(2,1)S(1)} %get-tuple-element.198.refs_0_.refs_3_.refs_2_, bf16[2048,768]{1,0:T(8,128)(2,1)S(1)} %copy-done.8, bf16[768,768]{1,0:T(8,128)(2,1)S(1)} %bitcast.14, bf16[384,768]{1,0:T(8,128)(2,1)S(1)} %copy-done.20), custom_call_target="tpu_custom_call" | custom-call | flops 5000000000 | bytes 17498112 | tf_op jit(solution)/shard_map/proj/pallas_call | solution.py:761
  42.0 2.7 %collective-permute-start.3 = (f32[136,384]{1,0:T(8,128)S(1)}, f32[136,384]{1,0:T(8,128)S(1)}, u32[]{:S(2)}, u32[]{:S(2)}) collective-permute-start(f32[136,384]{1,0:T(8,128)S(1)} %get-tuple-element.144.refs_1_), channel_id=1, source_target_pairs={{0,16},{4,20},{8,24},{12,28},{16,0},{20,4},{24,8},{28,12},{1,17},{... | collective-permute-start | bytes 626696 | tf_op jit(solution)/shard_map/ppermute | solution.py:783
  44.7 6.5 %within.1 = (f32[2048,384]{1,0:T(8,128)S(1)}, f32[2048,384]{1,0:T(8,128)S(1)}) custom-call(bf16[2048,384]{1,0:T(8,128)(2,1)S(1)} %get-tuple-element.149.refs_0_.refs_6_.refs_1_.refs_3_, bf16[2048,256]{1,0:T(8,128)(2,1)S(1)} %get-tuple-element.148.refs_1_.refs_3_.refs_7_.refs_2_.refs_4_, f32[2048,128]{1,0:T(8,128)S(1)} %get-tuple-element.150.refs_2_.refs_3_.refs_4_.refs_7_, ...), custom_call_target="tpu_custom_call" | custom-call | flops 5000000000 | bytes 11010048 | tf_op jit(solution)/shard_map/within/pallas_call | solution.py:761
  51.1 3.7 %collective-permute-done.3.refs_2_ = f32[136,384]{1,0:T(8,128)S(1)} collective-permute-done((f32[136,384]{1,0:T(8,128)S(1)}, f32[136,384]{1,0:T(8,128)S(1)}, u32[]{:S(2)}, u32[]{:S(2)}) %collective-permute-start.3) | collective-permute-done | bytes 208928 | tf_op jit(solution)/shard_map/ppermute | solution.py:783
  55.5 3.8 %gate.1 = (f32[2048,384]{1,0:T(8,128)S(1)}, f32[16,128,384]{2,1,0:T(8,128)S(1)}, f32[2,2048]{1,0:T(2,128)S(1)}) custom-call(f32[16,128,384]{2,1,0:T(8,128)S(1)} %get-tuple-element.139.refs_0_, f32[16,1,384]{2,1,0:T(1,128)S(1)} %get-tuple-element.140.refs_1_, f32[136,384]{1,0:T(8,128)S(1)} %merge.8.refs_2_, ...), custom_call_target="tpu_custom_call" | custom-call | flops 3000000000 | bytes 24897024 | tf_op jit(solution)/shard_map/gate/pallas_call | solution.py:761
  63.3 7.5 %gate_back.1 = (bf16[2048,384]{1,0:T(8,128)(2,1)}, bf16[2048,384]{1,0:T(8,128)(2,1)S(1)}, bf16[2048,384]{1,0:T(8,128)(2,1)S(1)}, f32[16,128,384]{2,1,0:T(8,128)S...) custom-call(s32[8]{0:T(128)S(1)} %copy-done.16, ...), custom_call_target="tpu_custom_call" | custom-call | flops 3000000000 | bytes 26539552 | tf_op jit(solution)/shard_map/gate_back/pallas_call | solution.py:761
  72.4 7.1 %weights.1 = (f32[4,576,128]{2,1,0:T(8,128)S(1)}, f32[4,576,128]{2,1,0:T(8,128)S(1)}) custom-call(s32[4]{0:T(128)S(1)} %pad_add_fusion.refs_0_, bf16[2048,384]{1,0:T(8,128)(2,1)} %get-tuple-element.231.refs_1_, bf16[2048,768]{1,0:T(8,128)(2,1)S(1)} %copy-done.8, bf16[2048,768]{1,0:T(8,128)(2,1)S(1)} %copy-done.35, ...), custom_call_target="tpu_custom_call" | custom-call | flops 12000000000 | bytes 47185920 | tf_op jit(solution)/shard_map/weights/pallas_call | solution.py:761
  82.2 4.2 %collective-permute-done.11.refs_2_ = f32[136,384]{1,0:T(8,128)S(1)} collective-permute-done((f32[136,384]{1,0:T(8,128)S(1)}, f32[136,384]{1,0:T(8,128)S(1)}, u32[]{:S(2)}, u32[]{:S(2)}) %collective-permute-start.11) | collective-permute-done | bytes 208928 | tf_op jit(solution)/shard_map/ppermute | solution.py:783
  88.3 13.1 %within_back.1 = (f32[2048,384]{1,0:T(8,128)S(1)}, f32[2048,256]{1,0:T(8,128)S(1)}, f32[2048,128]{1,0:T(8,128)S(1)}, f32[2048,128]{1,0:T(8,128)S(1)}) custom-call(bf16[2048,384]{1,0:T(8,128)(2,1)S(1)} %get-tuple-element.149.refs_0_.refs_6_.refs_1_.refs_3_, bf16[2048,256]{1,0:T(8,128)(2,1)S(1)} %get-tuple-element.148.refs_1_.refs_3_.refs_7_.refs_2_.refs_4_, ...), custom_call_target="tpu_custom_call" | custom-call | flops 40000000000 | bytes 79708160 | tf_op jit(solution)/shard_map/within_back/pallas_call | solution.py:761
  102.1 3.0 %rim.1 = (f32[8,16,640]{2,1,0:T(8,128)S(1)}, f32[8,640]{1,0:T(8,128)S(1)}) custom-call(s32[8]{0:T(128)S(1)} %copy-done.16, bf16[2048,384]{1,0:T(8,128)(2,1)S(1)} %get-tuple-element.149.refs_0_.refs_6_.refs_1_.refs_3_, bf16[2048,256]{1,0:T(8,128)(2,1)S(1)} %get-tuple-element.148.refs_1_.refs_3_.refs_7_.refs_2_.refs_4_, ...), custom_call_target="tpu_custom_call" | custom-call | flops 1000000000 | bytes 16642080 | tf_op jit(solution)/shard_map/rim/pallas_call | solution.py:761
  113.7 12.9 %back_start.1 = (bf16[2048,384]{1,0:T(8,128)(2,1)S(1)}, bf16[2048,512]{1,0:T(8,128)(2,1)S(1)}, bf16[2048,128]{1,0:T(8,128)(2,1)S(1)}, f32[768,384]{1,0:T(8,128)S...) custom-call(s32[4]{0:T(128)S(1)} %pad_add_fusion.refs_0_, ...), custom_call_target="tpu_custom_call" | custom-call | flops 20000000000 | bytes 145787008 | tf_op jit(solution)/shard_map/back_start/pallas_call | solution.py:761
  126.8 2.4 %collective-permute-start.21 = (bf16[576,128]{1,0:T(8,128)(2,1)S(1)}, bf16[576,128]{1,0:T(8,128)(2,1)S(1)}, u32[]{:S(2)}, u32[]{:S(2)}) collective-permute-start(bf16[576,128]{1,0:T(8,128)(2,1)S(1)} %reduce.3.refs_1_), channel_id=1, source_target_pairs={{0,24},{4,28},{8,16},{12,20},{16,8},{20,12},{24,0},{28,4},{1,25},{... | collective-permute-start | bytes 442376 | tf_op jit(solution)/shard_map/ppermute | solution.py:783
  129.2 2.0 collective-permute-start.19
  131.3 15.0 %back_end.1 = (bf16[2048,384]{1,0:T(8,128)(2,1)S(1)}, bf16[2048,512]{1,0:T(8,128)(2,1)S(1)}, bf16[2048,128]{1,0:T(8,128)(2,1)S(1)}, f32[768,384]{1,0:T(8,128)S(1...) custom-call(s32[4]{0:T(128)S(1)} %pad_add_fusion.refs_0_, ...), custom_call_target="tpu_custom_call", output_to_operand_aliasing={{0}: (26, {}), {1}: (27, {}), {2}: (28, {}), {3}: (29, {}),... | custom-call | flops 20000000000 | bytes 177375360 | tf_op jit(solution)/shard_map/back_end/pallas_call | solution.py:761
  147.0 2.6 %input_sent.2 = (f32[512,768]{1,0:T(8,128)S(1)}, f32[8,768]{1,0:T(8,128)S(1)}) custom-call(s32[4]{0:T(128)S(1)} %pad_add_fusion.refs_0_, bf16[2048,768]{1,0:T(8,128)(2,1)S(1)} %copy-done.3, bf16[2048,384]{1,0:T(8,128)(2,1)S(1)} %get-tuple-element.162.refs_4_.refs_2_, bf16[2048,384]{1,0:T(8,128)(2,1)S(1)} %get-tuple-element.210.refs_3_, ...), custom_call_target="tpu_custom_call" | custom-call | flops 1000000000 | bytes 13459456 | tf_op jit(solution)/shard_map/input_sent/pallas_call | solution.py:761
  150.8 2.6 %input_sent.3 = (f32[512,768]{1,0:T(8,128)S(1)}, f32[8,768]{1,0:T(8,128)S(1)}) custom-call(s32[4]{0:T(128)S(1)} %pad_add_fusion.refs_0_, bf16[2048,768]{1,0:T(8,128)(2,1)S(1)} %copy-done.3, bf16[2048,384]{1,0:T(8,128)(2,1)S(1)} %get-tuple-element.162.refs_4_.refs_2_, bf16[2048,384]{1,0:T(8,128)(2,1)S(1)} %get-tuple-element.210.refs_3_, ...), custom_call_target="tpu_custom_call" | custom-call | flops 1000000000 | bytes 13484032 | tf_op jit(solution)/shard_map/input_sent/pallas_call | solution.py:761
  154.0 2.7 %input_own.2 = (bf16[512,768]{1,0:T(8,128)(2,1)S(1)}, f32[8,768]{1,0:T(8,128)S(1)}) custom-call(s32[4]{0:T(128)S(1)} %pad_add_fusion.refs_0_, bf16[2048,768]{1,0:T(8,128)(2,1)S(1)} %copy-done.3, bf16[2048,384]{1,0:T(8,128)(2,1)S(1)} %get-tuple-element.162.refs_4_.refs_2_, bf16[2048,384]{1,0:T(8,128)(2,1)S(1)} %get-tuple-element.210.refs_3_, ...), custom_call_target="tpu_custom_call" | custom-call | flops 1000000000 | bytes 14270464 | tf_op jit(solution)/shard_map/input_own/pallas_call | solution.py:761
  156.8 2.7 %input_own.3 = (bf16[512,768]{1,0:T(8,128)(2,1)S(1)}, f32[8,128]{1,0:T(8,128)S(1)}) custom-call(s32[4]{0:T(128)S(1)} %pad_add_fusion.refs_0_, bf16[2048,768]{1,0:T(8,128)(2,1)S(1)} %copy-done.3, bf16[2048,384]{1,0:T(8,128)(2,1)S(1)} %get-tuple-element.162.refs_4_.refs_2_, bf16[2048,384]{1,0:T(8,128)(2,1)S(1)} %get-tuple-element.210.refs_3_, ...), custom_call_target="tpu_custom_call" | custom-call | flops 1000000000 | bytes 14249984 | tf_op jit(solution)/shard_map/input_own/pallas_call | solution.py:761
  162.4 4.4 %all-to-all-start = ((bf16[8,368,128]{2,1,0:T(8,128)(2,1)}), bf16[8,368,128]{2,1,0:T(8,128)(2,1)}, u32[]{:S(2)}, u32[]{:S(2)}) async-start(bf16[8,368,128]{2,1,0:T(8,128)(2,1)} %copy-done.10), calls=%async_computation | async-start | bytes 1507328 | tf_op jit(solution)/shard_map/all_to_all | solution.py:850
  173.2 10.9 %out.1 = bf16[2048,768]{1,0:T(8,128)(2,1)} custom-call(bf16[2048,768]{1,0:T(8,128)(2,1)S(1)} %copy-done.3, bf16[2048,384]{1,0:T(8,128)(2,1)} %get-tuple-element.231.refs_1_, bf16[2048,384]{1,0:T(8,128)(2,1)} %collective-permute-done.17.refs_2_, bf16[2048,384]{1,0:T(8,128)(2,1)} %collective-permute-done.26.refs_3_, ...), custom_call_target="tpu_custom_call" | custom-call | flops 5000000000 | bytes 14942208 | tf_op jit(solution)/shard_map/out/pallas_call | solution.py:761
  184.1 2.9 %all-to-all-done.refs_0_ = bf16[8,368,128]{2,1,0:T(8,128)(2,1)} async-done(((bf16[8,368,128]{2,1,0:T(8,128)(2,1)}), bf16[8,368,128]{2,1,0:T(8,128)(2,1)}, u32[]{:S(2)}, u32[]{:S(2)}) %all-to-all-start) | async-done | bytes 753696 | tf_op jit(solution)/shard_map/all_to_all | solution.py:850
  189.1 4.2 %all-to-all-start.1 = ((bf16[8,368,128]{2,1,0:T(8,128)(2,1)}), bf16[8,368,128]{2,1,0:T(8,128)(2,1)}, u32[]{:S(2)}, u32[]{:S(2)}) async-start(bf16[8,368,128]{2,1,0:T(8,128)(2,1)} %copy-done.11), calls=%async_computation.1 | async-start | bytes 1507328 | tf_op jit(solution)/shard_map/all_to_all | solution.py:850
  193.9 10.1 %collective-permute-done.29.refs_7_ = bf16[512,768]{1,0:T(8,128)(2,1)} collective-permute-done((bf16[512,768]{1,0:T(8,128)(2,1)}, bf16[512,768]{1,0:T(8,128)(2,1)}, u32[]{:S(2)}, u32[]{:S(2)}) %collective-permute-start.29) | collective-permute-done | bytes 786464 | tf_op jit(solution)/shard_map/ppermute | solution.py:783
  207.6 1.9 copy-done.9
  211.8 7.8 %in_back.1 = f32[2048,768]{1,0:T(8,128)} custom-call(s32[4]{0:T(128)S(1)} %pad_add_fusion.refs_0_, bf16[2048,768]{1,0:T(8,128)(2,1)S(1)} %copy-done.3, bf16[2048,768]{1,0:T(8,128)(2,1)S(1)} %copy-done.9, f32[1,768]{1,0:T(1,128)S(1)} %broadcast_in_dim.6.refs_4_.refs_3_, bf16[512,768]{1,0:T(8,128)(2,1)S(1)} %copy-done.13, ...), custom_call_target="tpu_custom_call" | custom-call | flops 1000000000 | bytes 18877440 | tf_op jit(solution)/shard_map/in_back/pallas_call | solution.py:761
  224.1 2.7 %unpack_out.1 = f32[384,768]{1,0:T(8,128)} custom-call(s32[4]{0:T(128)S(1)} %pad_add_fusion.refs_0_, bf16[4,576,128]{2,1,0:T(8,128)(2,1)S(1)} %copy-done.6, bf16[4,576,128]{2,1,0:T(8,128)(2,1)} %collective-permute-done.37.refs_2_), custom_call_target="tpu_custom_call" | custom-call | flops 1000000 | bytes 2359296 | tf_op jit(solution)/shard_map/unpack_out/pallas_call | solution.py:761
  226.8 3.8 %unpack.1 = f32[768,2,384]{2,1,0:T(2,128)} custom-call(s32[4]{0:T(128)S(1)} %pad_add_fusion.refs_0_, bf16[4,576,128]{2,1,0:T(8,128)(2,1)S(1)} %copy-done.7, bf16[4,576,128]{2,1,0:T(8,128)(2,1)} %collective-permute-done.37.refs_2_, bf16[8,368,128]{2,1,0:T(8,128)(2,1)} %all-to-all-done.1.refs_0_.refs_3_), custom_call_target="tpu_custom_call" | custom-call | flops 1000000 | bytes 4292608 | tf_op jit(solution)/shard_map/unpack/pallas_call | solution.py:761
  230.7 3.3 %collective-permute-done.36.refs_4_ = f32[456,128]{1,0:T(8,128)S(1)} collective-permute-done((f32[456,128]{1,0:T(8,128)S(1)}, f32[456,128]{1,0:T(8,128)S(1)}, u32[]{:S(2)}, u32[]{:S(2)}) %collective-permute-start.36) | collective-permute-done | bytes 233504 | tf_op jit(solution)/shard_map/ppermute | solution.py:783
  (174 shorter events, 58.6 us)
Async XLA Ops:
  1.5 10.4 %collective-permute-start = (bf16[16,768]{1,0:T(8,128)(2,1)S(1)}, bf16[16,768]{1,0:T(8,128)(2,1)S(1)}, u32[]{:S(2)}, u32[]{:S(2)}) collective-permute-start(bf16[16,768]{1,0:T(8,128)(2,1)S(1)} %slice.3), channel_id=1, source_target_pairs={{0,4},{4,8},{8,12},{12,16},{16,20},{20,24},{24,28},{1,5},{5,9},{9,... | collective-permute-start | bytes 73736 | tf_op jit(solution)/shard_map/ppermute | solution.py:886
  10.4 26.2 %collective-permute-start.4 = (bf16[384,768]{1,0:T(8,128)(2,1)S(1)}, bf16[384,768]{1,0:T(8,128)(2,1)S(1)}, u32[]{:S(2)}, u32[]{:S(2)}) collective-permute-start(bf16[384,768]{1,0:T(8,128)(2,1)S(1)} %copy-done.20), channel_id=1, source_target_pairs={{0,2},{1,3},{2,0},{3,1},{4,6},{5,7},{6,4},{7,5},{8,10},{9,11},{10,... | collective-permute-start | bytes 1769480 | tf_op jit(solution)/shard_map/ppermute | solution.py:783
  28.0 6.4 %collective-permute-start.1 = (f32[136,384]{1,0:T(8,128)S(1)}, f32[136,384]{1,0:T(8,128)S(1)}, u32[]{:S(2)}, u32[]{:S(2)}) collective-permute-start(f32[136,384]{1,0:T(8,128)S(1)} %get-tuple-element.141.refs_1_), channel_id=1, source_target_pairs={{0,4},{4,0},{8,12},{12,8},{16,20},{20,16},{24,28},{28,24},{1,5},{5... | collective-permute-start | bytes 626696 | tf_op jit(solution)/shard_map/ppermute | solution.py:783
  29.5 25.9 %collective-permute-start.5 = (bf16[384,768]{1,0:T(8,128)(2,1)S(1)}, bf16[384,768]{1,0:T(8,128)(2,1)S(1)}, u32[]{:S(2)}, u32[]{:S(2)}) collective-permute-start(bf16[384,768]{1,0:T(8,128)(2,1)S(1)} %copy-done.20), channel_id=1, source_target_pairs={{0,1},{1,0},{2,3},{3,2},{4,5},{5,4},{6,7},{7,6},{8,9},{9,8},{10,11... | collective-permute-start | bytes 1769480 | tf_op jit(solution)/shard_map/ppermute | solution.py:783
  35.0 6.4 %collective-permute-start.2 = (f32[136,384]{1,0:T(8,128)S(1)}, f32[136,384]{1,0:T(8,128)S(1)}, u32[]{:S(2)}, u32[]{:S(2)}) collective-permute-start(f32[136,384]{1,0:T(8,128)S(1)} %get-tuple-element.142.refs_1_), channel_id=1, source_target_pairs={{0,8},{4,12},{8,0},{12,4},{16,24},{20,28},{24,16},{28,20},{1,9},{5... | collective-permute-start | bytes 626696 | tf_op jit(solution)/shard_map/ppermute | solution.py:783
  36.6 18.9 %collective-permute-start.6 = (bf16[384,768]{1,0:T(8,128)(2,1)S(1)}, bf16[384,768]{1,0:T(8,128)(2,1)S(1)}, u32[]{:S(2)}, u32[]{:S(2)}) collective-permute-start(bf16[384,768]{1,0:T(8,128)(2,1)S(1)} %collective-permute-done.4.refs_6_), channel_id=1, source_target_pairs={{0,1},{1,0},{2,3},{3,2},{4,5},{5,4},{6,7},{7,6},{8,9},{9,8},{10,11... | collective-permute-start | bytes 1769480 | tf_op jit(solution)/shard_map/ppermute | solution.py:783
  42.0 12.9 %collective-permute-start.3 = (f32[136,384]{1,0:T(8,128)S(1)}, f32[136,384]{1,0:T(8,128)S(1)}, u32[]{:S(2)}, u32[]{:S(2)}) collective-permute-start(f32[136,384]{1,0:T(8,128)S(1)} %get-tuple-element.144.refs_1_), channel_id=1, source_target_pairs={{0,16},{4,20},{8,24},{12,28},{16,0},{20,4},{24,8},{28,12},{1,17},{... | collective-permute-start | bytes 626696 | tf_op jit(solution)/shard_map/ppermute | solution.py:783
  70.9 8.6 %collective-permute-start.10 = (f32[136,384]{1,0:T(8,128)S(1)}, f32[136,384]{1,0:T(8,128)S(1)}, u32[]{:S(2)}, u32[]{:S(2)}) collective-permute-start(f32[136,384]{1,0:T(8,128)S(1)} %get-tuple-element.172.refs_1_), channel_id=1, source_target_pairs={{0,4},{4,0},{8,12},{12,8},{16,20},{20,16},{24,28},{28,24},{1,5},{5... | collective-permute-start | bytes 626696 | tf_op jit(solution)/shard_map/ppermute | solution.py:783
  80.1 6.3 %collective-permute-start.11 = (f32[136,384]{1,0:T(8,128)S(1)}, f32[136,384]{1,0:T(8,128)S(1)}, u32[]{:S(2)}, u32[]{:S(2)}) collective-permute-start(f32[136,384]{1,0:T(8,128)S(1)} %get-tuple-element.174.refs_1_), channel_id=1, source_target_pairs={{0,8},{4,12},{8,0},{12,4},{16,24},{20,28},{24,16},{28,20},{1,9},{5... | collective-permute-start | bytes 626696 | tf_op jit(solution)/shard_map/ppermute | solution.py:783
  80.2 51.1 %collective-permute-start.17 = (bf16[2048,384]{1,0:T(8,128)(2,1)}, bf16[2048,384]{1,0:T(8,128)(2,1)}, u32[]{:S(2)}, u32[]{:S(2)}) collective-permute-start(bf16[2048,384]{1,0:T(8,128)(2,1)} %get-tuple-element.231.refs_1_), channel_id=1, source_target_pairs={{0,2},{1,3},{2,0},{3,1},{4,6},{5,7},{6,4},{7,5},{8,10},{9,11},{10,... | collective-permute-start | bytes 4718600 | tf_op jit(solution)/shard_map/ppermute | solution.py:783
  81.7 26.8 %collective-permute-start.13 = (f32[4,576,128]{2,1,0:T(8,128)S(1)}, f32[4,576,128]{2,1,0:T(8,128)S(1)}, u32[]{:S(2)}, u32[]{:S(2)}) collective-permute-start(f32[4,576,128]{2,1,0:T(8,128)S(1)} %get-tuple-element.181), channel_id=1, source_target_pairs={{0,4},{4,0},{8,12},{12,8},{16,20},{20,16},{24,28},{28,24},{1,5},{5... | collective-permute-start | bytes 3538952 | tf_op jit(solution)/shard_map/ppermute | solution.py:783
  87.0 14.4 %collective-permute-start.12 = (f32[136,384]{1,0:T(8,128)S(1)}, f32[136,384]{1,0:T(8,128)S(1)}, u32[]{:S(2)}, u32[]{:S(2)}) collective-permute-start(f32[136,384]{1,0:T(8,128)S(1)} %get-tuple-element.176.refs_1_), channel_id=1, source_target_pairs={{0,16},{4,20},{8,24},{12,28},{16,0},{20,4},{24,8},{28,12},{1,17},{... | collective-permute-start | bytes 626696 | tf_op jit(solution)/shard_map/ppermute | solution.py:783
  105.1 26.2 %collective-permute-start.18 = (f32[8,640]{1,0:T(8,128)S(1)}, f32[8,640]{1,0:T(8,128)S(1)}, u32[]{:S(2)}, u32[]{:S(2)}) collective-permute-start(f32[8,640]{1,0:T(8,128)S(1)} %get-tuple-element.178), channel_id=1, source_target_pairs={{4,0},{8,4},{12,8},{16,12},{20,16},{24,20},{28,24},{5,1},{9,5},{13... | collective-permute-start | bytes 61448 | tf_op jit(solution)/shard_map/ppermute | solution.py:1054
  109.2 17.5 %collective-permute-start.14 = (bf16[576,128]{1,0:T(8,128)(2,1)S(1)}, bf16[576,128]{1,0:T(8,128)(2,1)S(1)}, u32[]{:S(2)}, u32[]{:S(2)}) collective-permute-start(bf16[576,128]{1,0:T(8,128)(2,1)S(1)} %get-tuple-element.192), channel_id=1, source_target_pairs={{0,8},{4,12},{8,0},{12,4},{16,24},{20,28},{24,16},{28,20},{1,9},{5... | collective-permute-start | bytes 442376 | tf_op jit(solution)/shard_map/ppermute | solution.py:783
  110.9 15.7 %collective-permute-start.15 = (bf16[576,128]{1,0:T(8,128)(2,1)S(1)}, bf16[576,128]{1,0:T(8,128)(2,1)S(1)}, u32[]{:S(2)}, u32[]{:S(2)}) collective-permute-start(bf16[576,128]{1,0:T(8,128)(2,1)S(1)} %get-tuple-element.194), channel_id=1, source_target_pairs={{0,16},{4,20},{8,24},{12,28},{16,0},{20,4},{24,8},{28,12},{1,17},{... | collective-permute-start | bytes 442376 | tf_op jit(solution)/shard_map/ppermute | solution.py:783
  112.2 14.5 %collective-permute-start.16 = (bf16[576,128]{1,0:T(8,128)(2,1)S(1)}, bf16[576,128]{1,0:T(8,128)(2,1)S(1)}, u32[]{:S(2)}, u32[]{:S(2)}) collective-permute-start(bf16[576,128]{1,0:T(8,128)(2,1)S(1)} %get-tuple-element.196), channel_id=1, source_target_pairs={{0,24},{4,28},{8,16},{12,20},{16,8},{20,12},{24,0},{28,4},{1,25},{... | collective-permute-start | bytes 442376 | tf_op jit(solution)/shard_map/ppermute | solution.py:783
  126.8 19.5 %collective-permute-start.21 = (bf16[576,128]{1,0:T(8,128)(2,1)S(1)}, bf16[576,128]{1,0:T(8,128)(2,1)S(1)}, u32[]{:S(2)}, u32[]{:S(2)}) collective-permute-start(bf16[576,128]{1,0:T(8,128)(2,1)S(1)} %reduce.3.refs_1_), channel_id=1, source_target_pairs={{0,24},{4,28},{8,16},{12,20},{16,8},{20,12},{24,0},{28,4},{1,25},{... | collective-permute-start | bytes 442376 | tf_op jit(solution)/shard_map/ppermute | solution.py:783
  129.2 17.1 %collective-permute-start.20 = (bf16[576,128]{1,0:T(8,128)(2,1)S(1)}, bf16[576,128]{1,0:T(8,128)(2,1)S(1)}, u32[]{:S(2)}, u32[]{:S(2)}) collective-permute-start(bf16[576,128]{1,0:T(8,128)(2,1)S(1)} %reduce.3.refs_1_), channel_id=1, source_target_pairs={{0,16},{4,20},{8,24},{12,28},{16,0},{20,4},{24,8},{28,12},{1,17},{... | collective-permute-start | bytes 442376 | tf_op jit(solution)/shard_map/ppermute | solution.py:783
  129.2 17.1 %collective-permute-start.19 = (bf16[576,128]{1,0:T(8,128)(2,1)S(1)}, bf16[576,128]{1,0:T(8,128)(2,1)S(1)}, u32[]{:S(2)}, u32[]{:S(2)}) collective-permute-start(bf16[576,128]{1,0:T(8,128)(2,1)S(1)} %reduce.3.refs_1_), channel_id=1, source_target_pairs={{0,8},{4,12},{8,0},{12,4},{16,24},{20,28},{24,16},{28,20},{1,9},{5... | collective-permute-start | bytes 442376 | tf_op jit(solution)/shard_map/ppermute | solution.py:783
  149.6 4.4 %collective-permute-start.25 = (f32[512,768]{1,0:T(8,128)S(1)}, f32[512,768]{1,0:T(8,128)S(1)}, u32[]{:S(2)}, u32[]{:S(2)}) collective-permute-start(f32[512,768]{1,0:T(8,128)S(1)} %get-tuple-element.219), channel_id=1, source_target_pairs={{0,1},{1,0},{2,3},{3,2},{4,5},{5,4},{6,7},{7,6},{8,9},{9,8},{10,11... | collective-permute-start | bytes 4718600 | tf_op jit(solution)/shard_map/ppermute | solution.py:783
  153.4 8.0 %collective-permute-start.23 = (f32[448,128]{1,0:T(8,128)S(1)}, f32[448,128]{1,0:T(8,128)S(1)}, u32[]{:S(2)}, u32[]{:S(2)}) collective-permute-start(f32[448,128]{1,0:T(8,128)S(1)} %get-tuple-element.222), channel_id=1, source_target_pairs={{0,2},{1,3},{2,0},{3,1},{4,6},{5,7},{6,4},{7,5},{8,10},{9,11},{10,... | collective-permute-start | bytes 688136 | tf_op jit(solution)/shard_map/ppermute | solution.py:783
  161.5 7.4 %collective-permute-start.26 = (bf16[2048,384]{1,0:T(8,128)(2,1)}, bf16[2048,384]{1,0:T(8,128)(2,1)}, u32[]{:S(2)}, u32[]{:S(2)}) collective-permute-start(bf16[2048,384]{1,0:T(8,128)(2,1)} %get-tuple-element.231.refs_1_), channel_id=1, source_target_pairs={{0,1},{1,0},{2,3},{3,2},{4,5},{5,4},{6,7},{7,6},{8,9},{9,8},{10,11... | collective-permute-start | bytes 4718600 | tf_op jit(solution)/shard_map/ppermute | solution.py:783
  162.4 6.5 %collective-permute-start.27 = (bf16[2048,384]{1,0:T(8,128)(2,1)}, bf16[2048,384]{1,0:T(8,128)(2,1)}, u32[]{:S(2)}, u32[]{:S(2)}) collective-permute-start(bf16[2048,384]{1,0:T(8,128)(2,1)} %collective-permute-done.17.refs_2_), channel_id=1, source_target_pairs={{0,1},{1,0},{2,3},{3,2},{4,5},{5,4},{6,7},{7,6},{8,9},{9,8},{10,11... | collective-permute-start | bytes 4718600 | tf_op jit(solution)/shard_map/ppermute | solution.py:783
  162.4 24.6 %all-to-all-start = ((bf16[8,368,128]{2,1,0:T(8,128)(2,1)}), bf16[8,368,128]{2,1,0:T(8,128)(2,1)}, u32[]{:S(2)}, u32[]{:S(2)}) async-start(bf16[8,368,128]{2,1,0:T(8,128)(2,1)} %copy-done.10), calls=%async_computation | async-start | bytes 1507328 | tf_op jit(solution)/shard_map/all_to_all | solution.py:850
  166.8 37.2 %collective-permute-start.28 = (bf16[512,768]{1,0:T(8,128)(2,1)}, bf16[512,768]{1,0:T(8,128)(2,1)}, u32[]{:S(2)}, u32[]{:S(2)}) collective-permute-start(bf16[512,768]{1,0:T(8,128)(2,1)} %copy-done.12), channel_id=1, source_target_pairs={{0,2},{1,3},{2,0},{3,1},{4,6},{5,7},{6,4},{7,5},{8,10},{9,11},{10,... | collective-permute-start | bytes 2359304 | tf_op jit(solution)/shard_map/ppermute | solution.py:783
  167.4 36.6 %collective-permute-start.29 = (bf16[512,768]{1,0:T(8,128)(2,1)}, bf16[512,768]{1,0:T(8,128)(2,1)}, u32[]{:S(2)}, u32[]{:S(2)}) collective-permute-start(bf16[512,768]{1,0:T(8,128)(2,1)} %copy-done.14), channel_id=1, source_target_pairs={{0,2},{1,3},{2,0},{3,1},{4,6},{5,7},{6,4},{7,5},{8,10},{9,11},{10,... | collective-permute-start | bytes 2359304 | tf_op jit(solution)/shard_map/ppermute | solution.py:783
  189.1 30.5 %all-to-all-start.1 = ((bf16[8,368,128]{2,1,0:T(8,128)(2,1)}), bf16[8,368,128]{2,1,0:T(8,128)(2,1)}, u32[]{:S(2)}, u32[]{:S(2)}) async-start(bf16[8,368,128]{2,1,0:T(8,128)(2,1)} %copy-done.11), calls=%async_computation.1 | async-start | bytes 1507328 | tf_op jit(solution)/shard_map/all_to_all | solution.py:850
  193.3 12.5 %collective-permute-start.30 = (bf16[512,768]{1,0:T(8,128)(2,1)}, bf16[512,768]{1,0:T(8,128)(2,1)S(1)}, u32[]{:S(2)}, u32[]{:S(2)}) collective-permute-start(bf16[512,768]{1,0:T(8,128)(2,1)} %copy-done.12), channel_id=1, source_target_pairs={{0,1},{1,0},{2,3},{3,2},{4,5},{5,4},{6,7},{7,6},{8,9},{9,8},{10,11... | collective-permute-start | bytes 2359304 | tf_op jit(solution)/shard_map/ppermute | solution.py:783
  193.4 12.5 %collective-permute-start.32 = (bf16[512,768]{1,0:T(8,128)(2,1)}, bf16[512,768]{1,0:T(8,128)(2,1)S(1)}, u32[]{:S(2)}, u32[]{:S(2)}) collective-permute-start(bf16[512,768]{1,0:T(8,128)(2,1)} %copy-done.14), channel_id=1, source_target_pairs={{0,1},{1,0},{2,3},{3,2},{4,5},{5,4},{6,7},{7,6},{8,9},{9,8},{10,11... | collective-permute-start | bytes 2359304 | tf_op jit(solution)/shard_map/ppermute | solution.py:783
  204.5 18.6 %collective-permute-start.37 = (bf16[4,576,128]{2,1,0:T(8,128)(2,1)}, bf16[4,576,128]{2,1,0:T(8,128)(2,1)}, u32[]{:S(2)}, u32[]{:S(2)}) collective-permute-start(bf16[4,576,128]{2,1,0:T(8,128)(2,1)} %copy-done.5), channel_id=1, source_target_pairs={{0,4},{4,0},{8,12},{12,8},{16,20},{20,16},{24,28},{28,24},{1,5},{5... | collective-permute-start | bytes 1769480 | tf_op jit(solution)/shard_map/ppermute | solution.py:783
  221.0 9.6 %collective-permute-start.35 = (f32[456,128]{1,0:T(8,128)S(1)}, f32[456,128]{1,0:T(8,128)S(1)}, u32[]{:S(2)}, u32[]{:S(2)}) collective-permute-start(f32[456,128]{1,0:T(8,128)S(1)} %quarter.1.refs_1_), channel_id=1, source_target_pairs={{0,2},{1,3},{2,0},{3,1},{4,6},{5,7},{6,4},{7,5},{8,10},{9,11},{10,... | collective-permute-start | bytes 700424 | tf_op jit(solution)/shard_map/ppermute | solution.py:783
  222.4 11.6 %collective-permute-start.36 = (f32[456,128]{1,0:T(8,128)S(1)}, f32[456,128]{1,0:T(8,128)S(1)}, u32[]{:S(2)}, u32[]{:S(2)}) collective-permute-start(f32[456,128]{1,0:T(8,128)S(1)} %collective-permute-done.34.refs_2_), channel_id=1, source_target_pairs={{0,2},{1,3},{2,0},{3,1},{4,6},{5,7},{6,4},{7,5},{8,10},{9,11},{10,... | collective-permute-start | bytes 700424 | tf_op jit(solution)/shard_map/ppermute | solution.py:783
  (48 other events, 361.1 us)

commit v4 on v3

--- a/solution.py
+++ b/solution.py
@@ -599,16 +599,10 @@
     out[...] = value[0, 0:16, :]
 
 
-def k_quarter(cut, slots, parts, out):
-    count = parts.shape[0]
-    _, each, rest = slots
-    rows = each + rest
-    for k in range(count):
-        value = parts[k, cut:, :].astype(F32)
-        small = value[each : each + rest + 8] + value[each + rest + 8 :]
-        out[k * rows : k * rows + each, :] = value[:each]
-        out[k * rows + each : (k + 1) * rows, :] = small[:rest]
-        out[count * rows + k : count * rows + k + 1, :] = small[rest : rest + 1]
+def k_quarter(cut, parts, out):
+    rows = parts.shape[1] - cut
+    for k in range(parts.shape[0]):
+        out[k * rows : (k + 1) * rows, :] = parts[k, cut:, :]
 
 
 def unstack(value, rows):
@@ -648,21 +642,23 @@
     w_bc_o, w_dt_o, bc_taps_o, bias_o, alog_o, skip_o, norm_o, taps_o, gain_o, buf = refs[count:]
     total, each, rest = slots
     steps = total // count
-    norms = []
+    tall = each + 2 * (rest + 8)
+    dim = w_bc_o.shape[0]
+    norms = [[] for _ in range(dim // LANES)]
     for k in range(count):
         from_head, at = place[2] ^ k, 0
         for mask in powers(count):
             at = 2 * at + (from_head // mask) % 2
         for t in range(steps):
             slot = at * steps + t
-            value = refs[k][t * (each + rest) : (t + 1) * (each + rest), :]
+            value = refs[k][t * tall : (t + 1) * tall, :].astype(F32)
+            small = value[each : each + rest + 8] + value[each + rest + 8 :]
             buf[pl.ds(pl.multiple_of(slot * each, 8), each), :] = value[:each]
-            buf[pl.ds(pl.multiple_of(total * each + slot * rest, 8), rest), :] = value[each:]
-        norms.append(refs[k][steps * (each + rest) : steps * (each + rest) + 8, :])
-    norm = tree(norms)
-    dim = w_bc_o.shape[0]
-    for k in range(dim // LANES):
-        norm_o[:, k * LANES : (k + 1) * LANES] = norm[k : k + 1, :]
+            buf[pl.ds(pl.multiple_of(total * each + slot * rest, 8), rest), :] = small[:rest]
+            if t < len(norms):
+                norms[t].append(small[rest : rest + 1])
+    for k, rows in enumerate(norms):
+        norm_o[:, k * LANES : (k + 1) * LANES] = tree(rows)
     w_bc_o[:, :LANES] = buf[0:dim, :]
     w_bc_o[:, LANES:] = buf[dim : 2 * dim, :]
     at = total * each
@@ -779,6 +775,10 @@
     )(*scalars, *[a for a, _ in ins])
 
 
+def far(pair):
+    return (pltpu.with_memory_space_constraint(pair[0], pltpu.HBM), pair[1])
+
+
 def swap(value, axis, mask):
     return lax.ppermute(value, axis, [(i, i ^ mask) for i in range(lax.axis_size(axis))])
 
@@ -932,7 +932,7 @@
         k_front,
         groups,
         [
-            (group_first, SMEM), (group_valid, SMEM), rows(hidden_in), full(rim), full(gain_in),
+            (group_first, SMEM), (group_valid, SMEM), far(rows(hidden_in)), full(rim), full(gain_in),
             part_x, full(w_bc), full(w_dt_here), full(per_head), full(cx), full(conv_bc),
         ],
         [
@@ -1223,7 +1223,7 @@
     (grad_in,) = call(
         functools.partial(k_in_back, steps),
         groups,
-        [rows(hidden_in, turned_back), rows(out_grad, turned_back), full(gain_in)]
+        [far(rows(hidden_in, turned_back)), far(rows(out_grad, turned_back)), full(gain_in)]
         + [in_cut(a, k) for k, found in enumerate(parts + others) for a in found],
         [out_rows(dim, F32, turned_back)],
         [],
@@ -1231,9 +1231,9 @@
         "in_back",
         place,
     )
-    shape = (small_rows // head_count + tok_count, LANES)
+    shape = (tok_count * (each + 2 * (rest + 8)), LANES)
     (quarter,) = call(
-        functools.partial(k_quarter, piece_b, slots), 1, [full(after(sum_b, grad_in))], [out_full(shape, F32)],
+        functools.partial(k_quarter, piece_b), 1, [full(after(sum_b, grad_in))], [out_full(shape, BF16)],
         [], 10**6, "quarter",
     )
     quarters = [(quarter, 0)]

time: 238 us -> 232 us (0.975)
  local copies, waits for them, and re-layouts: 18 us -> 10.8 us
    unnamed x82 -> x78, local copies, waits for them, and re-layouts: 15.7 us -> 8.52 us
  transfers between devices with their start and end apart: 40 -> 40, of which waited for: 14 -> 15; matrix products, arithmetic and copies ran while one was open for 2% -> 2% of each run, Pallas kernels for 50% -> 51%
where the time goes in v4:
time: 232 us; the launch traced here: 231 us
  Pallas kernels  133 us (57%)
  starting transfers between devices  44.8 us (19%)
  waiting for transfers between devices  38.9 us (17%)
  local copies, waits for them, and re-layouts  10.8 us (5%)
    pallas_call x32, Pallas kernels, call(): pl.pallas_call(body, grid_spec=pltpu.PrefetchScalarGridSpec(num_scalar_pr...  133 us
    ppermute x36, waiting for transfers between devices, swap(): lax.ppermute(value, axis, [(i, i ^ mask) for i in range(lax.axis_size(axi...  36.1 us
    ppermute x36, starting transfers between devices, swap(): lax.ppermute(value, axis, [(i, i ^ mask) for i in range(lax.axis_size(axi...  30.3 us
    unnamed x78, local copies, waits for them, and re-layouts  8.52 us
    all_to_all x2, starting transfers between devices, exchange(): return lax.all_to_all(pieces, axis, 0, 0, tiled=True)  8.04 us
    ppermute x1, starting transfers between devices, on_device(): rim = lax.ppermute(hidden_in[tokens - 16:], 'tok', route)  4.86 us
  transfers between devices with their start and end apart: 40, of which 15 were waited for; matrix products, arithmetic and copies ran while one was open for 2% of the time, Pallas kernels for 51%

profile of v4, /device:TPU:0, one launch (start us, length us, event | category | flops | bytes accessed | tf_op | source)
XLA Modules:
  0.0 230.7 jit_solution(17792979362674449121)
XLA Ops:
  1.5 4.9 %collective-permute-start = (bf16[16,768]{1,0:T(8,128)(2,1)S(1)}, bf16[16,768]{1,0:T(8,128)(2,1)S(1)}, u32[]{:S(2)}, u32[]{:S(2)}) collective-permute-start(bf16[16,768]{1,0:T(8,128)(2,1)S(1)} %slice.3), channel_id=1, source_target_pairs={{0,4},{4,8},{8,12},{12,16},{16,20},{20,24},{24,28},{1,5},{5,9},{9,... | collective-permute-start | bytes 73736 | tf_op jit(solution)/shard_map/ppermute | solution.py:886
  12.0 14.6 %front.1 = (bf16[2048,768]{1,0:T(8,128)(2,1)S(1)}, f32[2048,640]{1,0:T(8,128)S(1)}, f32[2048,128]{1,0:T(8,128)S(1)}, f32[8,8,640]{2,1,0:T(8,128)S(1)}, f32[8,16,...) custom-call(s32[8]{0:T(128)S(1)} %copy-done.13, ...), custom_call_target="tpu_custom_call" | custom-call | flops 4000000000 | bytes 22986304 | tf_op jit(solution)/shard_map/front/pallas_call | solution.py:757
  28.2 4.8 %collective-permute-done.1.refs_2_ = f32[136,384]{1,0:T(8,128)S(1)} collective-permute-done((f32[136,384]{1,0:T(8,128)S(1)}, f32[136,384]{1,0:T(8,128)S(1)}, u32[]{:S(2)}, u32[]{:S(2)}) %collective-permute-start.1) | collective-permute-done | bytes 208928 | tf_op jit(solution)/shard_map/ppermute | solution.py:783
  35.3 4.7 %proj.1 = (f32[2048,384]{1,0:T(8,128)S(1)}, f32[2048,384]{1,0:T(8,128)S(1)}, f32[2048,384]{1,0:T(8,128)S(1)}) custom-call(bf16[2048,768]{1,0:T(8,128)(2,1)S(1)} %get-tuple-element.198.refs_0_.refs_3_.refs_2_, bf16[2048,768]{1,0:T(8,128)(2,1)S(1)} %copy-done.6, bf16[768,768]{1,0:T(8,128)(2,1)S(1)} %bitcast.14, bf16[384,768]{1,0:T(8,128)(2,1)S(1)} %copy-done.18), custom_call_target="tpu_custom_call" | custom-call | flops 5000000000 | bytes 17498112 | tf_op jit(solution)/shard_map/proj/pallas_call | solution.py:757
  40.7 2.6 %collective-permute-start.3 = (f32[136,384]{1,0:T(8,128)S(1)}, f32[136,384]{1,0:T(8,128)S(1)}, u32[]{:S(2)}, u32[]{:S(2)}) collective-permute-start(f32[136,384]{1,0:T(8,128)S(1)} %get-tuple-element.144.refs_1_), channel_id=1, source_target_pairs={{0,16},{4,20},{8,24},{12,28},{16,0},{20,4},{24,8},{28,12},{1,17},{... | collective-permute-start | bytes 626696 | tf_op jit(solution)/shard_map/ppermute | solution.py:783
  43.3 6.5 %within.1 = (f32[2048,384]{1,0:T(8,128)S(1)}, f32[2048,384]{1,0:T(8,128)S(1)}) custom-call(bf16[2048,384]{1,0:T(8,128)(2,1)S(1)} %get-tuple-element.149.refs_0_.refs_6_.refs_1_.refs_3_, bf16[2048,256]{1,0:T(8,128)(2,1)S(1)} %get-tuple-element.148.refs_1_.refs_3_.refs_7_.refs_2_.refs_4_, f32[2048,128]{1,0:T(8,128)S(1)} %get-tuple-element.150.refs_2_.refs_3_.refs_4_.refs_7_, ...), custom_call_target="tpu_custom_call" | custom-call | flops 5000000000 | bytes 11010048 | tf_op jit(solution)/shard_map/within/pallas_call | solution.py:757
  49.8 3.7 %collective-permute-done.3.refs_2_ = f32[136,384]{1,0:T(8,128)S(1)} collective-permute-done((f32[136,384]{1,0:T(8,128)S(1)}, f32[136,384]{1,0:T(8,128)S(1)}, u32[]{:S(2)}, u32[]{:S(2)}) %collective-permute-start.3) | collective-permute-done | bytes 208928 | tf_op jit(solution)/shard_map/ppermute | solution.py:783
  54.2 3.9 %gate.1 = (f32[2048,384]{1,0:T(8,128)S(1)}, f32[16,128,384]{2,1,0:T(8,128)S(1)}, f32[2,2048]{1,0:T(2,128)S(1)}) custom-call(f32[16,128,384]{2,1,0:T(8,128)S(1)} %get-tuple-element.139.refs_0_, f32[16,1,384]{2,1,0:T(1,128)S(1)} %get-tuple-element.140.refs_1_, f32[136,384]{1,0:T(8,128)S(1)} %merge.8.refs_2_, ...), custom_call_target="tpu_custom_call" | custom-call | flops 3000000000 | bytes 24897024 | tf_op jit(solution)/shard_map/gate/pallas_call | solution.py:757
  63.9 7.5 %gate_back.1 = (bf16[2048,384]{1,0:T(8,128)(2,1)}, bf16[2048,384]{1,0:T(8,128)(2,1)S(1)}, bf16[2048,384]{1,0:T(8,128)(2,1)S(1)}, f32[16,128,384]{2,1,0:T(8,128)S...) custom-call(s32[8]{0:T(128)S(1)} %copy-done.13, ...), custom_call_target="tpu_custom_call" | custom-call | flops 3000000000 | bytes 26539552 | tf_op jit(solution)/shard_map/gate_back/pallas_call | solution.py:757
  73.0 7.3 %weights.1 = (f32[4,576,128]{2,1,0:T(8,128)S(1)}, f32[4,576,128]{2,1,0:T(8,128)S(1)}) custom-call(s32[4]{0:T(128)S(1)} %pad_add_fusion.refs_0_, bf16[2048,384]{1,0:T(8,128)(2,1)} %get-tuple-element.231.refs_1_, bf16[2048,768]{1,0:T(8,128)(2,1)S(1)} %copy-done.7, bf16[2048,768]{1,0:T(8,128)(2,1)S(1)} %copy-done.33, ...), custom_call_target="tpu_custom_call" | custom-call | flops 12000000000 | bytes 47185920 | tf_op jit(solution)/shard_map/weights/pallas_call | solution.py:757
  82.8 4.2 %collective-permute-done.11.refs_2_ = f32[136,384]{1,0:T(8,128)S(1)} collective-permute-done((f32[136,384]{1,0:T(8,128)S(1)}, f32[136,384]{1,0:T(8,128)S(1)}, u32[]{:S(2)}, u32[]{:S(2)}) %collective-permute-start.11) | collective-permute-done | bytes 208928 | tf_op jit(solution)/shard_map/ppermute | solution.py:783
  88.9 13.2 %within_back.1 = (f32[2048,384]{1,0:T(8,128)S(1)}, f32[2048,256]{1,0:T(8,128)S(1)}, f32[2048,128]{1,0:T(8,128)S(1)}, f32[2048,128]{1,0:T(8,128)S(1)}) custom-call(bf16[2048,384]{1,0:T(8,128)(2,1)S(1)} %get-tuple-element.149.refs_0_.refs_6_.refs_1_.refs_3_, bf16[2048,256]{1,0:T(8,128)(2,1)S(1)} %get-tuple-element.148.refs_1_.refs_3_.refs_7_.refs_2_.refs_4_, ...), custom_call_target="tpu_custom_call" | custom-call | flops 40000000000 | bytes 79708160 | tf_op jit(solution)/shard_map/within_back/pallas_call | solution.py:757
  102.7 3.0 %rim.1 = (f32[8,16,640]{2,1,0:T(8,128)S(1)}, f32[8,640]{1,0:T(8,128)S(1)}) custom-call(s32[8]{0:T(128)S(1)} %copy-done.13, bf16[2048,384]{1,0:T(8,128)(2,1)S(1)} %get-tuple-element.149.refs_0_.refs_6_.refs_1_.refs_3_, bf16[2048,256]{1,0:T(8,128)(2,1)S(1)} %get-tuple-element.148.refs_1_.refs_3_.refs_7_.refs_2_.refs_4_, ...), custom_call_target="tpu_custom_call" | custom-call | flops 1000000000 | bytes 16642080 | tf_op jit(solution)/shard_map/rim/pallas_call | solution.py:757
  107.3 1.8 collective-permute-done.13.refs_2_
  114.3 12.9 %back_start.1 = (bf16[2048,384]{1,0:T(8,128)(2,1)S(1)}, bf16[2048,512]{1,0:T(8,128)(2,1)S(1)}, bf16[2048,128]{1,0:T(8,128)(2,1)S(1)}, f32[768,384]{1,0:T(8,128)S...) custom-call(s32[4]{0:T(128)S(1)} %pad_add_fusion.refs_0_, ...), custom_call_target="tpu_custom_call" | custom-call | flops 20000000000 | bytes 145787008 | tf_op jit(solution)/shard_map/back_start/pallas_call | solution.py:757
  127.4 2.4 %collective-permute-start.21 = (bf16[576,128]{1,0:T(8,128)(2,1)S(1)}, bf16[576,128]{1,0:T(8,128)(2,1)S(1)}, u32[]{:S(2)}, u32[]{:S(2)}) collective-permute-start(bf16[576,128]{1,0:T(8,128)(2,1)S(1)} %reduce.3.refs_1_), channel_id=1, source_target_pairs={{0,24},{4,28},{8,16},{12,20},{16,8},{20,12},{24,0},{28,4},{1,25},{... | collective-permute-start | bytes 442376 | tf_op jit(solution)/shard_map/ppermute | solution.py:783
  129.8 2.0 collective-permute-start.19
  131.9 15.0 %back_end.1 = (bf16[2048,384]{1,0:T(8,128)(2,1)S(1)}, bf16[2048,512]{1,0:T(8,128)(2,1)S(1)}, bf16[2048,128]{1,0:T(8,128)(2,1)S(1)}, f32[768,384]{1,0:T(8,128)S(1...) custom-call(s32[4]{0:T(128)S(1)} %pad_add_fusion.refs_0_, ...), custom_call_target="tpu_custom_call", output_to_operand_aliasing={{0}: (26, {}), {1}: (27, {}), {2}: (28, {}), {3}: (29, {}),... | custom-call | flops 20000000000 | bytes 177375360 | tf_op jit(solution)/shard_map/back_end/pallas_call | solution.py:757
  147.6 2.6 %input_sent.2 = (f32[512,768]{1,0:T(8,128)S(1)}, f32[8,768]{1,0:T(8,128)S(1)}) custom-call(s32[4]{0:T(128)S(1)} %pad_add_fusion.refs_0_, bf16[2048,768]{1,0:T(8,128)(2,1)S(1)} %copy-done.2, bf16[2048,384]{1,0:T(8,128)(2,1)S(1)} %get-tuple-element.162.refs_4_.refs_2_, bf16[2048,384]{1,0:T(8,128)(2,1)S(1)} %get-tuple-element.210.refs_3_, ...), custom_call_target="tpu_custom_call" | custom-call | flops 1000000000 | bytes 13459456 | tf_op jit(solution)/shard_map/input_sent/pallas_call | solution.py:757
  151.4 2.6 %input_sent.3 = (f32[512,768]{1,0:T(8,128)S(1)}, f32[8,768]{1,0:T(8,128)S(1)}) custom-call(s32[4]{0:T(128)S(1)} %pad_add_fusion.refs_0_, bf16[2048,768]{1,0:T(8,128)(2,1)S(1)} %copy-done.2, bf16[2048,384]{1,0:T(8,128)(2,1)S(1)} %get-tuple-element.162.refs_4_.refs_2_, bf16[2048,384]{1,0:T(8,128)(2,1)S(1)} %get-tuple-element.210.refs_3_, ...), custom_call_target="tpu_custom_call" | custom-call | flops 1000000000 | bytes 13484032 | tf_op jit(solution)/shard_map/input_sent/pallas_call | solution.py:757
  154.6 2.7 %input_own.2 = (bf16[512,768]{1,0:T(8,128)(2,1)S(1)}, f32[8,768]{1,0:T(8,128)S(1)}) custom-call(s32[4]{0:T(128)S(1)} %pad_add_fusion.refs_0_, bf16[2048,768]{1,0:T(8,128)(2,1)S(1)} %copy-done.2, bf16[2048,384]{1,0:T(8,128)(2,1)S(1)} %get-tuple-element.162.refs_4_.refs_2_, bf16[2048,384]{1,0:T(8,128)(2,1)S(1)} %get-tuple-element.210.refs_3_, ...), custom_call_target="tpu_custom_call" | custom-call | flops 1000000000 | bytes 14270464 | tf_op jit(solution)/shard_map/input_own/pallas_call | solution.py:757
  157.4 2.7 %input_own.3 = (bf16[512,768]{1,0:T(8,128)(2,1)S(1)}, f32[8,128]{1,0:T(8,128)S(1)}) custom-call(s32[4]{0:T(128)S(1)} %pad_add_fusion.refs_0_, bf16[2048,768]{1,0:T(8,128)(2,1)S(1)} %copy-done.2, bf16[2048,384]{1,0:T(8,128)(2,1)S(1)} %get-tuple-element.162.refs_4_.refs_2_, bf16[2048,384]{1,0:T(8,128)(2,1)S(1)} %get-tuple-element.210.refs_3_, ...), custom_call_target="tpu_custom_call" | custom-call | flops 1000000000 | bytes 14249984 | tf_op jit(solution)/shard_map/input_own/pallas_call | solution.py:757
  160.1 1.9 collective-permute-done.23.refs_1_
  163.0 4.4 %all-to-all-start = ((bf16[8,368,128]{2,1,0:T(8,128)(2,1)}), bf16[8,368,128]{2,1,0:T(8,128)(2,1)}, u32[]{:S(2)}, u32[]{:S(2)}) async-start(bf16[8,368,128]{2,1,0:T(8,128)(2,1)} %copy-done.8), calls=%async_computation | async-start | bytes 1507328 | tf_op jit(solution)/shard_map/all_to_all | solution.py:850
  173.8 10.9 %out.1 = bf16[2048,768]{1,0:T(8,128)(2,1)} custom-call(bf16[2048,768]{1,0:T(8,128)(2,1)S(1)} %copy-done.2, bf16[2048,384]{1,0:T(8,128)(2,1)} %get-tuple-element.231.refs_1_, bf16[2048,384]{1,0:T(8,128)(2,1)} %collective-permute-done.17.refs_2_, bf16[2048,384]{1,0:T(8,128)(2,1)} %collective-permute-done.26.refs_3_, ...), custom_call_target="tpu_custom_call" | custom-call | flops 5000000000 | bytes 14942208 | tf_op jit(solution)/shard_map/out/pallas_call | solution.py:757
  184.7 2.9 %all-to-all-done.refs_0_ = bf16[8,368,128]{2,1,0:T(8,128)(2,1)} async-done(((bf16[8,368,128]{2,1,0:T(8,128)(2,1)}), bf16[8,368,128]{2,1,0:T(8,128)(2,1)}, u32[]{:S(2)}, u32[]{:S(2)}) %all-to-all-start) | async-done | bytes 753696 | tf_op jit(solution)/shard_map/all_to_all | solution.py:850
  187.6 2.1 reduce_both.1
  189.7 3.6 %all-to-all-start.1 = ((bf16[8,368,128]{2,1,0:T(8,128)(2,1)}), bf16[8,368,128]{2,1,0:T(8,128)(2,1)S(1)}, u32[]{:S(2)}, u32[]{:S(2)}) async-start(bf16[8,368,128]{2,1,0:T(8,128)(2,1)} %reduce_both.1), calls=%async_computation.1 | async-start | bytes 1507328 | tf_op jit(solution)/shard_map/all_to_all | solution.py:850
  193.9 10.7 %collective-permute-done.29.refs_7_ = bf16[512,768]{1,0:T(8,128)(2,1)} collective-permute-done((bf16[512,768]{1,0:T(8,128)(2,1)}, bf16[512,768]{1,0:T(8,128)(2,1)}, u32[]{:S(2)}, u32[]{:S(2)}) %collective-permute-start.29) | collective-permute-done | bytes 786464 | tf_op jit(solution)/shard_map/ppermute | solution.py:783
  208.2 9.5 %in_back.1 = f32[2048,768]{1,0:T(8,128)} custom-call(s32[4]{0:T(128)S(1)} %pad_add_fusion.refs_0_, bf16[2048,768]{1,0:T(8,128)(2,1)} %refs_1_.11, bf16[2048,768]{1,0:T(8,128)(2,1)} %refs_2_.4, f32[1,768]{1,0:T(1,128)S(1)} %broadcast_in_dim.6.refs_4_.refs_3_, bf16[512,768]{1,0:T(8,128)(2,1)S(1)} %copy-done.10, ...), custom_call_target="tpu_custom_call" | custom-call | flops 1000000000 | bytes 18877440 | tf_op jit(solution)/shard_map/in_back/pallas_call | solution.py:757
  223.0 2.5 %unpack.1 = f32[768,2,384]{2,1,0:T(2,128)} custom-call(s32[4]{0:T(128)S(1)} %pad_add_fusion.refs_0_, bf16[4,576,128]{2,1,0:T(8,128)(2,1)S(1)} %copy-done.5, bf16[4,576,128]{2,1,0:T(8,128)(2,1)S(1)} %collective-permute-done.37.refs_2_, bf16[8,368,128]{2,1,0:T(8,128)(2,1)S(1)} %all-to-all-done.1.refs_0_.refs_3_), custom_call_target="tpu_custom_call" | custom-call | flops 1000000 | bytes 4292608 | tf_op jit(solution)/shard_map/unpack/pallas_call | solution.py:757
  225.5 2.4 %collective-permute-done.36.refs_4_ = bf16[640,128]{1,0:T(8,128)(2,1)S(1)} collective-permute-done((bf16[640,128]{1,0:T(8,128)(2,1)S(1)}, bf16[640,128]{1,0:T(8,128)(2,1)S(1)}, u32[]{:S(2)}, u32[]{:S(2)}) %collective-permute-start.36) | collective-permute-done | bytes 163872 | tf_op jit(solution)/shard_map/ppermute | solution.py:783
  (170 shorter events, 52.8 us)
Async XLA Ops:
  1.5 10.5 %collective-permute-start = (bf16[16,768]{1,0:T(8,128)(2,1)S(1)}, bf16[16,768]{1,0:T(8,128)(2,1)S(1)}, u32[]{:S(2)}, u32[]{:S(2)}) collective-permute-start(bf16[16,768]{1,0:T(8,128)(2,1)S(1)} %slice.3), channel_id=1, source_target_pairs={{0,4},{4,8},{8,12},{12,16},{16,20},{20,24},{24,28},{1,5},{5,9},{9,... | collective-permute-start | bytes 73736 | tf_op jit(solution)/shard_map/ppermute | solution.py:886
  10.4 24.9 %collective-permute-start.4 = (bf16[384,768]{1,0:T(8,128)(2,1)S(1)}, bf16[384,768]{1,0:T(8,128)(2,1)S(1)}, u32[]{:S(2)}, u32[]{:S(2)}) collective-permute-start(bf16[384,768]{1,0:T(8,128)(2,1)S(1)} %copy-done.18), channel_id=1, source_target_pairs={{0,2},{1,3},{2,0},{3,1},{4,6},{5,7},{6,4},{7,5},{8,10},{9,11},{10,... | collective-permute-start | bytes 1769480 | tf_op jit(solution)/shard_map/ppermute | solution.py:783
  26.6 6.4 %collective-permute-start.1 = (f32[136,384]{1,0:T(8,128)S(1)}, f32[136,384]{1,0:T(8,128)S(1)}, u32[]{:S(2)}, u32[]{:S(2)}) collective-permute-start(f32[136,384]{1,0:T(8,128)S(1)} %get-tuple-element.141.refs_1_), channel_id=1, source_target_pairs={{0,4},{4,0},{8,12},{12,8},{16,20},{20,16},{24,28},{28,24},{1,5},{5... | collective-permute-start | bytes 626696 | tf_op jit(solution)/shard_map/ppermute | solution.py:783
  28.2 25.9 %collective-permute-start.5 = (bf16[384,768]{1,0:T(8,128)(2,1)S(1)}, bf16[384,768]{1,0:T(8,128)(2,1)S(1)}, u32[]{:S(2)}, u32[]{:S(2)}) collective-permute-start(bf16[384,768]{1,0:T(8,128)(2,1)S(1)} %copy-done.18), channel_id=1, source_target_pairs={{0,1},{1,0},{2,3},{3,2},{4,5},{5,4},{6,7},{7,6},{8,9},{9,8},{10,11... | collective-permute-start | bytes 1769480 | tf_op jit(solution)/shard_map/ppermute | solution.py:783
  33.6 6.4 %collective-permute-start.2 = (f32[136,384]{1,0:T(8,128)S(1)}, f32[136,384]{1,0:T(8,128)S(1)}, u32[]{:S(2)}, u32[]{:S(2)}) collective-permute-start(f32[136,384]{1,0:T(8,128)S(1)} %get-tuple-element.142.refs_1_), channel_id=1, source_target_pairs={{0,8},{4,12},{8,0},{12,4},{16,24},{20,28},{24,16},{28,20},{1,9},{5... | collective-permute-start | bytes 626696 | tf_op jit(solution)/shard_map/ppermute | solution.py:783
  35.3 18.9 %collective-permute-start.6 = (bf16[384,768]{1,0:T(8,128)(2,1)S(1)}, bf16[384,768]{1,0:T(8,128)(2,1)S(1)}, u32[]{:S(2)}, u32[]{:S(2)}) collective-permute-start(bf16[384,768]{1,0:T(8,128)(2,1)S(1)} %collective-permute-done.4.refs_6_), channel_id=1, source_target_pairs={{0,1},{1,0},{2,3},{3,2},{4,5},{5,4},{6,7},{7,6},{8,9},{9,8},{10,11... | collective-permute-start | bytes 1769480 | tf_op jit(solution)/shard_map/ppermute | solution.py:783
  40.7 12.9 %collective-permute-start.3 = (f32[136,384]{1,0:T(8,128)S(1)}, f32[136,384]{1,0:T(8,128)S(1)}, u32[]{:S(2)}, u32[]{:S(2)}) collective-permute-start(f32[136,384]{1,0:T(8,128)S(1)} %get-tuple-element.144.refs_1_), channel_id=1, source_target_pairs={{0,16},{4,20},{8,24},{12,28},{16,0},{20,4},{24,8},{28,12},{1,17},{... | collective-permute-start | bytes 626696 | tf_op jit(solution)/shard_map/ppermute | solution.py:783
  71.4 8.9 %collective-permute-start.10 = (f32[136,384]{1,0:T(8,128)S(1)}, f32[136,384]{1,0:T(8,128)S(1)}, u32[]{:S(2)}, u32[]{:S(2)}) collective-permute-start(f32[136,384]{1,0:T(8,128)S(1)} %get-tuple-element.172.refs_1_), channel_id=1, source_target_pairs={{0,4},{4,0},{8,12},{12,8},{16,20},{20,16},{24,28},{28,24},{1,5},{5... | collective-permute-start | bytes 626696 | tf_op jit(solution)/shard_map/ppermute | solution.py:783
  80.9 6.1 %collective-permute-start.11 = (f32[136,384]{1,0:T(8,128)S(1)}, f32[136,384]{1,0:T(8,128)S(1)}, u32[]{:S(2)}, u32[]{:S(2)}) collective-permute-start(f32[136,384]{1,0:T(8,128)S(1)} %get-tuple-element.174.refs_1_), channel_id=1, source_target_pairs={{0,8},{4,12},{8,0},{12,4},{16,24},{20,28},{24,16},{28,20},{1,9},{5... | collective-permute-start | bytes 626696 | tf_op jit(solution)/shard_map/ppermute | solution.py:783
  81.0 50.9 %collective-permute-start.17 = (bf16[2048,384]{1,0:T(8,128)(2,1)}, bf16[2048,384]{1,0:T(8,128)(2,1)}, u32[]{:S(2)}, u32[]{:S(2)}) collective-permute-start(bf16[2048,384]{1,0:T(8,128)(2,1)} %get-tuple-element.231.refs_1_), channel_id=1, source_target_pairs={{0,2},{1,3},{2,0},{3,1},{4,6},{5,7},{6,4},{7,5},{8,10},{9,11},{10,... | collective-permute-start | bytes 4718600 | tf_op jit(solution)/shard_map/ppermute | solution.py:783
  82.3 26.8 %collective-permute-start.13 = (f32[4,576,128]{2,1,0:T(8,128)S(1)}, f32[4,576,128]{2,1,0:T(8,128)S(1)}, u32[]{:S(2)}, u32[]{:S(2)}) collective-permute-start(f32[4,576,128]{2,1,0:T(8,128)S(1)} %get-tuple-element.181), channel_id=1, source_target_pairs={{0,4},{4,0},{8,12},{12,8},{16,20},{20,16},{24,28},{28,24},{1,5},{5... | collective-permute-start | bytes 3538952 | tf_op jit(solution)/shard_map/ppermute | solution.py:783
  87.7 14.4 %collective-permute-start.12 = (f32[136,384]{1,0:T(8,128)S(1)}, f32[136,384]{1,0:T(8,128)S(1)}, u32[]{:S(2)}, u32[]{:S(2)}) collective-permute-start(f32[136,384]{1,0:T(8,128)S(1)} %get-tuple-element.176.refs_1_), channel_id=1, source_target_pairs={{0,16},{4,20},{8,24},{12,28},{16,0},{20,4},{24,8},{28,12},{1,17},{... | collective-permute-start | bytes 626696 | tf_op jit(solution)/shard_map/ppermute | solution.py:783
  105.7 26.1 %collective-permute-start.18 = (f32[8,640]{1,0:T(8,128)S(1)}, f32[8,640]{1,0:T(8,128)S(1)}, u32[]{:S(2)}, u32[]{:S(2)}) collective-permute-start(f32[8,640]{1,0:T(8,128)S(1)} %get-tuple-element.178), channel_id=1, source_target_pairs={{4,0},{8,4},{12,8},{16,12},{20,16},{24,20},{28,24},{5,1},{9,5},{13... | collective-permute-start | bytes 61448 | tf_op jit(solution)/shard_map/ppermute | solution.py:1054
  109.8 17.5 %collective-permute-start.14 = (bf16[576,128]{1,0:T(8,128)(2,1)S(1)}, bf16[576,128]{1,0:T(8,128)(2,1)S(1)}, u32[]{:S(2)}, u32[]{:S(2)}) collective-permute-start(bf16[576,128]{1,0:T(8,128)(2,1)S(1)} %get-tuple-element.192), channel_id=1, source_target_pairs={{0,8},{4,12},{8,0},{12,4},{16,24},{20,28},{24,16},{28,20},{1,9},{5... | collective-permute-start | bytes 442376 | tf_op jit(solution)/shard_map/ppermute | solution.py:783
  111.5 15.7 %collective-permute-start.15 = (bf16[576,128]{1,0:T(8,128)(2,1)S(1)}, bf16[576,128]{1,0:T(8,128)(2,1)S(1)}, u32[]{:S(2)}, u32[]{:S(2)}) collective-permute-start(bf16[576,128]{1,0:T(8,128)(2,1)S(1)} %get-tuple-element.194), channel_id=1, source_target_pairs={{0,16},{4,20},{8,24},{12,28},{16,0},{20,4},{24,8},{28,12},{1,17},{... | collective-permute-start | bytes 442376 | tf_op jit(solution)/shard_map/ppermute | solution.py:783
  112.8 14.5 %collective-permute-start.16 = (bf16[576,128]{1,0:T(8,128)(2,1)S(1)}, bf16[576,128]{1,0:T(8,128)(2,1)S(1)}, u32[]{:S(2)}, u32[]{:S(2)}) collective-permute-start(bf16[576,128]{1,0:T(8,128)(2,1)S(1)} %get-tuple-element.196), channel_id=1, source_target_pairs={{0,24},{4,28},{8,16},{12,20},{16,8},{20,12},{24,0},{28,4},{1,25},{... | collective-permute-start | bytes 442376 | tf_op jit(solution)/shard_map/ppermute | solution.py:783
  127.4 19.5 %collective-permute-start.21 = (bf16[576,128]{1,0:T(8,128)(2,1)S(1)}, bf16[576,128]{1,0:T(8,128)(2,1)S(1)}, u32[]{:S(2)}, u32[]{:S(2)}) collective-permute-start(bf16[576,128]{1,0:T(8,128)(2,1)S(1)} %reduce.3.refs_1_), channel_id=1, source_target_pairs={{0,24},{4,28},{8,16},{12,20},{16,8},{20,12},{24,0},{28,4},{1,25},{... | collective-permute-start | bytes 442376 | tf_op jit(solution)/shard_map/ppermute | solution.py:783
  129.8 17.1 %collective-permute-start.20 = (bf16[576,128]{1,0:T(8,128)(2,1)S(1)}, bf16[576,128]{1,0:T(8,128)(2,1)S(1)}, u32[]{:S(2)}, u32[]{:S(2)}) collective-permute-start(bf16[576,128]{1,0:T(8,128)(2,1)S(1)} %reduce.3.refs_1_), channel_id=1, source_target_pairs={{0,16},{4,20},{8,24},{12,28},{16,0},{20,4},{24,8},{28,12},{1,17},{... | collective-permute-start | bytes 442376 | tf_op jit(solution)/shard_map/ppermute | solution.py:783
  129.8 17.1 %collective-permute-start.19 = (bf16[576,128]{1,0:T(8,128)(2,1)S(1)}, bf16[576,128]{1,0:T(8,128)(2,1)S(1)}, u32[]{:S(2)}, u32[]{:S(2)}) collective-permute-start(bf16[576,128]{1,0:T(8,128)(2,1)S(1)} %reduce.3.refs_1_), channel_id=1, source_target_pairs={{0,8},{4,12},{8,0},{12,4},{16,24},{20,28},{24,16},{28,20},{1,9},{5... | collective-permute-start | bytes 442376 | tf_op jit(solution)/shard_map/ppermute | solution.py:783
  150.2 4.4 %collective-permute-start.25 = (f32[512,768]{1,0:T(8,128)S(1)}, f32[512,768]{1,0:T(8,128)S(1)}, u32[]{:S(2)}, u32[]{:S(2)}) collective-permute-start(f32[512,768]{1,0:T(8,128)S(1)} %get-tuple-element.219), channel_id=1, source_target_pairs={{0,1},{1,0},{2,3},{3,2},{4,5},{5,4},{6,7},{7,6},{8,9},{9,8},{10,11... | collective-permute-start | bytes 4718600 | tf_op jit(solution)/shard_map/ppermute | solution.py:783
  154.0 8.0 %collective-permute-start.23 = (f32[448,128]{1,0:T(8,128)S(1)}, f32[448,128]{1,0:T(8,128)S(1)}, u32[]{:S(2)}, u32[]{:S(2)}) collective-permute-start(f32[448,128]{1,0:T(8,128)S(1)} %get-tuple-element.222), channel_id=1, source_target_pairs={{0,2},{1,3},{2,0},{3,1},{4,6},{5,7},{6,4},{7,5},{8,10},{9,11},{10,... | collective-permute-start | bytes 688136 | tf_op jit(solution)/shard_map/ppermute | solution.py:783
  162.1 7.4 %collective-permute-start.26 = (bf16[2048,384]{1,0:T(8,128)(2,1)}, bf16[2048,384]{1,0:T(8,128)(2,1)}, u32[]{:S(2)}, u32[]{:S(2)}) collective-permute-start(bf16[2048,384]{1,0:T(8,128)(2,1)} %get-tuple-element.231.refs_1_), channel_id=1, source_target_pairs={{0,1},{1,0},{2,3},{3,2},{4,5},{5,4},{6,7},{7,6},{8,9},{9,8},{10,11... | collective-permute-start | bytes 4718600 | tf_op jit(solution)/shard_map/ppermute | solution.py:783
  163.0 6.5 %collective-permute-start.27 = (bf16[2048,384]{1,0:T(8,128)(2,1)}, bf16[2048,384]{1,0:T(8,128)(2,1)}, u32[]{:S(2)}, u32[]{:S(2)}) collective-permute-start(bf16[2048,384]{1,0:T(8,128)(2,1)} %collective-permute-done.17.refs_2_), channel_id=1, source_target_pairs={{0,1},{1,0},{2,3},{3,2},{4,5},{5,4},{6,7},{7,6},{8,9},{9,8},{10,11... | collective-permute-start | bytes 4718600 | tf_op jit(solution)/shard_map/ppermute | solution.py:783
  163.0 24.6 %all-to-all-start = ((bf16[8,368,128]{2,1,0:T(8,128)(2,1)}), bf16[8,368,128]{2,1,0:T(8,128)(2,1)}, u32[]{:S(2)}, u32[]{:S(2)}) async-start(bf16[8,368,128]{2,1,0:T(8,128)(2,1)} %copy-done.8), calls=%async_computation | async-start | bytes 1507328 | tf_op jit(solution)/shard_map/all_to_all | solution.py:850
  167.4 37.2 %collective-permute-start.28 = (bf16[512,768]{1,0:T(8,128)(2,1)}, bf16[512,768]{1,0:T(8,128)(2,1)}, u32[]{:S(2)}, u32[]{:S(2)}) collective-permute-start(bf16[512,768]{1,0:T(8,128)(2,1)} %copy-done.9), channel_id=1, source_target_pairs={{0,2},{1,3},{2,0},{3,1},{4,6},{5,7},{6,4},{7,5},{8,10},{9,11},{10,... | collective-permute-start | bytes 2359304 | tf_op jit(solution)/shard_map/ppermute | solution.py:783
  168.0 36.6 %collective-permute-start.29 = (bf16[512,768]{1,0:T(8,128)(2,1)}, bf16[512,768]{1,0:T(8,128)(2,1)}, u32[]{:S(2)}, u32[]{:S(2)}) collective-permute-start(bf16[512,768]{1,0:T(8,128)(2,1)} %copy-done.11), channel_id=1, source_target_pairs={{0,2},{1,3},{2,0},{3,1},{4,6},{5,7},{6,4},{7,5},{8,10},{9,11},{10,... | collective-permute-start | bytes 2359304 | tf_op jit(solution)/shard_map/ppermute | solution.py:783
  189.7 28.0 %all-to-all-start.1 = ((bf16[8,368,128]{2,1,0:T(8,128)(2,1)}), bf16[8,368,128]{2,1,0:T(8,128)(2,1)S(1)}, u32[]{:S(2)}, u32[]{:S(2)}) async-start(bf16[8,368,128]{2,1,0:T(8,128)(2,1)} %reduce_both.1), calls=%async_computation.1 | async-start | bytes 1507328 | tf_op jit(solution)/shard_map/all_to_all | solution.py:850
  193.3 13.1 %collective-permute-start.30 = (bf16[512,768]{1,0:T(8,128)(2,1)S(1)}, bf16[512,768]{1,0:T(8,128)(2,1)S(1)}, u32[]{:S(2)}, u32[]{:S(2)}) collective-permute-start(bf16[512,768]{1,0:T(8,128)(2,1)S(1)} %copy-done.10), channel_id=1, source_target_pairs={{0,1},{1,0},{2,3},{3,2},{4,5},{5,4},{6,7},{7,6},{8,9},{9,8},{10,11... | collective-permute-start | bytes 2359304 | tf_op jit(solution)/shard_map/ppermute | solution.py:783
  193.4 13.1 %collective-permute-start.32 = (bf16[512,768]{1,0:T(8,128)(2,1)S(1)}, bf16[512,768]{1,0:T(8,128)(2,1)S(1)}, u32[]{:S(2)}, u32[]{:S(2)}) collective-permute-start(bf16[512,768]{1,0:T(8,128)(2,1)S(1)} %copy-done.12), channel_id=1, source_target_pairs={{0,1},{1,0},{2,3},{3,2},{4,5},{5,4},{6,7},{7,6},{8,9},{9,8},{10,11... | collective-permute-start | bytes 2359304 | tf_op jit(solution)/shard_map/ppermute | solution.py:783
  205.1 16.2 %collective-permute-start.37 = (bf16[4,576,128]{2,1,0:T(8,128)(2,1)S(1)}, bf16[4,576,128]{2,1,0:T(8,128)(2,1)S(1)}, u32[]{:S(2)}, u32[]{:S(2)}) collective-permute-start(bf16[4,576,128]{2,1,0:T(8,128)(2,1)S(1)} %copy-done.5), channel_id=1, source_target_pairs={{0,4},{4,0},{8,12},{12,8},{16,20},{20,16},{24,28},{28,24},{1,5},{5... | collective-permute-start | bytes 1769480 | tf_op jit(solution)/shard_map/ppermute | solution.py:783
  217.9 7.6 %collective-permute-start.35 = (bf16[640,128]{1,0:T(8,128)(2,1)S(1)}, bf16[640,128]{1,0:T(8,128)(2,1)S(1)}, u32[]{:S(2)}, u32[]{:S(2)}) collective-permute-start(bf16[640,128]{1,0:T(8,128)(2,1)S(1)} %quarter.1.refs_1_), channel_id=1, source_target_pairs={{0,2},{1,3},{2,0},{3,1},{4,6},{5,7},{6,4},{7,5},{8,10},{9,11},{10,... | collective-permute-start | bytes 491528 | tf_op jit(solution)/shard_map/ppermute | solution.py:783
  219.2 8.7 %collective-permute-start.36 = (bf16[640,128]{1,0:T(8,128)(2,1)S(1)}, bf16[640,128]{1,0:T(8,128)(2,1)S(1)}, u32[]{:S(2)}, u32[]{:S(2)}) collective-permute-start(bf16[640,128]{1,0:T(8,128)(2,1)S(1)} %collective-permute-done.34.refs_2_), channel_id=1, source_target_pairs={{0,2},{1,3},{2,0},{3,1},{4,6},{5,7},{6,4},{7,5},{8,10},{9,11},{10,... | collective-permute-start | bytes 491528 | tf_op jit(solution)/shard_map/ppermute | solution.py:783
  (46 other events, 381.5 us)

commit v5 on v4

--- a/solution.py
+++ b/solution.py
@@ -76,6 +76,9 @@
 
 def mm_right(a, b, ca=1, cb=0):
     high, low = split2(b)
+    if ca == 0:
+        both = mm(a, jnp.concatenate([high, low], axis=1), ca, cb)
+        return both[:, : b.shape[1]] + both[:, b.shape[1] :]
     return mm(a, high, ca, cb) + mm(a, low, ca, cb)
 
 
@@ -366,7 +369,7 @@
         lead_o[...] = out[0, 0:8, :]
 
 
-def k_back(final, slots, place, *refs):
+def k_back(final, slots, n_heads, place, *refs):
     (
         valid, h, xs, bc, g, pre, dt, cum, v, vprev, dxw, dbc, rq, qw, ent, ds, qd, endg, rims, cx, cb, hp,
     ) = refs[:22]
@@ -433,7 +436,6 @@
         acc_heads[8:16, :] += fold_rows(g_ld * step * rate)
         low = g_pre.astype(BF16)
         gpre_o[rows, :] = low
-        acc_dt[...] += mm(pltpu.roll(low.astype(F32), place[1], 1).astype(BF16), h[rows, :], 0, 0)[0 : acc_dt.shape[0]]
 
     gbuf[GROUP:, :] = rims[0, 0:8, :]
     if final:
@@ -455,8 +457,12 @@
     gbc_o[:, : 2 * N] = bc_high
     gbc_o[:, 2 * N :] = bc_low
     hh = h[...]
-    acc_x[...] += mm(hh, gx_low, 0, 0)
-    acc_bc[...] += mm(hh, bc_high, 0, 0) + mm(hh, bc_low, 0, 0)
+    moved = pltpu.roll(gpre_o[...].astype(F32), place[1], 1).astype(BF16)
+    both = mm(hh, jnp.concatenate([gx_low, moved], axis=1), 0, 0)
+    acc_x[...] += both[:, :width]
+    acc_dt[...] += both[:, width:]
+    both = mm(hh, jnp.concatenate([bc_high, bc_low], axis=1), 0, 0)
+    acc_bc[...] += both[:, : 2 * N] + both[:, 2 * N :]
     if not final:
         return
 
@@ -479,7 +485,8 @@
         count, each, rest = slots
         if at < count * each:
             put(jnp.zeros((count * each - at, LANES), F32))
-        put(stacked(acc_dt[...]))
+        for k in range(0, dim, LANES):
+            put(jnp.transpose(acc_dt[k : k + LANES, :])[0:n_heads])
 
         def line(value):
             return jnp.sum(value, axis=0, keepdims=True)
@@ -1073,14 +1080,14 @@
     rest = -(-(heads * dim // LANES + 16 + head_count * 8 * tiles) // (8 * count)) * 8
     slots = (count, each, rest)
     small_rows = count * (each + rest)
-    acc_shapes = [(dim, width), (dim, 2 * N), (heads, dim), (8 * KCONV + 8, conv_width), (16, LANES)]
+    acc_shapes = [(dim, width), (dim, 2 * N), (dim, LANES), (8 * KCONV + 8, conv_width), (16, LANES)]
 
     def back_call(final, more_in, more_out, more_scratch, alias, ready):
         def at(i, *s):
             return i + half if final else i
 
         return call(
-            functools.partial(k_back, final, slots),
+            functools.partial(k_back, final, slots, heads),
             half,
             [(group_valid, SMEM)]
             + [
@@ -1193,6 +1200,8 @@
         [],
         5 * 10**9,
         "out",
+        None,
+        16,
     )
 
     (copies,) = call(

time: 232 us -> 226 us (0.974)
  waiting for transfers between devices: 38.9 us -> 33.7 us
    ppermute x36, waiting for transfers between devices: 36.1 us -> 29.8 us  [swap(): lax.ppermute(value, axis, [(i, i ^ mask) for i in range(lax.axis_size(axi...]
  transfers between devices with their start and end apart: 40 -> 40, of which waited for: 15 -> 15; matrix products, arithmetic and copies ran while one was open for 2% -> 2% of each run, Pallas kernels for 51% -> 52%
where the time goes in v5:
time: 226 us; the launch traced here: 225 us
  Pallas kernels  132 us (58%)
  starting transfers between devices  45.4 us (20%)
  waiting for transfers between devices  33.7 us (15%)
  local copies, waits for them, and re-layouts  10.4 us (5%)
    pallas_call x32, Pallas kernels, call(): pl.pallas_call(body, grid_spec=pltpu.PrefetchScalarGridSpec(num_scalar_pr...  132 us
    ppermute x36, starting transfers between devices, swap(): lax.ppermute(value, axis, [(i, i ^ mask) for i in range(lax.axis_size(axi...  30.9 us
    ppermute x36, waiting for transfers between devices, swap(): lax.ppermute(value, axis, [(i, i ^ mask) for i in range(lax.axis_size(axi...  29.8 us
    unnamed x78, local copies, waits for them, and re-layouts  8.03 us
    all_to_all x2, starting transfers between devices, exchange(): return lax.all_to_all(pieces, axis, 0, 0, tiled=True)  8 us
    ppermute x1, starting transfers between devices, on_device(): rim = lax.ppermute(hidden_in[tokens - 16:], 'tok', route)  4.86 us
  transfers between devices with their start and end apart: 40, of which 15 were waited for; matrix products, arithmetic and copies ran while one was open for 2% of the time, Pallas kernels for 52%

profile of v5, /device:TPU:0, one launch (start us, length us, event | category | flops | bytes accessed | tf_op | source)
XLA Modules:
  0.0 225.1 jit_solution(3312415898393042505)
XLA Ops:
  1.5 4.9 %collective-permute-start = (bf16[16,768]{1,0:T(8,128)(2,1)S(1)}, bf16[16,768]{1,0:T(8,128)(2,1)S(1)}, u32[]{:S(2)}, u32[]{:S(2)}) collective-permute-start(bf16[16,768]{1,0:T(8,128)(2,1)S(1)} %slice.3), channel_id=1, source_target_pairs={{0,4},{4,8},{8,12},{12,16},{16,20},{20,24},{24,28},{1,5},{5,9},{9,... | collective-permute-start | bytes 73736 | tf_op jit(solution)/shard_map/ppermute | solution.py:893
  12.1 14.5 %front.1 = (bf16[2048,768]{1,0:T(8,128)(2,1)S(1)}, f32[2048,640]{1,0:T(8,128)S(1)}, f32[2048,128]{1,0:T(8,128)S(1)}, f32[8,8,640]{2,1,0:T(8,128)S(1)}, f32[8,16,...) custom-call(s32[8]{0:T(128)S(1)} %copy-done.13, ...), custom_call_target="tpu_custom_call" | custom-call | flops 4000000000 | bytes 22986304 | tf_op jit(solution)/shard_map/front/pallas_call | solution.py:764
  28.2 4.8 %collective-permute-done.1.refs_2_ = f32[136,384]{1,0:T(8,128)S(1)} collective-permute-done((f32[136,384]{1,0:T(8,128)S(1)}, f32[136,384]{1,0:T(8,128)S(1)}, u32[]{:S(2)}, u32[]{:S(2)}) %collective-permute-start.1) | collective-permute-done | bytes 208928 | tf_op jit(solution)/shard_map/ppermute | solution.py:790
  35.2 4.7 %proj.1 = (f32[2048,384]{1,0:T(8,128)S(1)}, f32[2048,384]{1,0:T(8,128)S(1)}, f32[2048,384]{1,0:T(8,128)S(1)}) custom-call(bf16[2048,768]{1,0:T(8,128)(2,1)S(1)} %get-tuple-element.198.refs_0_.refs_3_.refs_2_, bf16[2048,768]{1,0:T(8,128)(2,1)S(1)} %copy-done.6, bf16[768,768]{1,0:T(8,128)(2,1)S(1)} %bitcast.14, bf16[384,768]{1,0:T(8,128)(2,1)S(1)} %copy-done.18), custom_call_target="tpu_custom_call" | custom-call | flops 5000000000 | bytes 17498112 | tf_op jit(solution)/shard_map/proj/pallas_call | solution.py:764
  40.6 2.7 %collective-permute-start.3 = (f32[136,384]{1,0:T(8,128)S(1)}, f32[136,384]{1,0:T(8,128)S(1)}, u32[]{:S(2)}, u32[]{:S(2)}) collective-permute-start(f32[136,384]{1,0:T(8,128)S(1)} %get-tuple-element.144.refs_1_), channel_id=1, source_target_pairs={{0,16},{4,20},{8,24},{12,28},{16,0},{20,4},{24,8},{28,12},{1,17},{... | collective-permute-start | bytes 626696 | tf_op jit(solution)/shard_map/ppermute | solution.py:790
  43.3 6.4 %within.1 = (f32[2048,384]{1,0:T(8,128)S(1)}, f32[2048,384]{1,0:T(8,128)S(1)}) custom-call(bf16[2048,384]{1,0:T(8,128)(2,1)S(1)} %get-tuple-element.149.refs_0_.refs_6_.refs_1_.refs_3_, bf16[2048,256]{1,0:T(8,128)(2,1)S(1)} %get-tuple-element.148.refs_1_.refs_3_.refs_7_.refs_2_.refs_4_, f32[2048,128]{1,0:T(8,128)S(1)} %get-tuple-element.150.refs_2_.refs_3_.refs_4_.refs_7_, ...), custom_call_target="tpu_custom_call" | custom-call | flops 5000000000 | bytes 11010048 | tf_op jit(solution)/shard_map/within/pallas_call | solution.py:764
  49.7 3.8 %collective-permute-done.3.refs_2_ = f32[136,384]{1,0:T(8,128)S(1)} collective-permute-done((f32[136,384]{1,0:T(8,128)S(1)}, f32[136,384]{1,0:T(8,128)S(1)}, u32[]{:S(2)}, u32[]{:S(2)}) %collective-permute-start.3) | collective-permute-done | bytes 208928 | tf_op jit(solution)/shard_map/ppermute | solution.py:790
  54.1 3.9 %gate.1 = (f32[2048,384]{1,0:T(8,128)S(1)}, f32[16,128,384]{2,1,0:T(8,128)S(1)}, f32[2,2048]{1,0:T(2,128)S(1)}) custom-call(f32[16,128,384]{2,1,0:T(8,128)S(1)} %get-tuple-element.139.refs_0_, f32[16,1,384]{2,1,0:T(1,128)S(1)} %get-tuple-element.140.refs_1_, f32[136,384]{1,0:T(8,128)S(1)} %merge.8.refs_2_, ...), custom_call_target="tpu_custom_call" | custom-call | flops 3000000000 | bytes 24897024 | tf_op jit(solution)/shard_map/gate/pallas_call | solution.py:764
  63.8 7.5 %gate_back.1 = (bf16[2048,384]{1,0:T(8,128)(2,1)}, bf16[2048,384]{1,0:T(8,128)(2,1)S(1)}, bf16[2048,384]{1,0:T(8,128)(2,1)S(1)}, f32[16,128,384]{2,1,0:T(8,128)S...) custom-call(s32[8]{0:T(128)S(1)} %copy-done.13, ...), custom_call_target="tpu_custom_call" | custom-call | flops 3000000000 | bytes 26539552 | tf_op jit(solution)/shard_map/gate_back/pallas_call | solution.py:764
  72.9 7.3 %weights.1 = (f32[4,576,128]{2,1,0:T(8,128)S(1)}, f32[4,576,128]{2,1,0:T(8,128)S(1)}) custom-call(s32[4]{0:T(128)S(1)} %pad_add_fusion.refs_0_, bf16[2048,384]{1,0:T(8,128)(2,1)} %get-tuple-element.231.refs_1_, bf16[2048,768]{1,0:T(8,128)(2,1)S(1)} %copy-done.7, bf16[2048,768]{1,0:T(8,128)(2,1)S(1)} %copy-done.33, ...), custom_call_target="tpu_custom_call" | custom-call | flops 12000000000 | bytes 47185920 | tf_op jit(solution)/shard_map/weights/pallas_call | solution.py:764
  82.7 4.2 %collective-permute-done.11.refs_2_ = f32[136,384]{1,0:T(8,128)S(1)} collective-permute-done((f32[136,384]{1,0:T(8,128)S(1)}, f32[136,384]{1,0:T(8,128)S(1)}, u32[]{:S(2)}, u32[]{:S(2)}) %collective-permute-start.11) | collective-permute-done | bytes 208928 | tf_op jit(solution)/shard_map/ppermute | solution.py:790
  88.8 13.1 %within_back.1 = (f32[2048,384]{1,0:T(8,128)S(1)}, f32[2048,256]{1,0:T(8,128)S(1)}, f32[2048,128]{1,0:T(8,128)S(1)}, f32[2048,128]{1,0:T(8,128)S(1)}) custom-call(bf16[2048,384]{1,0:T(8,128)(2,1)S(1)} %get-tuple-element.149.refs_0_.refs_6_.refs_1_.refs_3_, bf16[2048,256]{1,0:T(8,128)(2,1)S(1)} %get-tuple-element.148.refs_1_.refs_3_.refs_7_.refs_2_.refs_4_, ...), custom_call_target="tpu_custom_call" | custom-call | flops 40000000000 | bytes 79708160 | tf_op jit(solution)/shard_map/within_back/pallas_call | solution.py:764
  102.6 2.9 %rim.1 = (f32[8,16,640]{2,1,0:T(8,128)S(1)}, f32[8,640]{1,0:T(8,128)S(1)}) custom-call(s32[8]{0:T(128)S(1)} %copy-done.13, bf16[2048,384]{1,0:T(8,128)(2,1)S(1)} %get-tuple-element.149.refs_0_.refs_6_.refs_1_.refs_3_, bf16[2048,256]{1,0:T(8,128)(2,1)S(1)} %get-tuple-element.148.refs_1_.refs_3_.refs_7_.refs_2_.refs_4_, ...), custom_call_target="tpu_custom_call" | custom-call | flops 1000000000 | bytes 16642080 | tf_op jit(solution)/shard_map/rim/pallas_call | solution.py:764
  107.1 1.9 collective-permute-done.13.refs_2_
  109.8 1.7 collective-permute-start.14
  114.3 12.7 %back_start.1 = (bf16[2048,384]{1,0:T(8,128)(2,1)S(1)}, bf16[2048,512]{1,0:T(8,128)(2,1)S(1)}, bf16[2048,128]{1,0:T(8,128)(2,1)S(1)}, f32[768,384]{1,0:T(8,128)S...) custom-call(s32[4]{0:T(128)S(1)} %pad_add_fusion.refs_0_, ...), custom_call_target="tpu_custom_call" | custom-call | flops 20000000000 | bytes 147064960 | tf_op jit(solution)/shard_map/back_start/pallas_call | solution.py:764
  127.2 2.4 %collective-permute-start.21 = (bf16[576,128]{1,0:T(8,128)(2,1)S(1)}, bf16[576,128]{1,0:T(8,128)(2,1)S(1)}, u32[]{:S(2)}, u32[]{:S(2)}) collective-permute-start(bf16[576,128]{1,0:T(8,128)(2,1)S(1)} %reduce.3.refs_1_), channel_id=1, source_target_pairs={{0,24},{4,28},{8,16},{12,20},{16,8},{20,12},{24,0},{28,4},{1,25},{... | collective-permute-start | bytes 442376 | tf_op jit(solution)/shard_map/ppermute | solution.py:790
  129.6 2.0 collective-permute-start.19
  131.7 14.0 %back_end.1 = (bf16[2048,384]{1,0:T(8,128)(2,1)S(1)}, bf16[2048,512]{1,0:T(8,128)(2,1)S(1)}, bf16[2048,128]{1,0:T(8,128)(2,1)S(1)}, f32[768,384]{1,0:T(8,128)S(1...) custom-call(s32[4]{0:T(128)S(1)} %pad_add_fusion.refs_0_, ...), custom_call_target="tpu_custom_call", output_to_operand_aliasing={{0}: (26, {}), {1}: (27, {}), {2}: (28, {}), {3}: (29, {}),... | custom-call | flops 20000000000 | bytes 179931264 | tf_op jit(solution)/shard_map/back_end/pallas_call | solution.py:764
  146.4 2.6 %input_sent.2 = (f32[512,768]{1,0:T(8,128)S(1)}, f32[8,768]{1,0:T(8,128)S(1)}) custom-call(s32[4]{0:T(128)S(1)} %pad_add_fusion.refs_0_, bf16[2048,768]{1,0:T(8,128)(2,1)S(1)} %copy-done.2, bf16[2048,384]{1,0:T(8,128)(2,1)S(1)} %get-tuple-element.162.refs_4_.refs_2_, bf16[2048,384]{1,0:T(8,128)(2,1)S(1)} %get-tuple-element.210.refs_3_, ...), custom_call_target="tpu_custom_call" | custom-call | flops 1000000000 | bytes 13459456 | tf_op jit(solution)/shard_map/input_sent/pallas_call | solution.py:764
  150.1 2.6 %input_sent.3 = (f32[512,768]{1,0:T(8,128)S(1)}, f32[8,768]{1,0:T(8,128)S(1)}) custom-call(s32[4]{0:T(128)S(1)} %pad_add_fusion.refs_0_, bf16[2048,768]{1,0:T(8,128)(2,1)S(1)} %copy-done.2, bf16[2048,384]{1,0:T(8,128)(2,1)S(1)} %get-tuple-element.162.refs_4_.refs_2_, bf16[2048,384]{1,0:T(8,128)(2,1)S(1)} %get-tuple-element.210.refs_3_, ...), custom_call_target="tpu_custom_call" | custom-call | flops 1000000000 | bytes 13484032 | tf_op jit(solution)/shard_map/input_sent/pallas_call | solution.py:764
  153.3 3.4 %input_own.2 = (bf16[512,768]{1,0:T(8,128)(2,1)}, f32[8,768]{1,0:T(8,128)S(1)}) custom-call(s32[4]{0:T(128)S(1)} %pad_add_fusion.refs_0_, bf16[2048,768]{1,0:T(8,128)(2,1)S(1)} %copy-done.2, bf16[2048,384]{1,0:T(8,128)(2,1)S(1)} %get-tuple-element.162.refs_4_.refs_2_, bf16[2048,384]{1,0:T(8,128)(2,1)S(1)} %get-tuple-element.210.refs_3_, ...), custom_call_target="tpu_custom_call" | custom-call | flops 1000000000 | bytes 14270464 | tf_op jit(solution)/shard_map/input_own/pallas_call | solution.py:764
  156.8 2.7 %input_own.3 = (bf16[512,768]{1,0:T(8,128)(2,1)S(1)}, f32[8,128]{1,0:T(8,128)S(1)}) custom-call(s32[4]{0:T(128)S(1)} %pad_add_fusion.refs_0_, bf16[2048,768]{1,0:T(8,128)(2,1)S(1)} %copy-done.2, bf16[2048,384]{1,0:T(8,128)(2,1)S(1)} %get-tuple-element.162.refs_4_.refs_2_, bf16[2048,384]{1,0:T(8,128)(2,1)S(1)} %get-tuple-element.210.refs_3_, ...), custom_call_target="tpu_custom_call" | custom-call | flops 1000000000 | bytes 14249984 | tf_op jit(solution)/shard_map/input_own/pallas_call | solution.py:764
  162.8 4.4 %all-to-all-start = ((bf16[8,368,128]{2,1,0:T(8,128)(2,1)}), bf16[8,368,128]{2,1,0:T(8,128)(2,1)}, u32[]{:S(2)}, u32[]{:S(2)}) async-start(bf16[8,368,128]{2,1,0:T(8,128)(2,1)} %copy-done.8), calls=%async_computation | async-start | bytes 1507328 | tf_op jit(solution)/shard_map/all_to_all | solution.py:857
  172.5 10.9 %out.1 = bf16[2048,768]{1,0:T(8,128)(2,1)} custom-call(bf16[2048,768]{1,0:T(8,128)(2,1)S(1)} %copy-done.2, bf16[2048,384]{1,0:T(8,128)(2,1)} %get-tuple-element.231.refs_1_, bf16[2048,384]{1,0:T(8,128)(2,1)} %collective-permute-done.17.refs_2_, bf16[2048,384]{1,0:T(8,128)(2,1)} %collective-permute-done.26.refs_3_, ...), custom_call_target="tpu_custom_call" | custom-call | flops 80000000000 | bytes 239075328 | tf_op jit(solution)/shard_map/out/pallas_call | solution.py:764
  183.5 3.3 %all-to-all-done.refs_0_ = bf16[8,368,128]{2,1,0:T(8,128)(2,1)} async-done(((bf16[8,368,128]{2,1,0:T(8,128)(2,1)}), bf16[8,368,128]{2,1,0:T(8,128)(2,1)}, u32[]{:S(2)}, u32[]{:S(2)}) %all-to-all-start) | async-done | bytes 753696 | tf_op jit(solution)/shard_map/all_to_all | solution.py:857
  186.7 2.1 reduce_both.1
  188.8 3.6 %all-to-all-start.1 = ((bf16[8,368,128]{2,1,0:T(8,128)(2,1)}), bf16[8,368,128]{2,1,0:T(8,128)(2,1)S(1)}, u32[]{:S(2)}, u32[]{:S(2)}) async-start(bf16[8,368,128]{2,1,0:T(8,128)(2,1)} %reduce_both.1), calls=%async_computation.1 | async-start | bytes 1507328 | tf_op jit(solution)/shard_map/all_to_all | solution.py:857
  193.0 5.2 %collective-permute-done.29.refs_7_ = bf16[512,768]{1,0:T(8,128)(2,1)} collective-permute-done((bf16[512,768]{1,0:T(8,128)(2,1)}, bf16[512,768]{1,0:T(8,128)(2,1)}, u32[]{:S(2)}, u32[]{:S(2)}) %collective-permute-start.29) | collective-permute-done | bytes 786464 | tf_op jit(solution)/shard_map/ppermute | solution.py:790
  201.8 9.6 %in_back.1 = f32[2048,768]{1,0:T(8,128)} custom-call(s32[4]{0:T(128)S(1)} %pad_add_fusion.refs_0_, bf16[2048,768]{1,0:T(8,128)(2,1)} %refs_1_.11, bf16[2048,768]{1,0:T(8,128)(2,1)} %refs_2_.4, f32[1,768]{1,0:T(1,128)S(1)} %copy-done.12, bf16[512,768]{1,0:T(8,128)(2,1)} %get-tuple-element.233.refs_4_, bf16[512,768]{1,0:T(8,128)(2,1)} %collective-permute-done.28.refs_5_, ...), custom_call_target="tpu_custom_call" | custom-call | flops 1000000000 | bytes 18877440 | tf_op jit(solution)/shard_map/in_back/pallas_call | solution.py:764
  214.2 2.7 %collective-permute-done.37.refs_2_ = bf16[4,576,128]{2,1,0:T(8,128)(2,1)S(1)} collective-permute-done((bf16[4,576,128]{2,1,0:T(8,128)(2,1)S(1)}, bf16[4,576,128]{2,1,0:T(8,128)(2,1)S(1)}, u32[]{:S(2)}, u32[]{:S(2)}) %collective-permute-start.37) | collective-permute-done | bytes 589856 | tf_op jit(solution)/shard_map/ppermute | solution.py:790
  218.6 2.5 %unpack.1 = f32[768,2,384]{2,1,0:T(2,128)} custom-call(s32[4]{0:T(128)S(1)} %pad_add_fusion.refs_0_, bf16[4,576,128]{2,1,0:T(8,128)(2,1)S(1)} %copy-done.5, bf16[4,576,128]{2,1,0:T(8,128)(2,1)S(1)} %collective-permute-done.37.refs_2_, bf16[8,368,128]{2,1,0:T(8,128)(2,1)S(1)} %all-to-all-done.1.refs_0_.refs_3_), custom_call_target="tpu_custom_call" | custom-call | flops 1000000 | bytes 4292608 | tf_op jit(solution)/shard_map/unpack/pallas_call | solution.py:764
  (170 shorter events, 52.8 us)
Async XLA Ops:
  1.5 10.5 %collective-permute-start = (bf16[16,768]{1,0:T(8,128)(2,1)S(1)}, bf16[16,768]{1,0:T(8,128)(2,1)S(1)}, u32[]{:S(2)}, u32[]{:S(2)}) collective-permute-start(bf16[16,768]{1,0:T(8,128)(2,1)S(1)} %slice.3), channel_id=1, source_target_pairs={{0,4},{4,8},{8,12},{12,16},{16,20},{20,24},{24,28},{1,5},{5,9},{9,... | collective-permute-start | bytes 73736 | tf_op jit(solution)/shard_map/ppermute | solution.py:893
  10.5 24.8 %collective-permute-start.4 = (bf16[384,768]{1,0:T(8,128)(2,1)S(1)}, bf16[384,768]{1,0:T(8,128)(2,1)S(1)}, u32[]{:S(2)}, u32[]{:S(2)}) collective-permute-start(bf16[384,768]{1,0:T(8,128)(2,1)S(1)} %copy-done.18), channel_id=1, source_target_pairs={{0,2},{1,3},{2,0},{3,1},{4,6},{5,7},{6,4},{7,5},{8,10},{9,11},{10,... | collective-permute-start | bytes 1769480 | tf_op jit(solution)/shard_map/ppermute | solution.py:790
  26.6 6.4 %collective-permute-start.1 = (f32[136,384]{1,0:T(8,128)S(1)}, f32[136,384]{1,0:T(8,128)S(1)}, u32[]{:S(2)}, u32[]{:S(2)}) collective-permute-start(f32[136,384]{1,0:T(8,128)S(1)} %get-tuple-element.141.refs_1_), channel_id=1, source_target_pairs={{0,4},{4,0},{8,12},{12,8},{16,20},{20,16},{24,28},{28,24},{1,5},{5... | collective-permute-start | bytes 626696 | tf_op jit(solution)/shard_map/ppermute | solution.py:790
  28.2 25.9 %collective-permute-start.5 = (bf16[384,768]{1,0:T(8,128)(2,1)S(1)}, bf16[384,768]{1,0:T(8,128)(2,1)S(1)}, u32[]{:S(2)}, u32[]{:S(2)}) collective-permute-start(bf16[384,768]{1,0:T(8,128)(2,1)S(1)} %copy-done.18), channel_id=1, source_target_pairs={{0,1},{1,0},{2,3},{3,2},{4,5},{5,4},{6,7},{7,6},{8,9},{9,8},{10,11... | collective-permute-start | bytes 1769480 | tf_op jit(solution)/shard_map/ppermute | solution.py:790
  33.6 6.4 %collective-permute-start.2 = (f32[136,384]{1,0:T(8,128)S(1)}, f32[136,384]{1,0:T(8,128)S(1)}, u32[]{:S(2)}, u32[]{:S(2)}) collective-permute-start(f32[136,384]{1,0:T(8,128)S(1)} %get-tuple-element.142.refs_1_), channel_id=1, source_target_pairs={{0,8},{4,12},{8,0},{12,4},{16,24},{20,28},{24,16},{28,20},{1,9},{5... | collective-permute-start | bytes 626696 | tf_op jit(solution)/shard_map/ppermute | solution.py:790
  35.2 18.9 %collective-permute-start.6 = (bf16[384,768]{1,0:T(8,128)(2,1)S(1)}, bf16[384,768]{1,0:T(8,128)(2,1)S(1)}, u32[]{:S(2)}, u32[]{:S(2)}) collective-permute-start(bf16[384,768]{1,0:T(8,128)(2,1)S(1)} %collective-permute-done.4.refs_6_), channel_id=1, source_target_pairs={{0,1},{1,0},{2,3},{3,2},{4,5},{5,4},{6,7},{7,6},{8,9},{9,8},{10,11... | collective-permute-start | bytes 1769480 | tf_op jit(solution)/shard_map/ppermute | solution.py:790
  40.6 12.9 %collective-permute-start.3 = (f32[136,384]{1,0:T(8,128)S(1)}, f32[136,384]{1,0:T(8,128)S(1)}, u32[]{:S(2)}, u32[]{:S(2)}) collective-permute-start(f32[136,384]{1,0:T(8,128)S(1)} %get-tuple-element.144.refs_1_), channel_id=1, source_target_pairs={{0,16},{4,20},{8,24},{12,28},{16,0},{20,4},{24,8},{28,12},{1,17},{... | collective-permute-start | bytes 626696 | tf_op jit(solution)/shard_map/ppermute | solution.py:790
  71.3 8.9 %collective-permute-start.10 = (f32[136,384]{1,0:T(8,128)S(1)}, f32[136,384]{1,0:T(8,128)S(1)}, u32[]{:S(2)}, u32[]{:S(2)}) collective-permute-start(f32[136,384]{1,0:T(8,128)S(1)} %get-tuple-element.172.refs_1_), channel_id=1, source_target_pairs={{0,4},{4,0},{8,12},{12,8},{16,20},{20,16},{24,28},{28,24},{1,5},{5... | collective-permute-start | bytes 626696 | tf_op jit(solution)/shard_map/ppermute | solution.py:790
  80.8 6.1 %collective-permute-start.11 = (f32[136,384]{1,0:T(8,128)S(1)}, f32[136,384]{1,0:T(8,128)S(1)}, u32[]{:S(2)}, u32[]{:S(2)}) collective-permute-start(f32[136,384]{1,0:T(8,128)S(1)} %get-tuple-element.174.refs_1_), channel_id=1, source_target_pairs={{0,8},{4,12},{8,0},{12,4},{16,24},{20,28},{24,16},{28,20},{1,9},{5... | collective-permute-start | bytes 626696 | tf_op jit(solution)/shard_map/ppermute | solution.py:790
  80.9 50.7 %collective-permute-start.17 = (bf16[2048,384]{1,0:T(8,128)(2,1)}, bf16[2048,384]{1,0:T(8,128)(2,1)}, u32[]{:S(2)}, u32[]{:S(2)}) collective-permute-start(bf16[2048,384]{1,0:T(8,128)(2,1)} %get-tuple-element.231.refs_1_), channel_id=1, source_target_pairs={{0,2},{1,3},{2,0},{3,1},{4,6},{5,7},{6,4},{7,5},{8,10},{9,11},{10,... | collective-permute-start | bytes 4718600 | tf_op jit(solution)/shard_map/ppermute | solution.py:790
  82.2 26.8 %collective-permute-start.13 = (f32[4,576,128]{2,1,0:T(8,128)S(1)}, f32[4,576,128]{2,1,0:T(8,128)S(1)}, u32[]{:S(2)}, u32[]{:S(2)}) collective-permute-start(f32[4,576,128]{2,1,0:T(8,128)S(1)} %get-tuple-element.181), channel_id=1, source_target_pairs={{0,4},{4,0},{8,12},{12,8},{16,20},{20,16},{24,28},{28,24},{1,5},{5... | collective-permute-start | bytes 3538952 | tf_op jit(solution)/shard_map/ppermute | solution.py:790
  87.6 14.4 %collective-permute-start.12 = (f32[136,384]{1,0:T(8,128)S(1)}, f32[136,384]{1,0:T(8,128)S(1)}, u32[]{:S(2)}, u32[]{:S(2)}) collective-permute-start(f32[136,384]{1,0:T(8,128)S(1)} %get-tuple-element.176.refs_1_), channel_id=1, source_target_pairs={{0,16},{4,20},{8,24},{12,28},{16,0},{20,4},{24,8},{28,12},{1,17},{... | collective-permute-start | bytes 626696 | tf_op jit(solution)/shard_map/ppermute | solution.py:790
  105.5 26.1 %collective-permute-start.18 = (f32[8,640]{1,0:T(8,128)S(1)}, f32[8,640]{1,0:T(8,128)S(1)}, u32[]{:S(2)}, u32[]{:S(2)}) collective-permute-start(f32[8,640]{1,0:T(8,128)S(1)} %get-tuple-element.178), channel_id=1, source_target_pairs={{4,0},{8,4},{12,8},{16,12},{20,16},{24,20},{28,24},{5,1},{9,5},{13... | collective-permute-start | bytes 61448 | tf_op jit(solution)/shard_map/ppermute | solution.py:1061
  109.8 17.3 %collective-permute-start.14 = (bf16[576,128]{1,0:T(8,128)(2,1)S(1)}, bf16[576,128]{1,0:T(8,128)(2,1)S(1)}, u32[]{:S(2)}, u32[]{:S(2)}) collective-permute-start(bf16[576,128]{1,0:T(8,128)(2,1)S(1)} %get-tuple-element.192), channel_id=1, source_target_pairs={{0,8},{4,12},{8,0},{12,4},{16,24},{20,28},{24,16},{28,20},{1,9},{5... | collective-permute-start | bytes 442376 | tf_op jit(solution)/shard_map/ppermute | solution.py:790
  111.5 15.5 %collective-permute-start.15 = (bf16[576,128]{1,0:T(8,128)(2,1)S(1)}, bf16[576,128]{1,0:T(8,128)(2,1)S(1)}, u32[]{:S(2)}, u32[]{:S(2)}) collective-permute-start(bf16[576,128]{1,0:T(8,128)(2,1)S(1)} %get-tuple-element.194), channel_id=1, source_target_pairs={{0,16},{4,20},{8,24},{12,28},{16,0},{20,4},{24,8},{28,12},{1,17},{... | collective-permute-start | bytes 442376 | tf_op jit(solution)/shard_map/ppermute | solution.py:790
  112.8 14.2 %collective-permute-start.16 = (bf16[576,128]{1,0:T(8,128)(2,1)S(1)}, bf16[576,128]{1,0:T(8,128)(2,1)S(1)}, u32[]{:S(2)}, u32[]{:S(2)}) collective-permute-start(bf16[576,128]{1,0:T(8,128)(2,1)S(1)} %get-tuple-element.196), channel_id=1, source_target_pairs={{0,24},{4,28},{8,16},{12,20},{16,8},{20,12},{24,0},{28,4},{1,25},{... | collective-permute-start | bytes 442376 | tf_op jit(solution)/shard_map/ppermute | solution.py:790
  127.2 18.5 %collective-permute-start.21 = (bf16[576,128]{1,0:T(8,128)(2,1)S(1)}, bf16[576,128]{1,0:T(8,128)(2,1)S(1)}, u32[]{:S(2)}, u32[]{:S(2)}) collective-permute-start(bf16[576,128]{1,0:T(8,128)(2,1)S(1)} %reduce.3.refs_1_), channel_id=1, source_target_pairs={{0,24},{4,28},{8,16},{12,20},{16,8},{20,12},{24,0},{28,4},{1,25},{... | collective-permute-start | bytes 442376 | tf_op jit(solution)/shard_map/ppermute | solution.py:790
  129.6 16.1 %collective-permute-start.20 = (bf16[576,128]{1,0:T(8,128)(2,1)S(1)}, bf16[576,128]{1,0:T(8,128)(2,1)S(1)}, u32[]{:S(2)}, u32[]{:S(2)}) collective-permute-start(bf16[576,128]{1,0:T(8,128)(2,1)S(1)} %reduce.3.refs_1_), channel_id=1, source_target_pairs={{0,16},{4,20},{8,24},{12,28},{16,0},{20,4},{24,8},{28,12},{1,17},{... | collective-permute-start | bytes 442376 | tf_op jit(solution)/shard_map/ppermute | solution.py:790
  129.6 16.1 %collective-permute-start.19 = (bf16[576,128]{1,0:T(8,128)(2,1)S(1)}, bf16[576,128]{1,0:T(8,128)(2,1)S(1)}, u32[]{:S(2)}, u32[]{:S(2)}) collective-permute-start(bf16[576,128]{1,0:T(8,128)(2,1)S(1)} %reduce.3.refs_1_), channel_id=1, source_target_pairs={{0,8},{4,12},{8,0},{12,4},{16,24},{20,28},{24,16},{28,20},{1,9},{5... | collective-permute-start | bytes 442376 | tf_op jit(solution)/shard_map/ppermute | solution.py:790
  148.9 4.4 %collective-permute-start.25 = (f32[512,768]{1,0:T(8,128)S(1)}, f32[512,768]{1,0:T(8,128)S(1)}, u32[]{:S(2)}, u32[]{:S(2)}) collective-permute-start(f32[512,768]{1,0:T(8,128)S(1)} %get-tuple-element.219), channel_id=1, source_target_pairs={{0,1},{1,0},{2,3},{3,2},{4,5},{5,4},{6,7},{7,6},{8,9},{9,8},{10,11... | collective-permute-start | bytes 4718600 | tf_op jit(solution)/shard_map/ppermute | solution.py:790
  152.8 8.0 %collective-permute-start.23 = (f32[448,128]{1,0:T(8,128)S(1)}, f32[448,128]{1,0:T(8,128)S(1)}, u32[]{:S(2)}, u32[]{:S(2)}) collective-permute-start(f32[448,128]{1,0:T(8,128)S(1)} %get-tuple-element.222), channel_id=1, source_target_pairs={{0,2},{1,3},{2,0},{3,1},{4,6},{5,7},{6,4},{7,5},{8,10},{9,11},{10,... | collective-permute-start | bytes 688136 | tf_op jit(solution)/shard_map/ppermute | solution.py:790
  160.9 7.4 %collective-permute-start.26 = (bf16[2048,384]{1,0:T(8,128)(2,1)}, bf16[2048,384]{1,0:T(8,128)(2,1)}, u32[]{:S(2)}, u32[]{:S(2)}) collective-permute-start(bf16[2048,384]{1,0:T(8,128)(2,1)} %get-tuple-element.231.refs_1_), channel_id=1, source_target_pairs={{0,1},{1,0},{2,3},{3,2},{4,5},{5,4},{6,7},{7,6},{8,9},{9,8},{10,11... | collective-permute-start | bytes 4718600 | tf_op jit(solution)/shard_map/ppermute | solution.py:790
  160.9 7.3 %collective-permute-start.27 = (bf16[2048,384]{1,0:T(8,128)(2,1)}, bf16[2048,384]{1,0:T(8,128)(2,1)}, u32[]{:S(2)}, u32[]{:S(2)}) collective-permute-start(bf16[2048,384]{1,0:T(8,128)(2,1)} %collective-permute-done.17.refs_2_), channel_id=1, source_target_pairs={{0,1},{1,0},{2,3},{3,2},{4,5},{5,4},{6,7},{7,6},{8,9},{9,8},{10,11... | collective-permute-start | bytes 4718600 | tf_op jit(solution)/shard_map/ppermute | solution.py:790
  161.7 36.4 %collective-permute-start.28 = (bf16[512,768]{1,0:T(8,128)(2,1)}, bf16[512,768]{1,0:T(8,128)(2,1)}, u32[]{:S(2)}, u32[]{:S(2)}) collective-permute-start(bf16[512,768]{1,0:T(8,128)(2,1)} %get-tuple-element.233.refs_4_), channel_id=1, source_target_pairs={{0,2},{1,3},{2,0},{3,1},{4,6},{5,7},{6,4},{7,5},{8,10},{9,11},{10,... | collective-permute-start | bytes 2359304 | tf_op jit(solution)/shard_map/ppermute | solution.py:790
  162.8 24.0 %all-to-all-start = ((bf16[8,368,128]{2,1,0:T(8,128)(2,1)}), bf16[8,368,128]{2,1,0:T(8,128)(2,1)}, u32[]{:S(2)}, u32[]{:S(2)}) async-start(bf16[8,368,128]{2,1,0:T(8,128)(2,1)} %copy-done.8), calls=%async_computation | async-start | bytes 1507328 | tf_op jit(solution)/shard_map/all_to_all | solution.py:857
  167.2 31.0 %collective-permute-start.29 = (bf16[512,768]{1,0:T(8,128)(2,1)}, bf16[512,768]{1,0:T(8,128)(2,1)}, u32[]{:S(2)}, u32[]{:S(2)}) collective-permute-start(bf16[512,768]{1,0:T(8,128)(2,1)} %copy-done.9), channel_id=1, source_target_pairs={{0,2},{1,3},{2,0},{3,1},{4,6},{5,7},{6,4},{7,5},{8,10},{9,11},{10,... | collective-permute-start | bytes 2359304 | tf_op jit(solution)/shard_map/ppermute | solution.py:790
  188.8 23.2 %all-to-all-start.1 = ((bf16[8,368,128]{2,1,0:T(8,128)(2,1)}), bf16[8,368,128]{2,1,0:T(8,128)(2,1)S(1)}, u32[]{:S(2)}, u32[]{:S(2)}) async-start(bf16[8,368,128]{2,1,0:T(8,128)(2,1)} %reduce_both.1), calls=%async_computation.1 | async-start | bytes 1507328 | tf_op jit(solution)/shard_map/all_to_all | solution.py:857
  192.4 7.7 %collective-permute-start.30 = (bf16[512,768]{1,0:T(8,128)(2,1)}, bf16[512,768]{1,0:T(8,128)(2,1)S(1)}, u32[]{:S(2)}, u32[]{:S(2)}) collective-permute-start(bf16[512,768]{1,0:T(8,128)(2,1)} %get-tuple-element.233.refs_4_), channel_id=1, source_target_pairs={{0,1},{1,0},{2,3},{3,2},{4,5},{5,4},{6,7},{7,6},{8,9},{9,8},{10,11... | collective-permute-start | bytes 2359304 | tf_op jit(solution)/shard_map/ppermute | solution.py:790
  192.5 7.6 %collective-permute-start.32 = (bf16[512,768]{1,0:T(8,128)(2,1)S(1)}, bf16[512,768]{1,0:T(8,128)(2,1)S(1)}, u32[]{:S(2)}, u32[]{:S(2)}) collective-permute-start(bf16[512,768]{1,0:T(8,128)(2,1)S(1)} %copy-done.10), channel_id=1, source_target_pairs={{0,1},{1,0},{2,3},{3,2},{4,5},{5,4},{6,7},{7,6},{8,9},{9,8},{10,11... | collective-permute-start | bytes 2359304 | tf_op jit(solution)/shard_map/ppermute | solution.py:790
  198.7 18.3 %collective-permute-start.37 = (bf16[4,576,128]{2,1,0:T(8,128)(2,1)S(1)}, bf16[4,576,128]{2,1,0:T(8,128)(2,1)S(1)}, u32[]{:S(2)}, u32[]{:S(2)}) collective-permute-start(bf16[4,576,128]{2,1,0:T(8,128)(2,1)S(1)} %copy-done.5), channel_id=1, source_target_pairs={{0,4},{4,0},{8,12},{12,8},{16,20},{20,16},{24,28},{28,24},{1,5},{5... | collective-permute-start | bytes 1769480 | tf_op jit(solution)/shard_map/ppermute | solution.py:790
  212.1 8.9 %collective-permute-start.35 = (bf16[640,128]{1,0:T(8,128)(2,1)S(1)}, bf16[640,128]{1,0:T(8,128)(2,1)S(1)}, u32[]{:S(2)}, u32[]{:S(2)}) collective-permute-start(bf16[640,128]{1,0:T(8,128)(2,1)S(1)} %quarter.1.refs_1_), channel_id=1, source_target_pairs={{0,2},{1,3},{2,0},{3,1},{4,6},{5,7},{6,4},{7,5},{8,10},{9,11},{10,... | collective-permute-start | bytes 491528 | tf_op jit(solution)/shard_map/ppermute | solution.py:790
  213.5 8.7 %collective-permute-start.36 = (bf16[640,128]{1,0:T(8,128)(2,1)S(1)}, bf16[640,128]{1,0:T(8,128)(2,1)S(1)}, u32[]{:S(2)}, u32[]{:S(2)}) collective-permute-start(bf16[640,128]{1,0:T(8,128)(2,1)S(1)} %collective-permute-done.34.refs_2_), channel_id=1, source_target_pairs={{0,2},{1,3},{2,0},{3,1},{4,6},{5,7},{6,4},{7,5},{8,10},{9,11},{10,... | collective-permute-start | bytes 491528 | tf_op jit(solution)/shard_map/ppermute | solution.py:790
  (46 other events, 399.0 us)
